TPU v7x, 32 devices: a whole 2x2x4 slice. The times are simulated.
32 devices in a mesh: seq: 4 (over x, core), batch: 2 (over y), tensor: 4 (over z).
Axes of the slice: x: 2, y: 2, z: 4, core: 2. Of those that a mesh axis runs over, the one named last changes fastest.
Arguments:
- tokens: bfloat16 [8, 1024, 2048], P('batch', 'seq'), may hold values from -6 to 6
- cotangent: bfloat16 [8, 1024, 2048], P('batch', 'seq'), may hold values from -6 to 6
- lengths: int32 [8], P('batch'), may hold values from 512 to 1024, as said below
- block_slot: int32 [4], replicated, may hold values from 0 to 3, each once
- gain_attn: float32 [2048], replicated, may hold values from 0.5 to 1.5
- shift_attn: float32 [2048], replicated, may hold values from -1.75 to 1.75
- gain_mlp: float32 [2048], replicated, may hold values from 0.5 to 1.5
- shift_mlp: float32 [2048], replicated, may hold values from -1.75 to 1.75
- w_qkv: bfloat16 [2048, 8, 768], P(('seq', 'batch'), 'tensor'), may hold values from -0.125 to 0.125
- b_qkv: float32 [8, 768], P('tensor'), may hold values from -1.75 to 1.75
- w_out: bfloat16 [2048, 2048], P('tensor', ('seq', 'batch')), may hold values from -2 to 2
- b_out: float32 [2048], replicated, may hold values from -1.75 to 1.75
- w_up: bfloat16 [2048, 8192], P(('seq', 'batch'), 'tensor'), may hold values from -0.125 to 0.125
- b_up: float32 [8192], P('tensor'), may hold values from -1.75 to 1.75
- w_down: bfloat16 [8192, 2048], P('tensor', ('seq', 'batch')), may hold values from -0.0625 to 0.0625
- b_down: float32 [2048], replicated, may hold values from -1.75 to 1.75
Outputs:
- mixed: bfloat16 [8, 1024, 2048], P('batch', 'seq')
- tokens_grad: float32 [8, 1024, 2048], P('batch', 'seq')
- gain_attn_grad: float32 [2048], replicated
- shift_attn_grad: float32 [2048], replicated
- gain_mlp_grad: float32 [2048], replicated
- shift_mlp_grad: float32 [2048], replicated
- w_qkv_grad: float32 [2048, 8, 768], P(('seq', 'batch'), 'tensor')
- b_qkv_grad: float32 [8, 768], P('tensor')
- w_out_grad: float32 [2048, 2048], P('tensor', ('seq', 'batch'))
- b_out_grad: float32 [2048], replicated
- w_up_grad: float32 [2048, 8192], P(('seq', 'batch'), 'tensor')
- b_up_grad: float32 [8192], P('tensor')
- w_down_grad: float32 [8192, 2048], P('tensor', ('seq', 'batch'))
- b_down_grad: float32 [2048], replicated
Inputs may be any that keep to these rules, and one draw needn't show every extreme that they name: `lengths`: in every aligned block of 1 sequence one has length 1024. `block_slot`: every block index appears exactly once.
All inputs are finite; a program needn't handle non-finite values.
Results may differ from a plain program's by a relative error of at most 0.019.
Values may be sent and summed in bfloat16 or wider, within the bound.
No kernel may reach another device: no remote copies, remote signals or barrier semaphores. Data moves between devices by JAX's collectives and lax.ppermute only.
A program may use at most 192 MiB of HBM per device.

v0:
```python
from functools import partial

import jax
import jax.numpy as jnp
from jax import lax
from jax.sharding import PartitionSpec as P

D = 2048
HEAD_DIM = 256
ROT = 64
SEQS_DEV = 1
MICRO = 4


EPS = 1e-05
FLOOR = -1e30


def normalize(token_rows, gain_attn, shift_attn, gain_mlp, shift_mlp):
    centered = token_rows - jnp.mean(token_rows, -1, keepdims=True)
    scaled = centered * lax.rsqrt(jnp.mean(jnp.square(centered), -1, keepdims=True) + EPS)
    return (scaled * gain_attn + shift_attn, scaled * gain_mlp + shift_mlp)


def rotate(field_in, places):
    half_rot = ROT // 2
    frequency = 10000.0 ** (jnp.arange(half_rot, dtype=jnp.float32) * (-2.0 / ROT))
    angles = places.astype(jnp.float32)[:, None] * frequency[None, :]
    cosine = jnp.cos(angles)[:, None, :]
    sine_part = jnp.sin(angles)[:, None, :]
    front_part = field_in[..., :half_rot]
    back_part = field_in[..., half_rot:ROT]
    return jnp.concatenate(
        [
            front_part * cosine - back_part * sine_part,
            back_part * cosine + front_part * sine_part,
            field_in[..., ROT:],
        ],
        -1,
    )


def per_device(
    tokens,
    cotangent,
    lengths,
    block_slot,
    gain_attn,
    shift_attn,
    gain_mlp,
    shift_mlp,
    w_qkv,
    b_qkv,
    w_out,
    b_out,
    w_up,
    b_up,
    w_down,
    b_down,
):
    block_rows = tokens.shape[1]
    seq_count = lax.axis_size("seq")
    local_heads = w_qkv.shape[1]
    score_scale = HEAD_DIM ** (-0.5)
    seq_total = SEQS_DEV * block_rows
    device_ids = jnp.arange(seq_count, dtype=jnp.int32)
    own_slot = jnp.sum(jnp.where(device_ids == lax.axis_index("seq"), block_slot, 0))
    query_places = own_slot * block_rows + jnp.arange(block_rows, dtype=jnp.int32)

    def key_places(row_ids):
        owners = row_ids // block_rows
        slot_of = jnp.sum(
            jnp.where(owners[:, None] == device_ids[None, :], block_slot[None, :], 0), axis=1
        )
        return slot_of * block_rows + row_ids % block_rows

    def visible(places_keys, seq_lengths):
        causal = places_keys[None, None, :] <= query_places[None, :, None]
        inside = places_keys[None, None, :] < seq_lengths[:, None, None]
        return (causal & inside)[:, None]

    grad_store = tuple(
        (
            jnp.zeros(weight_shard.shape, jnp.float32)
            for weight_shard in (w_qkv, w_out, w_up, w_down)
        )
    )
    norm_totals = tuple((jnp.zeros((D,), jnp.float32) for counter_id in range(4)))
    bias_qkv_total = jnp.zeros(b_qkv.shape, jnp.float32)
    bias_out_total = jnp.zeros((D,), jnp.float32)
    bias_up_total = jnp.zeros(b_up.shape, jnp.float32)
    outputs_mixed = []
    outputs_grad = []
    for micro_step in range(MICRO):
        first_row = micro_step * SEQS_DEV
        batch_tokens = tokens[first_row : first_row + SEQS_DEV]
        batch_cotangent = cotangent[first_row : first_row + SEQS_DEV]
        seq_lengths = lengths[first_row : first_row + SEQS_DEV]
        fetched = (
            lax.all_gather(w_qkv, ("seq", "batch"), axis=0, tiled=True),
            lax.all_gather(w_out, ("seq", "batch"), axis=1, tiled=True),
            lax.all_gather(w_up, ("seq", "batch"), axis=0, tiled=True),
            lax.all_gather(w_down, ("seq", "batch"), axis=1, tiled=True),
        )
        full_qkv, full_out, full_up, full_down = fetched
        flat_qkv = full_qkv.reshape(D, -1)
        token_rows = batch_tokens.astype(jnp.float32).reshape(seq_total, D)
        (normed_attn, normed_mlp), norm_pull = jax.vjp(
            normalize, token_rows, gain_attn, shift_attn, gain_mlp, shift_mlp
        )
        input_attn = normed_attn.astype(jnp.bfloat16)
        input_mlp = normed_mlp.astype(jnp.bfloat16)
        project = (
            jnp.dot(input_attn, flat_qkv, preferred_element_type=jnp.float32).reshape(
                SEQS_DEV, block_rows, local_heads, 3 * HEAD_DIM
            )
            + b_qkv
        )
        (query_rot, key_rot), rope_pull = jax.vjp(
            lambda query_raw, key_raw: (
                rotate(query_raw, query_places),
                rotate(key_raw, query_places),
            ),
            project[..., :HEAD_DIM],
            project[..., HEAD_DIM : 2 * HEAD_DIM],
        )
        queries = query_rot.astype(jnp.bfloat16)
        keys_low = key_rot.astype(jnp.bfloat16)
        values = project[..., 2 * HEAD_DIM :].astype(jnp.bfloat16)
        running_top = jnp.full((SEQS_DEV, local_heads, block_rows), FLOOR, jnp.float32)
        key_piece = lax.all_gather(keys_low, "seq", axis=1, tiled=True)
        value_piece = lax.all_gather(values, "seq", axis=1, tiled=True)
        piece_rows = key_piece.shape[1]
        mask_piece = visible(key_places(jnp.arange(piece_rows, dtype=jnp.int32)), seq_lengths)
        scores = (
            jnp.einsum("schd,sthd->shct", queries, key_piece, preferred_element_type=jnp.float32)
            * score_scale
        )
        scores = jnp.where(mask_piece, scores, FLOOR)
        new_top = jnp.maximum(running_top, jnp.max(scores, -1))
        weights = jnp.where(mask_piece, jnp.exp(scores - new_top[..., None]), 0.0)
        running_sum = jnp.sum(weights, -1)
        running_acc = jnp.einsum(
            "shct,sthd->shcd",
            weights.astype(jnp.bfloat16),
            value_piece,
            preferred_element_type=jnp.float32,
        )
        attended = running_acc / running_sum[..., None]
        log_total = new_top + jnp.log(running_sum)
        attended_rows = jnp.transpose(attended.astype(jnp.bfloat16), (0, 2, 1, 3)).reshape(
            seq_total, local_heads * HEAD_DIM
        )
        hidden_pre = jnp.dot(input_mlp, full_up, preferred_element_type=jnp.float32) + b_up
        activated = jax.nn.gelu(hidden_pre, approximate=False).astype(jnp.bfloat16)
        partial_branch = jnp.dot(
            attended_rows, full_out, preferred_element_type=jnp.float32
        ) + jnp.dot(activated, full_down, preferred_element_type=jnp.float32)
        branch = lax.psum(partial_branch.astype(jnp.bfloat16), "tensor").astype(jnp.float32)
        outputs_mixed.append(
            (token_rows + branch + b_out + b_down)
            .astype(jnp.bfloat16)
            .reshape(SEQS_DEV, block_rows, D)
        )
        valid_rows = (query_places[None, :] < seq_lengths[:, None]).astype(jnp.float32)
        grad_rows = (batch_cotangent.astype(jnp.float32) * valid_rows[..., None]).reshape(
            seq_total, D
        )
        grad_low = grad_rows.astype(jnp.bfloat16)
        bias_out_total = bias_out_total + jnp.sum(grad_rows, 0)
        grad_w_out = jnp.einsum(
            "rk,rd->kd", attended_rows, grad_low, preferred_element_type=jnp.float32
        )
        grad_w_down = jnp.einsum(
            "rf,rd->fd", activated, grad_low, preferred_element_type=jnp.float32
        )
        grad_act = jnp.einsum("rd,fd->rf", grad_low, full_down, preferred_element_type=jnp.float32)
        grad_hidden = jax.vjp(partial(jax.nn.gelu, approximate=False), hidden_pre)[1](grad_act)[0]
        bias_up_total = bias_up_total + jnp.sum(grad_hidden, 0)
        hidden_low = grad_hidden.astype(jnp.bfloat16)
        grad_w_up = jnp.einsum(
            "rd,rf->df", input_mlp, hidden_low, preferred_element_type=jnp.float32
        )
        grad_att = (
            jnp.einsum("rd,kd->rk", grad_low, full_out, preferred_element_type=jnp.float32)
            .reshape(SEQS_DEV, block_rows, local_heads, HEAD_DIM)
            .astype(jnp.bfloat16)
        )
        all_keys, all_values = (
            lax.all_gather(keys_low, "seq", axis=1, tiled=True),
            lax.all_gather(values, "seq", axis=1, tiled=True),
        )
        total_rows = all_keys.shape[1]
        places_all = key_places(jnp.arange(total_rows, dtype=jnp.int32))
        mask_all = visible(places_all, seq_lengths)
        scores = (
            jnp.einsum("schd,sthd->shct", queries, all_keys, preferred_element_type=jnp.float32)
            * score_scale
        )
        probabilities = jnp.where(mask_all, jnp.exp(scores - log_total[..., None]), 0.0)
        prob_low = probabilities.astype(jnp.bfloat16)
        grad_probs = jnp.einsum(
            "schd,sthd->shct", grad_att, all_values, preferred_element_type=jnp.float32
        )
        row_delta = jnp.sum(probabilities * grad_probs, -1)
        grad_scores = (probabilities * (grad_probs - row_delta[..., None])).astype(jnp.bfloat16)
        grad_query = (
            jnp.einsum("shct,sthd->schd", grad_scores, all_keys, preferred_element_type=jnp.float32)
            * score_scale
        )
        key_term = (
            jnp.einsum("shct,schd->sthd", grad_scores, queries, preferred_element_type=jnp.float32)
            * score_scale
        )
        value_term = jnp.einsum(
            "shct,schd->sthd", prob_low, grad_att, preferred_element_type=jnp.float32
        )
        grad_key, grad_value = (
            lax.psum_scatter(
                key_term.astype(jnp.bfloat16), "seq", scatter_dimension=1, tiled=True
            ).astype(jnp.float32),
            lax.psum_scatter(
                value_term.astype(jnp.bfloat16), "seq", scatter_dimension=1, tiled=True
            ).astype(jnp.float32),
        )
        grad_q_raw, grad_k_raw = rope_pull((grad_query, grad_key))
        grad_project = jnp.concatenate([grad_q_raw, grad_k_raw, grad_value], -1)
        bias_qkv_total = bias_qkv_total + jnp.sum(grad_project, (0, 1))
        project_low = grad_project.reshape(seq_total, -1).astype(jnp.bfloat16)
        grad_w_qkv = jnp.einsum(
            "rd,rk->dk", input_attn, project_low, preferred_element_type=jnp.float32
        ).reshape(full_qkv.shape)
        grad_norm_attn = jnp.einsum(
            "rk,dk->rd", project_low, flat_qkv, preferred_element_type=jnp.float32
        )
        grad_norm_mlp = jnp.einsum(
            "rf,df->rd", hidden_low, full_up, preferred_element_type=jnp.float32
        )
        input_part, gain_a_part, shift_a_part, gain_m_part, shift_m_part = norm_pull(
            (grad_norm_attn, grad_norm_mlp)
        )
        summed = (
            lax.psum(input_part.astype(jnp.bfloat16), "tensor").astype(jnp.float32),
            lax.psum(gain_a_part.astype(jnp.bfloat16), "tensor").astype(jnp.float32),
            lax.psum(shift_a_part.astype(jnp.bfloat16), "tensor").astype(jnp.float32),
            lax.psum(gain_m_part.astype(jnp.bfloat16), "tensor").astype(jnp.float32),
            lax.psum(shift_m_part.astype(jnp.bfloat16), "tensor").astype(jnp.float32),
        )
        outputs_grad.append((grad_rows + summed[0]).reshape(SEQS_DEV, block_rows, D))
        norm_totals = tuple((stored + fresh for stored, fresh in zip(norm_totals, summed[1:])))
        reduced = (
            lax.psum_scatter(
                grad_w_qkv.astype(jnp.bfloat16), ("seq", "batch"), scatter_dimension=0, tiled=True
            ).astype(jnp.float32),
            lax.psum_scatter(
                grad_w_out.astype(jnp.bfloat16), ("seq", "batch"), scatter_dimension=1, tiled=True
            ).astype(jnp.float32),
            lax.psum_scatter(
                grad_w_up.astype(jnp.bfloat16), ("seq", "batch"), scatter_dimension=0, tiled=True
            ).astype(jnp.float32),
            lax.psum_scatter(
                grad_w_down.astype(jnp.bfloat16), ("seq", "batch"), scatter_dimension=1, tiled=True
            ).astype(jnp.float32),
        )
        grad_store = tuple((stored + fresh for stored, fresh in zip(grad_store, reduced)))
    small_sums = (
        lax.psum(norm_totals[0].astype(jnp.bfloat16), ("seq", "batch")).astype(jnp.float32),
        lax.psum(norm_totals[1].astype(jnp.bfloat16), ("seq", "batch")).astype(jnp.float32),
        lax.psum(norm_totals[2].astype(jnp.bfloat16), ("seq", "batch")).astype(jnp.float32),
        lax.psum(norm_totals[3].astype(jnp.bfloat16), ("seq", "batch")).astype(jnp.float32),
        lax.psum(bias_qkv_total.astype(jnp.bfloat16), ("seq", "batch")).astype(jnp.float32),
        lax.psum(bias_out_total.astype(jnp.bfloat16), ("seq", "batch")).astype(jnp.float32),
        lax.psum(bias_up_total.astype(jnp.bfloat16), ("seq", "batch")).astype(jnp.float32),
    )
    return (
        jnp.concatenate(outputs_mixed, 0),
        jnp.concatenate(outputs_grad, 0),
        small_sums[0],
        small_sums[1],
        small_sums[2],
        small_sums[3],
        grad_store[0],
        small_sums[4],
        grad_store[1],
        small_sums[5],
        grad_store[2],
        small_sums[6],
        grad_store[3],
        small_sums[5],
    )


def solution(mesh):
    placed = (
        P("batch", "seq", None),
        P("batch", "seq", None),
        P("batch"),
        P(),
        P(),
        P(),
        P(),
        P(),
        P(("seq", "batch"), "tensor", None),
        P("tensor", None),
        P("tensor", ("seq", "batch")),
        P(),
        P(("seq", "batch"), "tensor"),
        P("tensor"),
        P("tensor", ("seq", "batch")),
        P(),
    )
    return jax.shard_map(
        per_device,
        mesh=mesh,
        in_specs=placed,
        out_specs=(
            P("batch", "seq", None),
            P("batch", "seq", None),
            P(),
            P(),
            P(),
            P(),
            P(("seq", "batch"), "tensor", None),
            P("tensor", None),
            P("tensor", ("seq", "batch")),
            P(),
            P(("seq", "batch"), "tensor"),
            P("tensor"),
            P("tensor", ("seq", "batch")),
            P(),
        ),
        check_vma=False,
    )
```

profile of v0, /device:TPU:0, one launch (start us, length us, event | category | flops | bytes accessed | tf_op | source)
XLA Modules:
  0.0 2048.3 jit_solution(10231260898283002389)
XLA Ops:
  16.3 41.9 %all-gather.13.cloned.1.call-done = bf16[2048,2,768]{2,1,0:T(2,128)(2,1)} async-done(((bf16[256,2,768]{2,1,0:T(2,128)(2,1)}), bf16[2048,2,768]{2,1,0:T(2,128)(2,1)}) %all-gather.13.cloned.1.call-update) | async-done | bytes 6291472 | tf_op jit(solution)/shard_map/all_gather | solution.py:100
  90.9 16.2 all-gather.15.cloned.1.call-done
  109.6 16.3 all-gather.17.cloned.1.call-done
  136.7 19.5 reduce-scatter.25.cloned.1.call-done
  158.3 26.0 %reduce-scatter.27.cloned.1.call-done = bf16[1,256,2,256]{3,1,2,0:T(8,128)(2,1)} async-done(((bf16[1,1024,2,256]{3,1,2,0:T(8,128)(2,1)}), bf16[1,256,2,256]{3,1,2,0:T(8,128)(2,1)}) %reduce-scatter.27.cloned.1.call-update) | async-done | bytes 262160 | tf_op jit(solution)/shard_map/reduce_scatter | solution.py:222
  188.7 51.9 %all-gather.21.cloned.1.call-done = bf16[2048,2048]{1,0:T(8,128)(2,1)} async-done(((bf16[256,2048]{1,0:T(8,128)(2,1)}), bf16[2048,2048]{1,0:T(8,128)(2,1)}) %all-gather.21.cloned.1.call-update) | async-done | bytes 8388624 | tf_op jit(solution)/shard_map/all_gather | solution.py:102
  251.3 47.1 %all-gather.23.cloned.1.call-done = bf16[2048,2048]{1,0:T(8,128)(2,1)} async-done(((bf16[2048,256]{1,0:T(8,128)(2,1)}), bf16[2048,2048]{1,0:T(8,128)(2,1)}) %all-gather.23.cloned.1.call-update) | async-done | bytes 8388624 | tf_op jit(solution)/shard_map/all_gather | solution.py:103
  331.1 12.4 all-gather.33.cloned.1.call-done
  347.3 14.3 all-gather.35.cloned.1.call-done
  376.4 16.2 reduce-scatter.37.cloned.1.call-done
  417.8 14.4 all-gather.31.cloned.1.call-done
  469.3 11.2 multiply_convert_fusion.8
  485.9 11.4 fusion.347
  527.5 11.6 fusion.350
  571.5 21.8 %reduce-scatter.29.cloned.1.call-done = bf16[1,256,2,256]{3,1,2,0:T(8,128)(2,1)} async-done(((bf16[1,1024,2,256]{3,1,2,0:T(8,128)(2,1)}), bf16[1,256,2,256]{3,1,2,0:T(8,128)(2,1)}) %reduce-scatter.29.cloned.1.call-update) | async-done | bytes 262160 | tf_op jit(solution)/shard_map/reduce_scatter | solution.py:219
  597.3 24.1 %reduce-scatter.31.cloned.1.call-done = bf16[1,256,2,256]{3,1,2,0:T(8,128)(2,1)} async-done(((bf16[1,1024,2,256]{3,1,2,0:T(8,128)(2,1)}), bf16[1,256,2,256]{3,1,2,0:T(8,128)(2,1)}) %reduce-scatter.31.cloned.1.call-update) | async-done | bytes 262160 | tf_op jit(solution)/shard_map/reduce_scatter | solution.py:222
  634.3 15.7 fusion.73
  815.6 24.3 %all-reduce.24 = (bf16[2048]{0:T(1024)(128)(2,1)S(1)}, bf16[2048]{0:T(1024)(128)(2,1)S(1)}, bf16[2048]{0:T(1024)(128)(2,1)S(1)}, bf16[2048]{0:T(1024)(128)(2,1)S...) all-reduce(bf16[2048]{0:T(1024)(128)(2,1)S(1)} %add_convert_fusion., ...), channel_id=1, replica_groups=mesh['seq'=4,'batch'=2,'tensor'=4] {'seq','batch'}, use_global_device_ids=true, to_apply=%region_54.55 | all-reduce | flops 13824 | bytes 55296 | tf_op jit(solution)/shard_map/psum | solution.py:267
  843.5 32.8 %reduce-scatter.51.cloned.1.call-done = bf16[512,256]{1,0:T(8,128)(2,1)} async-done(((bf16[512,2048]{1,0:T(8,128)(2,1)}), bf16[512,256]{1,0:T(8,128)(2,1)}) %reduce-scatter.51.cloned.1.call-update) | async-done | bytes 262160 | tf_op jit(solution)/shard_map/reduce_scatter | solution.py:255
  878.3 72.9 %reduce-scatter.57.cloned.1.call-done = bf16[256,2048]{1,0:T(8,128)(2,1)} async-done(((bf16[2048,2048]{1,0:T(8,128)(2,1)}), bf16[256,2048]{1,0:T(8,128)(2,1)}) %reduce-scatter.57.cloned.1.call-update) | async-done | bytes 1048592 | tf_op jit(solution)/shard_map/reduce_scatter | solution.py:258
  951.3 75.2 %reduce-scatter.63.cloned.1.call-done = bf16[256,2048]{1,0:T(8,128)(2,1)} async-done(((bf16[2048,2048]{1,0:T(8,128)(2,1)}), bf16[256,2048]{1,0:T(8,128)(2,1)}) %reduce-scatter.63.cloned.1.call-update) | async-done | bytes 1048592 | tf_op jit(solution)/shard_map/reduce_scatter | solution.py:258
  1026.5 75.1 %reduce-scatter.59.cloned.1.call-done = bf16[256,2048]{1,0:T(8,128)(2,1)} async-done(((bf16[2048,2048]{1,0:T(8,128)(2,1)}), bf16[256,2048]{1,0:T(8,128)(2,1)}) %reduce-scatter.59.cloned.1.call-update) | async-done | bytes 1048592 | tf_op jit(solution)/shard_map/reduce_scatter | solution.py:258
  1101.6 74.8 %reduce-scatter.61.cloned.1.call-done = bf16[256,2048]{1,0:T(8,128)(2,1)} async-done(((bf16[2048,2048]{1,0:T(8,128)(2,1)}), bf16[256,2048]{1,0:T(8,128)(2,1)}) %reduce-scatter.61.cloned.1.call-update) | async-done | bytes 1048592 | tf_op jit(solution)/shard_map/reduce_scatter | solution.py:258
  1180.6 70.8 %reduce-scatter.67.cloned.1.call-done = bf16[2048,256]{1,0:T(8,128)(2,1)} async-done(((bf16[2048,2048]{1,0:T(8,128)(2,1)}), bf16[2048,256]{1,0:T(8,128)(2,1)}) %reduce-scatter.67.cloned.1.call-update) | async-done | bytes 1048592 | tf_op jit(solution)/shard_map/reduce_scatter | solution.py:261
  1251.4 74.8 %reduce-scatter.71.cloned.1.call-done = bf16[2048,256]{1,0:T(8,128)(2,1)} async-done(((bf16[2048,2048]{1,0:T(8,128)(2,1)}), bf16[2048,256]{1,0:T(8,128)(2,1)}) %reduce-scatter.71.cloned.1.call-update) | async-done | bytes 1048592 | tf_op jit(solution)/shard_map/reduce_scatter | solution.py:261
  1326.2 75.2 %reduce-scatter.69.cloned.1.call-done = bf16[2048,256]{1,0:T(8,128)(2,1)} async-done(((bf16[2048,2048]{1,0:T(8,128)(2,1)}), bf16[2048,256]{1,0:T(8,128)(2,1)}) %reduce-scatter.69.cloned.1.call-update) | async-done | bytes 1048592 | tf_op jit(solution)/shard_map/reduce_scatter | solution.py:261
  1401.4 74.6 %reduce-scatter.65.cloned.1.call-done = bf16[2048,256]{1,0:T(8,128)(2,1)} async-done(((bf16[2048,2048]{1,0:T(8,128)(2,1)}), bf16[2048,256]{1,0:T(8,128)(2,1)}) %reduce-scatter.65.cloned.1.call-update) | async-done | bytes 1048592 | tf_op jit(solution)/shard_map/reduce_scatter | solution.py:261
  1480.0 296.2 %all-reduce.32.cloned.1.call-done = (bf16[256,2048]{1,0:T(8,128)(2,1)}, bf16[256,2048]{1,0:T(8,128)(2,1)}, bf16[256,2048]{1,0:T(8,128)(2,1)}, bf16[256,2048]{1,0...) async-done(((bf16[256,2048]{1,0:T(8,128)(2,1)}, bf16[256,2048]{1,0:T(8,128)(2,1)}, ...) | async-done | bytes 8388624 | tf_op jit(solution)/shard_map/psum | solution.py:159
  1791.5 49.1 %reduce-scatter.41.cloned.1.call-done = bf16[256,2,768]{2,0,1:T(8,128)(2,1)} async-done(((bf16[2048,2,768]{2,0,1:T(8,128)(2,1)}), bf16[256,2,768]{2,0,1:T(8,128)(2,1)}) %reduce-scatter.41.cloned.1.call-update) | async-done | bytes 786448 | tf_op jit(solution)/shard_map/reduce_scatter | solution.py:252
  1840.6 65.0 %reduce-scatter.47.cloned.1.call-done = bf16[256,2,768]{2,0,1:T(8,128)(2,1)} async-done(((bf16[2048,2,768]{2,0,1:T(8,128)(2,1)}), bf16[256,2,768]{2,0,1:T(8,128)(2,1)}) %reduce-scatter.47.cloned.1.call-update) | async-done | bytes 786448 | tf_op jit(solution)/shard_map/reduce_scatter | solution.py:252
  1905.6 65.4 %reduce-scatter.45.cloned.1.call-done = bf16[256,2,768]{2,0,1:T(8,128)(2,1)} async-done(((bf16[2048,2,768]{2,0,1:T(8,128)(2,1)}), bf16[256,2,768]{2,0,1:T(8,128)(2,1)}) %reduce-scatter.45.cloned.1.call-update) | async-done | bytes 786448 | tf_op jit(solution)/shard_map/reduce_scatter | solution.py:252
  1971.0 65.1 %reduce-scatter.43.cloned.1.call-done = bf16[256,2,768]{2,0,1:T(8,128)(2,1)} async-done(((bf16[2048,2,768]{2,0,1:T(8,128)(2,1)}), bf16[256,2,768]{2,0,1:T(8,128)(2,1)}) %reduce-scatter.43.cloned.1.call-update) | async-done | bytes 786448 | tf_op jit(solution)/shard_map/reduce_scatter | solution.py:252
  (747 shorter events, 466.7 us)
Async XLA Ops:
  7.9 80.3 %all-gather.19.cloned.1.call-start = ((), (), s32[]{:S(2)}) async-start(), calls=%async_computation.27 | async-start | bytes 2359296 | tf_op jit(solution)/shard_map/all_gather | solution.py:101
  8.7 98.5 %all-gather.15.cloned.1.call-start = ((), (), s32[]{:S(2)}) async-start(), calls=%async_computation.25 | async-start | bytes 1310720 | tf_op jit(solution)/shard_map/all_gather | solution.py:131
  85.6 70.6 %reduce-scatter.25.cloned.1.call-start = ((), (), s32[]{:S(2)}) async-start(), calls=%async_computation.36 | async-start | bytes 1310720 | tf_op jit(solution)/shard_map/reduce_scatter | solution.py:219
  133.8 106.7 %all-gather.21.cloned.1.call-start = ((), (), s32[]{:S(2)}) async-start(), calls=%async_computation.28 | async-start | bytes 9437184 | tf_op jit(solution)/shard_map/all_gather | solution.py:102
  134.6 163.9 %all-gather.23.cloned.1.call-start = ((), (), s32[]{:S(2)}) async-start(), calls=%async_computation.29 | async-start | bytes 9437184 | tf_op jit(solution)/shard_map/all_gather | solution.py:103
  135.3 208.1 %all-gather.33.cloned.1.call-start = ((), (), s32[]{:S(2)}) async-start(), calls=%async_computation.34 | async-start | bytes 1310720 | tf_op jit(solution)/shard_map/all_gather | solution.py:131
  328.3 64.2 %reduce-scatter.37.cloned.1.call-start = ((), (), s32[]{:S(2)}) async-start(), calls=%async_computation.42 | async-start | bytes 1310720 | tf_op jit(solution)/shard_map/reduce_scatter | solution.py:219
  403.3 115.9 %all-gather.25.cloned.1.call-start = ((), (), s32[]{:S(2)}) async-start(), calls=%async_computation.30 | async-start | bytes 1310720 | tf_op jit(solution)/shard_map/all_gather | solution.py:131
  440.6 81.8 %all-gather.27.cloned.1.call-start = ((), (), s32[]{:S(2)}) async-start(), calls=%async_computation.31 | async-start | bytes 1310720 | tf_op jit(solution)/shard_map/all_gather | solution.py:132
  448.1 101.8 %reduce-scatter.39.cloned.1.call-start = ((), (), s32[]{:S(2)}) async-start(), calls=%async_computation.43 | async-start | bytes 1310720 | tf_op jit(solution)/shard_map/reduce_scatter | solution.py:222
  485.8 80.9 %reduce-scatter.33.cloned.1.call-start = ((), (), s32[]{:S(2)}) async-start(), calls=%async_computation.40 | async-start | bytes 1310720 | tf_op jit(solution)/shard_map/reduce_scatter | solution.py:219
  499.0 71.5 %reduce-scatter.35.cloned.1.call-start = ((), (), s32[]{:S(2)}) async-start(), calls=%async_computation.41 | async-start | bytes 1310720 | tf_op jit(solution)/shard_map/reduce_scatter | solution.py:222
  511.4 81.9 %reduce-scatter.29.cloned.1.call-start = ((), (), s32[]{:S(2)}) async-start(), calls=%async_computation.38 | async-start | bytes 1310720 | tf_op jit(solution)/shard_map/reduce_scatter | solution.py:219
  527.4 93.9 %reduce-scatter.31.cloned.1.call-start = ((), (), s32[]{:S(2)}) async-start(), calls=%async_computation.39 | async-start | bytes 1310720 | tf_op jit(solution)/shard_map/reduce_scatter | solution.py:222
  540.7 272.1 %all-reduce.30.cloned.1.call-start = ((), (), s32[]{:S(2)}) async-start(), calls=%async_computation.60 | async-start | bytes 131072 | tf_op jit(solution)/shard_map/psum | solution.py:244
  660.6 182.8 %reduce-scatter.49.cloned.1.call-start = ((), (), s32[]{:S(2)}) async-start(), calls=%async_computation.48 | async-start | bytes 2359296 | tf_op jit(solution)/shard_map/reduce_scatter | solution.py:255
  664.4 179.1 %reduce-scatter.55.cloned.1.call-start = ((), (), s32[]{:S(2)}) async-start(), calls=%async_computation.51 | async-start | bytes 2359296 | tf_op jit(solution)/shard_map/reduce_scatter | solution.py:255
  670.3 173.2 %reduce-scatter.53.cloned.1.call-start = ((), (), s32[]{:S(2)}) async-start(), calls=%async_computation.50 | async-start | bytes 2359296 | tf_op jit(solution)/shard_map/reduce_scatter | solution.py:255
  676.9 199.4 %reduce-scatter.51.cloned.1.call-start = ((), (), s32[]{:S(2)}) async-start(), calls=%async_computation.49 | async-start | bytes 2359296 | tf_op jit(solution)/shard_map/reduce_scatter | solution.py:255
  682.1 269.1 %reduce-scatter.57.cloned.1.call-start = ((), (), s32[]{:S(2)}) async-start(), calls=%async_computation.52 | async-start | bytes 9437184 | tf_op jit(solution)/shard_map/reduce_scatter | solution.py:258
  689.6 336.9 %reduce-scatter.63.cloned.1.call-start = ((), (), s32[]{:S(2)}) async-start(), calls=%async_computation.55 | async-start | bytes 9437184 | tf_op jit(solution)/shard_map/reduce_scatter | solution.py:258
  698.0 403.6 %reduce-scatter.59.cloned.1.call-start = ((), (), s32[]{:S(2)}) async-start(), calls=%async_computation.53 | async-start | bytes 9437184 | tf_op jit(solution)/shard_map/reduce_scatter | solution.py:258
  706.3 470.1 %reduce-scatter.61.cloned.1.call-start = ((), (), s32[]{:S(2)}) async-start(), calls=%async_computation.54 | async-start | bytes 9437184 | tf_op jit(solution)/shard_map/reduce_scatter | solution.py:258
  714.7 536.7 %reduce-scatter.67.cloned.1.call-start = ((), (), s32[]{:S(2)}) async-start(), calls=%async_computation.57 | async-start | bytes 9437184 | tf_op jit(solution)/shard_map/reduce_scatter | solution.py:261
  723.0 603.2 %reduce-scatter.71.cloned.1.call-start = ((), (), s32[]{:S(2)}) async-start(), calls=%async_computation.59 | async-start | bytes 9437184 | tf_op jit(solution)/shard_map/reduce_scatter | solution.py:261
  731.3 670.1 %reduce-scatter.69.cloned.1.call-start = ((), (), s32[]{:S(2)}) async-start(), calls=%async_computation.58 | async-start | bytes 9437184 | tf_op jit(solution)/shard_map/reduce_scatter | solution.py:261
  739.6 736.5 %reduce-scatter.65.cloned.1.call-start = ((), (), s32[]{:S(2)}) async-start(), calls=%async_computation.56 | async-start | bytes 9437184 | tf_op jit(solution)/shard_map/reduce_scatter | solution.py:261
  747.8 1028.4 %all-reduce.32.cloned.1.call-start = ((), (), s32[]{:S(2)}) async-start(), calls=%async_computation.61 | async-start | bytes 16777216 | tf_op jit(solution)/shard_map/psum | solution.py:159
  778.7 1061.9 %reduce-scatter.41.cloned.1.call-start = ((), (), s32[]{:S(2)}) async-start(), calls=%async_computation.44 | async-start | bytes 7077888 | tf_op jit(solution)/shard_map/reduce_scatter | solution.py:252
  785.8 1119.8 %reduce-scatter.47.cloned.1.call-start = ((), (), s32[]{:S(2)}) async-start(), calls=%async_computation.47 | async-start | bytes 7077888 | tf_op jit(solution)/shard_map/reduce_scatter | solution.py:252
  792.7 1178.3 %reduce-scatter.45.cloned.1.call-start = ((), (), s32[]{:S(2)}) async-start(), calls=%async_computation.46 | async-start | bytes 7077888 | tf_op jit(solution)/shard_map/reduce_scatter | solution.py:252
  799.8 1236.3 %reduce-scatter.43.cloned.1.call-start = ((), (), s32[]{:S(2)}) async-start(), calls=%async_computation.45 | async-start | bytes 7077888 | tf_op jit(solution)/shard_map/reduce_scatter | solution.py:252
  (234 other events, 6529.3 us)
Sparse Core Ops, SparseCore 0:
  9.9 48.2 all-gather.12
  60.0 28.1 all-gather.18
  131.3 24.8 reduce-scatter.24
  159.3 24.8 reduce-scatter.26
  186.1 54.3 all-gather.20
  242.4 55.9 all-gather.22
  367.6 24.8 reduce-scatter.36
  397.0 16.7 all-gather.28
  458.9 16.7 all-gather.26
  485.9 25.0 reduce-scatter.38
  513.4 24.8 reduce-scatter.32
  540.9 24.9 reduce-scatter.34
  568.4 24.8 reduce-scatter.28
  596.4 24.8 reduce-scatter.30
  660.8 36.0 all-reduce.29
  700.4 41.0 reduce-scatter.48
  745.4 41.2 reduce-scatter.54
  790.2 41.3 reduce-scatter.52
  834.9 41.3 reduce-scatter.50
  879.9 71.2 reduce-scatter.56
  955.1 71.2 reduce-scatter.62
  1030.3 71.2 reduce-scatter.58
  1105.1 71.2 reduce-scatter.60
  1180.1 71.2 reduce-scatter.66
  1254.9 71.2 reduce-scatter.70
  1330.1 71.2 reduce-scatter.68
  1404.7 71.2 reduce-scatter.64
  1480.4 295.6 all-reduce.31
  1779.9 60.6 reduce-scatter.40
  1843.9 61.7 reduce-scatter.46
  1909.2 61.7 reduce-scatter.44
  1974.4 61.7 reduce-scatter.42
  (6 shorter events, 100.0 us)
where the time goes:
time: 2060 us; the launch traced here: 2050 us
  waiting for transfers between devices  1490 us (72%)
  matrix products  336 us (16%)
  other arithmetic  101 us (5%)
  local copies, waits for them, and re-layouts  70.8 us (3%)
  blocking collectives  24.3 us (1%)
    reduce_scatter x4, waiting for transfers between devices, per_device(): lax.psum_scatter(grad_w_up.astype(jnp.bfloat16), ('seq', 'batch'), scatte...  298 us
    psum x1, waiting for transfers between devices, per_device(): lax.psum(partial_branch.astype(jnp.bfloat16), 'tensor').astype(jnp.float32)  296 us
    reduce_scatter x4, waiting for transfers between devices, per_device(): lax.psum_scatter(grad_w_down.astype(jnp.bfloat16), ('seq', 'batch'), scat...  295 us
    reduce_scatter x4, waiting for transfers between devices, per_device(): lax.psum_scatter(grad_w_qkv.astype(jnp.bfloat16), ('seq', 'batch'), scatt...  245 us
    reduce_scatter x4, waiting for transfers between devices, per_device(): lax.psum_scatter(key_term.astype(jnp.bfloat16), 'seq', scatter_dimension=...  57.6 us
    all_gather x1, waiting for transfers between devices, per_device(): lax.all_gather(w_up, ('seq', 'batch'), axis=0, tiled=True)  51.9 us
    reduce_scatter x4, waiting for transfers between devices, per_device(): lax.psum_scatter(value_term.astype(jnp.bfloat16), 'seq', scatter_dimensio...  50.1 us
    all_gather x1, waiting for transfers between devices, per_device(): lax.all_gather(w_down, ('seq', 'batch'), axis=1, tiled=True)  47.1 us
  transfers between devices with their start and end apart: 38, of which 29 were waited for; matrix products, arithmetic and copies ran while one was open for 19% of the time, Pallas kernels for 0%

commit v1 on v0

v1 whole, which is shorter than its diff:
```python
import jax
import jax.numpy as jnp
from jax import lax
from jax.sharding import PartitionSpec as P

D = 2048
HEAD_DIM = 256
ROT = 64
EPS = 1e-05
FLOOR = -1e30
BF = jnp.bfloat16
F32 = jnp.float32


def dot(a, b, dims):
    return lax.dot_general(a, b, (dims, ((), ())), preferred_element_type=F32)


def rotation(places):
    half_rot = ROT // 2
    frequency = 10000.0 ** (jnp.arange(half_rot, dtype=F32) * (-2.0 / ROT))
    angles = places.astype(F32)[:, None] * frequency[None, :]
    return jnp.cos(angles)[:, None, :], jnp.sin(angles)[:, None, :]


def rotate(field, cosine, sine):
    half_rot = ROT // 2
    front = field[..., :half_rot]
    back = field[..., half_rot:ROT]
    return jnp.concatenate(
        [front * cosine - back * sine, back * cosine + front * sine, field[..., ROT:]], -1
    )


def gelu_pair(z):
    phi_cdf = 0.5 * (1.0 + lax.erf(z * 0.7071067811865476))
    density = 0.3989422804014327 * jnp.exp(-0.5 * z * z)
    return z * phi_cdf, phi_cdf + z * density


def per_device(
    tokens,
    cotangent,
    lengths,
    block_slot,
    gain_attn,
    shift_attn,
    gain_mlp,
    shift_mlp,
    w_qkv,
    b_qkv,
    w_out,
    b_out,
    w_up,
    b_up,
    w_down,
    b_down,
):
    seqs, block_rows, _ = tokens.shape
    rows = seqs * block_rows
    shard = w_qkv.shape[0]
    heads = w_qkv.shape[1]
    width_qkv = heads * 3 * HEAD_DIM
    width_att = heads * HEAD_DIM
    units = w_up.shape[1]
    fsdp = ("seq", "batch")
    scale = HEAD_DIM ** (-0.5)
    seq_count = lax.axis_size("seq")
    device_ids = jnp.arange(seq_count, dtype=jnp.int32)
    own_slot = jnp.sum(jnp.where(device_ids == lax.axis_index("seq"), block_slot, 0))
    offsets = jnp.arange(block_rows, dtype=jnp.int32)
    query_places = own_slot * block_rows + offsets
    key_places = (block_slot[:, None] * block_rows + offsets[None, :]).reshape(-1)

    attn_shard = jnp.concatenate([w_qkv.reshape(shard, width_qkv), w_out.T], 1)
    mlp_shard = jnp.concatenate([w_up, w_down.T], 1)
    attn_full = lax.all_gather(attn_shard, fsdp, axis=0, tiled=True)
    mlp_full = lax.all_gather(mlp_shard, fsdp, axis=0, tiled=True)
    full_qkv = attn_full[:, :width_qkv]
    full_out_t = attn_full[:, width_qkv:]
    full_up = mlp_full[:, :units]
    full_down_t = mlp_full[:, units:]

    token_rows = tokens.astype(F32).reshape(rows, D)
    centered = token_rows - jnp.mean(token_rows, -1, keepdims=True)
    inverse = lax.rsqrt(jnp.mean(jnp.square(centered), -1, keepdims=True) + EPS)
    xhat = centered * inverse
    input_attn = (xhat * gain_attn + shift_attn).astype(BF)
    input_mlp = (xhat * gain_mlp + shift_mlp).astype(BF)

    valid = (query_places[None, :] < lengths[:, None]).astype(F32)
    grad_rows = (cotangent.astype(F32) * valid[..., None]).reshape(rows, D)
    grad_low = grad_rows.astype(BF)

    project = dot(input_attn, full_qkv, ((1,), (0,))).reshape(
        seqs, block_rows, heads, 3 * HEAD_DIM
    ) + b_qkv
    cosine, sine = rotation(query_places)
    queries = rotate(project[..., :HEAD_DIM], cosine, sine).astype(BF)
    keys = rotate(project[..., HEAD_DIM : 2 * HEAD_DIM], cosine, sine).astype(BF)
    values = project[..., 2 * HEAD_DIM :].astype(BF)
    pair = jnp.concatenate([keys, values], -1)
    gathered = lax.all_gather(pair, "seq", axis=0, tiled=False)
    gathered = jnp.transpose(gathered, (1, 3, 0, 2, 4)).reshape(
        seqs, heads, seq_count * block_rows, 2 * HEAD_DIM
    )
    all_keys = gathered[..., :HEAD_DIM]
    all_values = gathered[..., HEAD_DIM:]

    hidden_pre = dot(input_mlp, full_up, ((1,), (0,))) + b_up
    gelu, slope = gelu_pair(hidden_pre)
    activated = gelu.astype(BF)
    grad_hidden = dot(grad_low, full_down_t, ((1,), (0,))) * slope
    hidden_low = grad_hidden.astype(BF)
    bias_up_sum = jnp.sum(grad_hidden, 0)

    grad_att = dot(grad_low, full_out_t, ((1,), (0,))).reshape(
        seqs, block_rows, heads, HEAD_DIM
    ).astype(BF)

    causal = key_places[None, None, :] <= query_places[None, :, None]
    inside = key_places[None, None, :] < lengths[:, None, None]
    mask = (causal & inside)[:, None]
    scores = jnp.einsum("schd,shtd->shct", queries, all_keys, preferred_element_type=F32) * scale
    scores = jnp.where(mask, scores, FLOOR)
    top = jnp.max(scores, -1, keepdims=True)
    weights = jnp.where(mask, jnp.exp(scores - top), 0.0)
    probs = weights / jnp.sum(weights, -1, keepdims=True)
    prob_low = probs.astype(BF)
    attended = jnp.einsum("shct,shtd->schd", prob_low, all_values, preferred_element_type=F32)
    attended = attended.astype(BF).reshape(rows, width_att)

    partial = dot(attended, full_out_t, ((1,), (1,))) + dot(activated, full_down_t, ((1,), (1,)))
    branch = lax.psum(partial.astype(BF), "tensor").astype(F32)

    grad_mlp_weights = jnp.concatenate(
        [dot(input_mlp, hidden_low, ((0,), (0,))), dot(grad_low, activated, ((0,), (0,)))], 1
    ).astype(BF)
    mlp_reduced = lax.psum_scatter(
        grad_mlp_weights, fsdp, scatter_dimension=0, tiled=True
    ).astype(F32)

    grad_probs = jnp.einsum("schd,shtd->shct", grad_att, all_values, preferred_element_type=F32)
    delta = jnp.sum(probs * grad_probs, -1, keepdims=True)
    grad_scores = (probs * (grad_probs - delta)).astype(BF)
    grad_query = jnp.einsum("shct,shtd->schd", grad_scores, all_keys, preferred_element_type=F32) * scale
    key_term = jnp.einsum("shct,schd->tshd", grad_scores, queries, preferred_element_type=F32) * scale
    value_term = jnp.einsum("shct,schd->tshd", prob_low, grad_att, preferred_element_type=F32)
    terms = jnp.concatenate([key_term, value_term], -1).astype(BF)
    own_terms = lax.psum_scatter(terms, "seq", scatter_dimension=0, tiled=True).astype(F32)
    own_terms = jnp.swapaxes(own_terms, 0, 1)
    grad_key = own_terms[..., :HEAD_DIM]
    grad_value = own_terms[..., HEAD_DIM:]
    grad_project = jnp.concatenate(
        [rotate(grad_query, cosine, -sine), rotate(grad_key, cosine, -sine), grad_value], -1
    ).reshape(rows, width_qkv)
    bias_qkv_sum = jnp.sum(grad_project, 0)
    project_low = grad_project.astype(BF)

    grad_norm_attn = dot(project_low, full_qkv, ((1,), (1,)))
    grad_norm_mlp = dot(hidden_low, full_up, ((1,), (1,)))
    norm_sums = jnp.stack(
        [
            jnp.sum(grad_norm_attn * xhat, 0),
            jnp.sum(grad_norm_attn, 0),
            jnp.sum(grad_norm_mlp * xhat, 0),
            jnp.sum(grad_norm_mlp, 0),
        ]
    )
    grad_xhat = grad_norm_attn * gain_attn + grad_norm_mlp * gain_mlp
    input_part = inverse * (
        grad_xhat
        - jnp.mean(grad_xhat, -1, keepdims=True)
        - xhat * jnp.mean(grad_xhat * xhat, -1, keepdims=True)
    )
    input_part, branch = lax.optimization_barrier((input_part.astype(BF), branch))
    input_sum = lax.psum(input_part, "tensor").astype(F32)
    mixed = (token_rows + branch + b_out + b_down).astype(BF).reshape(tokens.shape)
    tokens_grad = (grad_rows + input_sum).reshape(tokens.shape)

    grad_attn_weights = jnp.concatenate(
        [dot(input_attn, project_low, ((0,), (0,))), dot(grad_low, attended, ((0,), (0,)))], 1
    ).astype(BF)
    attn_reduced = lax.psum_scatter(
        grad_attn_weights, fsdp, scatter_dimension=0, tiled=True
    ).astype(F32)

    norm_sums = lax.psum(norm_sums, "tensor").reshape(-1)
    small = lax.psum(
        jnp.concatenate([norm_sums, bias_qkv_sum, jnp.sum(grad_rows, 0), bias_up_sum]), fsdp
    )
    norm_sums = small[: 4 * D].reshape(4, D)
    small = small[4 * D :]
    bias_qkv_sum = small[:width_qkv].reshape(b_qkv.shape)
    bias_out_sum = small[width_qkv : width_qkv + D]
    bias_up_sum = small[width_qkv + D :]
    return (
        mixed,
        tokens_grad,
        norm_sums[0],
        norm_sums[1],
        norm_sums[2],
        norm_sums[3],
        attn_reduced[:, :width_qkv].reshape(w_qkv.shape),
        bias_qkv_sum,
        attn_reduced[:, width_qkv:].T,
        bias_out_sum,
        mlp_reduced[:, :units],
        bias_up_sum,
        mlp_reduced[:, units:].T,
        bias_out_sum,
    )


def solution(mesh):
    in_specs = (
        P("batch", "seq", None),
        P("batch", "seq", None),
        P("batch"),
        P(),
        P(),
        P(),
        P(),
        P(),
        P(("seq", "batch"), "tensor", None),
        P("tensor", None),
        P("tensor", ("seq", "batch")),
        P(),
        P(("seq", "batch"), "tensor"),
        P("tensor"),
        P("tensor", ("seq", "batch")),
        P(),
    )
    out_specs = (
        P("batch", "seq", None),
        P("batch", "seq", None),
        P(),
        P(),
        P(),
        P(),
        P(("seq", "batch"), "tensor", None),
        P("tensor", None),
        P("tensor", ("seq", "batch")),
        P(),
        P(("seq", "batch"), "tensor"),
        P("tensor"),
        P("tensor", ("seq", "batch")),
        P(),
    )
    return jax.shard_map(
        per_device, mesh=mesh, in_specs=in_specs, out_specs=out_specs, check_vma=False
    )
```

time: 2060 us -> 936 us (0.45)
  waiting for transfers between devices: 1490 us -> 509 us
  matrix products: 336 us -> 177 us
  blocking collectives: 24.3 us -> 46.1 us
    reduce_scatter x24 -> x3, waiting for transfers between devices: 979 us -> 243 us  [the longest x1 109 us: per_device(): lax.psum_scatter(grad_mlp_weights, fsdp, scatter_dimension=0, tiled=True)]
    psum x2, waiting for transfers between devices: 296 us -> 128 us  [the longest x1 82.7 us: per_device(): branch = lax.psum(partial.astype(BF), 'tensor').astype(F32)]
    dot_general x72 -> x18, matrix products: 336 us -> 177 us  [the longest x12 141 us: dot(): return lax.dot_general(a, b, (dims, ((), ())), preferred_element_type=F32)]
    all_gather x12 -> x3, waiting for transfers between devices: 215 us -> 137 us  [the longest x1 56.1 us: per_device(): mlp_full = lax.all_gather(mlp_shard, fsdp, axis=0, tiled=True)]
    unnamed x459 -> x96, local copies, waits for them, and re-layouts: 40.6 us -> 13.4 us
    psum x1 -> x2, blocking collectives: 24.3 us -> 46.1 us  [the longest x1 25.2 us: per_device(): lax.psum(jnp.concatenate([norm_sums, bias_qkv_sum, jnp.sum(grad_rows, 0),...]
  transfers between devices with their start and end apart: 38 -> 8, of which waited for: 29 -> 8; matrix products, arithmetic and copies ran while one was open for 19% -> 25% of each run, Pallas kernels for 0% -> 0%
where the time goes in v1:
time: 936 us; the launch traced here: 927 us
  waiting for transfers between devices  509 us (54%)
  matrix products  177 us (19%)
  other arithmetic  120 us (13%)
  local copies, waits for them, and re-layouts  58 us (6%)
  blocking collectives  46.1 us (5%)
  between operations  15.8 us (2%)
    dot_general x12, matrix products, dot(): return lax.dot_general(a, b, (dims, ((), ())), preferred_element_type=F32)  141 us
    reduce_scatter x1, waiting for transfers between devices, per_device(): lax.psum_scatter(grad_mlp_weights, fsdp, scatter_dimension=0, tiled=True)  109 us
    psum x1, waiting for transfers between devices, per_device(): branch = lax.psum(partial.astype(BF), 'tensor').astype(F32)  82.7 us
    reduce_scatter x1, waiting for transfers between devices, per_device(): lax.psum_scatter(grad_attn_weights, fsdp, scatter_dimension=0, tiled=True)  67.6 us
    reduce_scatter x1, waiting for transfers between devices, per_device(): lax.psum_scatter(terms, 'seq', scatter_dimension=0, tiled=True).astype(F32)  66.7 us
    all_gather x1, waiting for transfers between devices, per_device(): mlp_full = lax.all_gather(mlp_shard, fsdp, axis=0, tiled=True)  56.1 us
    all_gather x1, waiting for transfers between devices, per_device(): attn_full = lax.all_gather(attn_shard, fsdp, axis=0, tiled=True)  46.1 us
    psum x1, waiting for transfers between devices, per_device(): input_sum = lax.psum(input_part, 'tensor').astype(F32)  45.7 us
  transfers between devices with their start and end apart: 8, of which 8 were waited for; matrix products, arithmetic and copies ran while one was open for 25% of the time, Pallas kernels for 0%

profile of v1, /device:TPU:0, one launch (start us, length us, event | category | flops | bytes accessed | tf_op | source)
XLA Modules:
  0.0 926.7 jit_solution(11766982735649597109)
XLA Ops:
  24.2 46.1 %all-gather.5.cloned.1.call-done = bf16[2048,2048]{0,1:T(8,128)(2,1)} async-done(((bf16[256,2048]{0,1:T(8,128)(2,1)}), bf16[2048,2048]{0,1:T(8,128)(2,1)}) %all-gather.5.cloned.1.call-update) | async-done | bytes 8388624 | tf_op jit(solution)/shard_map/all_gather | solution.py:77
  74.3 6.7 fusion.92
  94.2 7.4 fusion.56
  111.4 35.2 %all-gather.9.cloned.1.call-done = bf16[16,256,2,512]{3,1,2,0:T(8,128)(2,1)} async-done(((bf16[4,256,2,512]{3,1,2,0:T(8,128)(2,1)}), bf16[16,256,2,512]{3,1,2,0:T(8,128)(2,1)}) %all-gather.9.cloned.1.call-update) | async-done | bytes 8388624 | tf_op jit(solution)/shard_map/all_gather | solution.py:103
  146.6 7.6 copy.71
  154.2 7.9 fusion.54
  162.0 14.2 %fusion.93 = (f32[4,2,256]{2,1,0:T(2,128)S(1)}, f32[4,2,256,1024]{2,3,1,0:T(8,128)}) fusion(f32[4,2,256,1024]{2,3,1,0:T(8,128)} %fusion.54, pred[4,256,1024]{1,2,0:T(8,128)(4,1)} %broadcast_and_fusion), kind=kOutput, calls=%fused_computation.137 | output fusion | flops 14681087 | bytes 17833984 | tf_op jit(solution)/shard_map/sub | solution.py:127
  186.1 56.1 %all-gather.7.cloned.1.call-done = bf16[2048,4096]{0,1:T(8,128)(2,1)} async-done(((bf16[256,4096]{0,1:T(8,128)(2,1)}), bf16[2048,4096]{0,1:T(8,128)(2,1)}) %all-gather.7.cloned.1.call-update) | async-done | bytes 16777232 | tf_op jit(solution)/shard_map/all_gather | solution.py:78
  242.2 27.6 %multiply_convert_fusion = (bf16[1024,2048]{1,0:T(8,128)(2,1)}, f32[1024,2048]{1,0:T(8,128)}) fusion(f32[2048]{0:T(1024)S(1)} %copy-done.36, bf16[1024,2048]{1,0:T(8,128)(2,1)} %fusion.19, bf16[2048,4096]{0,1:T(8,128)(2,1)} %all-gather.7.cloned.1.call-done), kind=kOutput, calls=%fused_computation.40 | convolution fusion | flops 8602517504 | bytes 25174016 | tf_op jit(solution)/shard_map/dot_general | solution.py:16
  269.8 12.9 %fusion.33 = f32[1024,2048]{1,0:T(8,128)} fusion(bf16[1024,2048]{1,0:T(8,128)(2,1)} %get-tuple-element.107, bf16[2048,4096]{0,1:T(8,128)(2,1)S(1)} %copy-done.35), kind=kOutput, calls=%fused_computation.56 | convolution fusion | flops 8589934592 | bytes 20971520 | tf_op jit(solution)/shard_map/dot_general | solution.py:16
  282.7 8.5 add_convert_fusion
  307.3 6.6 convert_bitcast_fusion.1
  313.9 7.3 pad_maximum_fusion.1
  333.4 15.7 %fusion.94 = (f32[2048]{0:T(1024)S(1)}, bf16[1024,2048]{1,0:T(8,128)(2,1)}) fusion(f32[1024,2048]{1,0:T(8,128)S(1)} %bitcast.171, f32[2048]{0:T(1024)S(1)} %copy-done.36, bf16[1024,2048]{1,0:T(8,128)(2,1)S(1)} %bitcast_convert_fusion, bf16[2048,4096]{0,1:T(8,128)(2,1)} %all-gather.7.cloned.1.call-done), kind=kOutput, calls=%fused_computation.138 | convolution fusion | flops 8615098368 | bytes 25182208 | tf_op jit(solution)/shard_map/dot_general | solution.py:16
  349.1 14.5 %fusion.29 = f32[1024,2048]{1,0:T(8,128)} fusion(bf16[2048,4096]{0,1:T(8,128)(2,1)} %all-gather.7.cloned.1.call-done, bf16[1024,2048]{1,0:T(8,128)(2,1)} %get-tuple-element.110), kind=kOutput, calls=%fused_computation.52 | convolution fusion | flops 8589934592 | bytes 20971520 | tf_op jit(solution)/shard_map/dot_general | solution.py:16
  363.6 82.7 %all-reduce.3.cloned.1.call-done = bf16[1024,2048]{1,0:T(8,128)(2,1)} async-done(((bf16[1024,2048]{1,0:T(8,128)(2,1)}), bf16[1024,2048]{1,0:T(8,128)(2,1)}) %all-reduce.3.cloned.1.call-update) | async-done | bytes 4194320 | tf_op jit(solution)/shard_map/psum | solution.py:134
  446.3 6.7 convert_element_type.120
  453.0 66.7 %reduce-scatter.4.cloned.1.call-done = bf16[256,4,2,512]{3,0,2,1:T(8,128)(2,1)} async-done(((bf16[1024,4,2,512]{3,0,2,1:T(8,128)(2,1)}), bf16[256,4,2,512]{3,0,2,1:T(8,128)(2,1)}) %reduce-scatter.4.cloned.1.call-update) | async-done | bytes 2097168 | tf_op jit(solution)/shard_map/reduce_scatter | solution.py:150
  527.3 9.6 %concatenate.39 = f32[4,256,2,768]{3,1,2,0:T(8,128)} concatenate(f32[4,256,2,32]{3,1,2,0:T(8,128)} %get-tuple-element.84, f32[4,256,2,32]{3,1,2,0:T(8,128)} %get-tuple-element.85, f32[4,256,2,192]{3,1,2,0:T(8,128)} %slice.163, f32[4,256,2,32]{3,1,2,0:T(8,128)} %get-tuple-element.78, f32[4,256,2,32]{3,1,2,0:T(8,128)S(1)} %get-tuple-element.77, f32[4,256,2,448]{3,1,2,0:T(8,128)} %slice.166), dimensions={3} | concatenate | bytes 12582912 | tf_op jit(solution)/shard_map/concatenate | solution.py:154
  546.1 13.1 %fusion.89 = (f32[1024]{0:T(1024)S(1)}, f32[1024]{0:T(1024)S(1)}, f32[2048]{0:T(1024)S(1)}, f32[2048]{0:T(1024)S(1)}, f32[2048]{0:T(1024)S(1)}, /*index=5*/f32[2048]{0:T(1024)S(1)}, f32[1024,2048]{1,0:T(8,128)S(1)}) fusion(f32[1024]{0:T(1024)S(1)} %bitcast.159, f32[1024]{0:T(1024)S(1)} %bitcast.162, bf16[4,256,2048]{2,1,0:T(8,128)(2,1)S(1)} %copy-done.2, ...), kind=kOutput, calls=%fused_computation.133 | convolution fusion | flops 6473897984 | bytes 30474240 | tf_op jit(solution)/shard_map/dot_general | solution.py:16
  563.1 12.3 %convolution_convert_fusion.1 = bf16[2048,2048]{0,1:T(8,128)(2,1)S(1)} fusion(bf16[1024,2048]{1,0:T(8,128)(2,1)} %fusion.19, bf16[1024,2048]{1,0:T(8,128)(2,1)} %get-tuple-element.110), kind=kOutput, calls=%fused_computation.50 | convolution fusion | flops 8594128896 | bytes 16777216 | tf_op jit(solution)/shard_map/dot_general | solution.py:16
  575.4 10.8 %convolution_convert_fusion = bf16[2048,2048]{0,1:T(8,128)(2,1)S(1)} fusion(bf16[1024,2048]{1,0:T(8,128)(2,1)S(1)} %copy-done.6, bf16[1024,2048]{1,0:T(8,128)(2,1)} %get-tuple-element.107), kind=kOutput, calls=%fused_computation.49 | convolution fusion | flops 8594128896 | bytes 16777216 | tf_op jit(solution)/shard_map/dot_general | solution.py:16
  586.2 7.5 pad_maximum_fusion
  600.1 9.2 convolution_convert_fusion.2
  609.3 8.3 pad_maximum_fusion.2
  617.7 20.8 %psum.30 = f32[8192]{0:T(1024)S(1)} all-reduce(f32[8192]{0:T(1024)S(1)} %bitcast.157), channel_id=1, replica_groups=mesh['seq'=4,'batch'=2,'tensor'=4] {'tensor'}, use_global_device_ids=true, to_apply=%region_15.16 | all-reduce | flops 8192 | bytes 65536 | tf_op jit(solution)/shard_map/psum | solution.py:188
  638.6 25.2 %psum.31 = f32[13824]{0:T(1024)S(1)} all-reduce(f32[13824]{0:T(1024)S(1)} %pad_maximum_fusion.7), channel_id=1, replica_groups=mesh['seq'=4,'batch'=2,'tensor'=4] {'seq','batch'}, use_global_device_ids=true, to_apply=%region_19.20 | all-reduce | flops 13824 | bytes 110592 | tf_op jit(solution)/shard_map/psum | solution.py:189
  665.0 8.4 fusion.28
  673.5 45.7 %all-reduce.5.cloned.1.call-done = bf16[1024,2048]{1,0:T(8,128)(2,1)} async-done(((bf16[1024,2048]{1,0:T(8,128)(2,1)}), bf16[1024,2048]{1,0:T(8,128)(2,1)}) %all-reduce.5.cloned.1.call-update) | async-done | bytes 4194320 | tf_op jit(solution)/shard_map/psum | solution.py:177
  719.1 10.3 %bitcast_add_fusion = f32[1024,2048]{1,0:T(8,128)} fusion(f32[4,256,2048]{2,1,0:T(8,128)} %get-tuple-element.81, bf16[1024,2048]{1,0:T(8,128)(2,1)} %all-reduce.5.cloned.1.call-done), kind=kLoop, calls=%fused_computation.10 | loop fusion | flops 4194304 | bytes 20971520 | tf_op jit(solution)/shard_map/add | solution.py:179
  729.5 108.7 %reduce-scatter.8.cloned.1.call-done = bf16[256,4096]{0,1:T(8,128)(2,1)} async-done(((bf16[2048,4096]{0,1:T(8,128)(2,1)}), bf16[256,4096]{0,1:T(8,128)(2,1)}) %reduce-scatter.8.cloned.1.call-update) | async-done | bytes 2097168 | tf_op jit(solution)/shard_map/reduce_scatter | solution.py:139
  845.6 67.6 %reduce-scatter.6.cloned.1.call-done = bf16[256,2048]{0,1:T(8,128)(2,1)} async-done(((bf16[2048,2048]{0,1:T(8,128)(2,1)}), bf16[256,2048]{0,1:T(8,128)(2,1)}) %reduce-scatter.6.cloned.1.call-update) | async-done | bytes 1048592 | tf_op jit(solution)/shard_map/reduce_scatter | solution.py:184
  (170 shorter events, 122.9 us)
Async XLA Ops:
  7.2 14.0 %copy-start.30 = (f32[2048]{0:T(1024)S(1)}, f32[2048]{0:T(1024)}, u32[]{:S(2)}) copy-start(f32[2048]{0:T(1024)} %param.20) | copy-start | bytes 24580
  7.2 14.0 %copy-start.28 = (f32[2048]{0:T(1024)S(1)}, f32[2048]{0:T(1024)}, u32[]{:S(2)}) copy-start(f32[2048]{0:T(1024)} %param.21) | copy-start | bytes 24580
  7.2 63.1 %all-gather.5.cloned.1.call-start = ((), (), s32[]{:S(2)}) async-start(), calls=%async_computation.3 | async-start | bytes 9437184 | tf_op jit(solution)/shard_map/all_gather | solution.py:77
  11.5 135.0 %all-gather.9.cloned.1.call-start = ((), (), s32[]{:S(2)}) async-start(), calls=%async_computation.10 | async-start | bytes 10485760 | tf_op jit(solution)/shard_map/all_gather | solution.py:103
  13.5 7.6 copy-start
  21.1 62.6 %copy-start.15 = (f32[256,32]{1,0:T(8,128)}, f32[256,32]{1,0:T(8,128)S(1)}, u32[]{:S(2)}) copy-start(f32[256,32]{1,0:T(8,128)S(1)} %get-tuple-element.98) | copy-start | bytes 98308
  24.2 46.2 %copy-start.37 = (f32[2,768]{1,0:T(2,128)S(1)}, f32[2,768]{1,0:T(2,128)}, u32[]{:S(2)}) copy-start(f32[2,768]{1,0:T(2,128)} %param.25) | copy-start | bytes 18436
  88.1 154.1 %all-gather.7.cloned.1.call-start = ((), (), s32[]{:S(2)}) async-start(), calls=%async_computation.5 | async-start | bytes 18874368 | tf_op jit(solution)/shard_map/all_gather | solution.py:78
  91.4 354.9 %all-reduce.3.cloned.1.call-start = ((), (), s32[]{:S(2)}) async-start(), calls=%async_computation.6 | async-start | bytes 8388608 | tf_op jit(solution)/shard_map/psum | solution.py:134
  91.8 9.8 %copy-start.20 = (f32[1,2,4,128]{3,1,2,0:T(2,128)}, f32[1,2,4,128]{3,1,2,0:T(2,128)S(1)}, u32[]{:S(2)}) copy-start(f32[1,2,4,128]{3,1,2,0:T(2,128)S(1)} %copy.107) | copy-start | bytes 12292
  91.8 9.8 %copy-start.22 = (f32[1,2,4,128]{3,1,2,0:T(2,128)}, f32[1,2,4,128]{3,1,2,0:T(2,128)S(1)}, u32[]{:S(2)}) copy-start(f32[1,2,4,128]{3,1,2,0:T(2,128)S(1)} %copy.110) | copy-start | bytes 12292
  146.5 7.6 copy-start.4
  146.5 7.6 copy-start.13
  154.2 22.1 %slice-start = ((s8[8388608]{0:T(1024)(128)(4,1)}), s8[4194304]{0:T(1024)(128)(4,1)S(1)}, s32[]{:S(2)}) async-start(s8[8388608]{0:T(1024)(128)(4,1)} %bitcast.137), calls=%async_computation.11 | async-start | bytes 8388608
  162.0 14.2 %slice-start.1 = ((s8[8388608]{0:T(1024)(128)(4,1)}), s8[4194304]{0:T(1024)(128)(4,1)S(1)}, s32[]{:S(2)}) async-start(s8[8388608]{0:T(1024)(128)(4,1)} %bitcast.137), calls=%async_computation.12 | async-start | bytes 8388608
  176.3 65.9 %copy-start.36 = (f32[2048]{0:T(1024)S(1)}, f32[2048]{0:T(1024)}, u32[]{:S(2)}) copy-start(f32[2048]{0:T(1024)} %param.29) | copy-start | bytes 24580
  242.2 27.6 %copy-start.35 = (bf16[2048,4096]{0,1:T(8,128)(2,1)S(1)}, bf16[2048,4096]{0,1:T(8,128)(2,1)}, u32[]{:S(2)}) copy-start(bf16[2048,4096]{0,1:T(8,128)(2,1)} %all-gather.7.cloned.1.call-done) | copy-start | bytes 50331652
  269.8 12.9 %copy-start.18 = (bf16[128,8,2,256]{3,1,2,0:T(8,128)(2,1)S(1)}, bf16[128,8,2,256]{3,1,2,0:T(8,128)(2,1)}, u32[]{:S(2)}) copy-start(bf16[128,8,2,256]{3,1,2,0:T(8,128)(2,1)} %copy.111) | copy-start | bytes 3145732
  291.1 228.5 %reduce-scatter.4.cloned.1.call-start = ((), (), s32[]{:S(2)}) async-start(), calls=%async_computation.4 | async-start | bytes 10485760 | tf_op jit(solution)/shard_map/reduce_scatter | solution.py:150
  321.2 397.9 %all-reduce.5.cloned.1.call-start = ((), (), s32[]{:S(2)}) async-start(), calls=%async_computation.7 | async-start | bytes 8388608 | tf_op jit(solution)/shard_map/psum | solution.py:177
  321.3 12.1 %slice-start.4 = ((s8[8388608]{0:T(1024)(128)(4,1)}), s8[4194304]{0:T(1024)(128)(4,1)S(1)}, s32[]{:S(2)}) async-start(s8[8388608]{0:T(1024)(128)(4,1)} %bitcast.170), calls=%async_computation.15 | async-start | bytes 8388608
  325.9 7.5 copy-start.5
  325.9 7.5 slice-start.5
  453.0 72.0 %copy-start.16 = (f32[256,32]{1,0:T(8,128)S(1)}, f32[256,32]{1,0:T(8,128)}, u32[]{:S(2)}) copy-start(f32[256,32]{1,0:T(8,128)} %copy-done.15) | copy-start | bytes 98308
  453.0 72.0 %copy-start.19 = (f32[256,32]{1,0:T(8,128)S(1)}, f32[256,32]{1,0:T(8,128)}, u32[]{:S(2)}) copy-start(f32[256,32]{1,0:T(8,128)} %get-tuple-element.96) | copy-start | bytes 98308
  563.0 275.1 %reduce-scatter.8.cloned.1.call-start = ((), (), s32[]{:S(2)}) async-start(), calls=%async_computation.9 | async-start | bytes 18874368 | tf_op jit(solution)/shard_map/reduce_scatter | solution.py:139
  563.1 12.4 %copy-start.6 = (bf16[1024,2048]{1,0:T(8,128)(2,1)S(1)}, bf16[1024,2048]{1,0:T(8,128)(2,1)}, u32[]{:S(2)}) copy-start(bf16[1024,2048]{1,0:T(8,128)(2,1)} %copy-done.5) | copy-start | bytes 12582916
  593.7 319.6 %reduce-scatter.6.cloned.1.call-start = ((), (), s32[]{:S(2)}) async-start(), calls=%async_computation.8 | async-start | bytes 9437184 | tf_op jit(solution)/shard_map/reduce_scatter | solution.py:184
  617.6 21.0 %copy-start.24 = (f32[2048]{0:T(1024)S(1)}, f32[2048]{0:T(1024)}, u32[]{:S(2)}) copy-start(f32[2048]{0:T(1024)} %get-tuple-element.79) | copy-start | bytes 24580
  617.6 47.4 %copy-start.26 = (f32[2048]{0:T(1024)S(1)}, f32[2048]{0:T(1024)}, u32[]{:S(2)}) copy-start(f32[2048]{0:T(1024)} %param.31) | copy-start | bytes 24580
  617.6 47.4 %copy-start.27 = (f32[2048]{0:T(1024)S(1)}, f32[2048]{0:T(1024)}, u32[]{:S(2)}) copy-start(f32[2048]{0:T(1024)} %param.27) | copy-start | bytes 24580
  664.4 254.4 %copy-start.25 = (f32[2048]{0:T(1024)}, f32[2048]{0:T(1024)S(1)}, u32[]{:S(2)}) copy-start(f32[2048]{0:T(1024)S(1)} %get-tuple-element.142) | copy-start | bytes 24580
  (21 other events, 103.4 us)
Sparse Core Ops, SparseCore 0:
  11.6 58.6 all-gather.4
  88.2 58.2 all-gather.8
  149.0 93.1 all-gather.6
  291.3 154.9 all-reduce.2
  448.9 70.7 reduce-scatter.3
  563.1 155.9 all-reduce.4
  723.1 114.9 reduce-scatter.7
  842.0 71.2 reduce-scatter.5

commit v2 on v1

--- a/solution.py
+++ b/solution.py
@@ -1,6 +1,8 @@
 import jax
 import jax.numpy as jnp
 from jax import lax
+from jax.experimental import pallas as pl
+from jax.experimental.pallas import tpu as pltpu
 from jax.sharding import PartitionSpec as P
 
 D = 2048
@@ -38,7 +40,7 @@
     return z * phi_cdf, phi_cdf + z * density
 
 
-def per_device(
+def per_device_any(
     tokens,
     cotangent,
     lengths,
@@ -212,6 +214,554 @@
     )
 
 
+def exchange(array, axis, flip):
+    size = lax.axis_size(axis)
+    return lax.ppermute(array, axis, [(i, i ^ flip) for i in range(size)])
+
+
+def after(array, *others):
+    return lax.optimization_barrier((array, *others))[0]
+
+
+def gather_blocks(shard):
+    by_x = exchange(shard, "seq", 2)
+    by_y = exchange(shard, "batch", 1)
+    half = shard.shape[0] // 2
+    far = jnp.concatenate(
+        [exchange(by_x[:half], "batch", 1), exchange(by_y[half:], "seq", 2)], 0
+    )
+    mine = [shard, by_y, by_x, far]
+    other = [exchange(block, "seq", 1) for block in mine]
+    return [mine[0], mine[1], other[0], other[1], mine[2], mine[3], other[2], other[3]], far
+
+
+def call(body, grid, ins, outs, scratch=(), flops=0, moved=0):
+    return pl.pallas_call(
+        body,
+        grid=grid,
+        in_specs=[spec for spec, _ in ins],
+        out_specs=[spec for spec, _ in outs],
+        out_shape=[shape for _, shape in outs],
+        scratch_shapes=list(scratch),
+        compiler_params=pltpu.CompilerParams(vmem_limit_bytes=60 * 1024 * 1024),
+        cost_estimate=pl.CostEstimate(flops=flops, bytes_accessed=moved, transcendentals=0),
+    )(*[array for _, array in ins])
+
+
+def smem():
+    return pl.BlockSpec(memory_space=pltpu.SMEM)
+
+
+def whole(array):
+    dims = len(array.shape)
+    return pl.BlockSpec(array.shape, lambda *_: (0,) * dims)
+
+
+def block(shape, index):
+    return pl.BlockSpec(shape, index)
+
+
+def struct(shape, dtype):
+    return jax.ShapeDtypeStruct(shape, dtype)
+
+
+def columns(ref, info, place):
+    start = pl.multiple_of((info[0] ^ place) * 256, 256)
+    return ref[:, pl.ds(start, 256)]
+
+
+def norm_body(info, tok, cot, gain_a, shift_a, gain_m, shift_m, in_a, in_m, grad, grad_sum):
+    step = pl.program_id(0)
+    t = tok[...].astype(F32)
+    centered = t - jnp.mean(t, -1, keepdims=True)
+    xhat = centered * lax.rsqrt(jnp.mean(centered * centered, -1, keepdims=True) + EPS)
+    in_a[...] = (xhat * gain_a[...] + shift_a[...]).astype(BF)
+    in_m[...] = (xhat * gain_m[...] + shift_m[...]).astype(BF)
+    place = info[1] * 256 + lax.broadcasted_iota(jnp.int32, t.shape, 0)
+    g = jnp.where(place < info[5 + step], cot[...].astype(F32), 0.0)
+    grad[...] = g.astype(BF)
+
+    @pl.when(step == 0)
+    def _():
+        grad_sum[...] = jnp.zeros_like(grad_sum)
+
+    grad_sum[...] += jnp.sum(g, 0, keepdims=True)
+
+
+def matched(x, blocks, info):
+    left = jnp.concatenate([columns(x, info, r) for r in range(8)], 1)
+    right = jnp.concatenate([b[...] for b in blocks], 0)
+    return jnp.dot(left, right, preferred_element_type=F32)
+
+
+def turn(z, cos, front, back):
+    first = z[:, :128]
+    first = (
+        first * cos
+        + pltpu.roll(first, 96, 1) * front
+        + pltpu.roll(first, 32, 1) * back
+    )
+    return jnp.concatenate([first, z[:, 128:]], 1)
+
+
+def qkv_body(info, x, bias, cos, front, back, *refs):
+    blocks, (q, kv_a, kv_b) = refs[:8], refs[8:]
+    step = pl.program_id(0)
+    z = matched(x, blocks, info) + bias[...]
+
+    def turned():
+        c, f, b = (jnp.concatenate([t[...]] * 4, 0) for t in (cos, front, back))
+        return turn(z, c, f, b).astype(BF)
+
+    @pl.when(step < 2)
+    def _():
+        q[...] = turned()
+
+    @pl.when((step >= 2) & (step < 4))
+    def _():
+        k = turned()
+        kv_a[...] = k[:512]
+        kv_b[...] = k[512:]
+
+    @pl.when(step >= 4)
+    def _():
+        v = z.astype(BF)
+        kv_a[...] = v[:512]
+        kv_b[...] = v[512:]
+
+
+def grad_att_body(info, g, *refs):
+    refs[8][...] = matched(g, refs[:8], info).astype(BF)
+
+
+ERFC = (
+    0.17087277,
+    -0.82215223,
+    1.48851587,
+    -1.13520398,
+    0.27886807,
+    -0.18628806,
+    0.09678418,
+    0.37409196,
+    1.00002368,
+    -1.26551223,
+)
+
+
+def gelu_terms(z):
+    size = jnp.abs(z)
+    t = 1.0 / (1.0 + size * 0.35355339059327373)
+    p = jnp.full_like(t, ERFC[0])
+    for c in ERFC[1:]:
+        p = p * t + c
+    square = -0.5 * z * z
+    tail = 0.5 * t * jnp.exp(square + p)
+    return jnp.where(z < 0, tail, 1.0 - tail), 0.3989422804014327 * jnp.exp(square)
+
+
+def up_body(info, x, bias, *refs):
+    blocks, (act, slope) = refs[:8], refs[8:]
+    z = matched(x, blocks, info) + bias[...]
+    phi, density = gelu_terms(z)
+    act[...] = (z * phi).astype(BF)
+    slope[...] = (phi + z * density).astype(BF)
+
+
+def hidden_body(info, g, slope, *refs):
+    blocks, (low, total) = refs[:8], refs[8:]
+    grad = matched(g, blocks, info) * slope[...].astype(F32)
+    low[...] = grad.astype(BF)
+    total[...] = jnp.sum(grad, 0, keepdims=True)
+
+
+def nt(a, b):
+    return lax.dot_general(a, b, (((1,), (1,)), ((), ())), preferred_element_type=F32)
+
+
+def tn(a, b):
+    return lax.dot_general(a, b, (((0,), (0,)), ((), ())), preferred_element_type=F32)
+
+
+def attention_body(first_seq, info, q_ref, ga_ref, cos, front, back, *refs):
+    keys, values = refs[:4], refs[4:8]
+    att, dq, dq_sum, terms = refs[8], refs[9], refs[10], refs[11:]
+    seq = pl.program_id(0)
+    head = pl.program_id(1)
+    scale = HEAD_DIM ** (-0.5)
+    length = info[5 + first_seq + seq]
+    q = q_ref[...]
+    ga = ga_ref[...]
+    row_place = info[1] * 256 + lax.broadcasted_iota(jnp.int32, (256, 256), 0)
+    column = lax.broadcasted_iota(jnp.int32, (256, 256), 1)
+    scores = []
+    masks = []
+    for r in range(4):
+        key_place = info[1 + r] * 256 + column
+        allowed = (key_place <= row_place) & (key_place < length)
+        masks.append(allowed)
+        scores.append(jnp.where(allowed, nt(q, keys[r][...]) * scale, FLOOR))
+    top = jnp.max(jnp.maximum(jnp.maximum(scores[0], scores[1]), jnp.maximum(scores[2], scores[3])), -1, keepdims=True)
+    weights = [jnp.where(m, jnp.exp(s - top), 0.0) for s, m in zip(scores, masks)]
+    total = jnp.sum(weights[0] + weights[1] + weights[2] + weights[3], -1, keepdims=True)
+    inverse = 1.0 / total
+    probs = [w * inverse for w in weights]
+    low = [p.astype(BF) for p in probs]
+    out = jnp.zeros((256, 256), F32)
+    for r in range(4):
+        out += jnp.dot(low[r], values[r][...], preferred_element_type=F32)
+    att[...] = out.astype(BF)
+    grad_probs = [nt(ga, values[r][...]) for r in range(4)]
+    products = [p * g for p, g in zip(probs, grad_probs)]
+    delta = jnp.sum(products[0] + products[1] + products[2] + products[3], -1, keepdims=True)
+    grad_q = jnp.zeros((256, 256), F32)
+    key_columns = pl.ds(pl.multiple_of(head * 256, 256), 256)
+    value_columns = pl.ds(pl.multiple_of(head * 256 + 512, 256), 256)
+    for r in range(4):
+        grad_scores = (probs[r] * (grad_probs[r] - delta)).astype(BF)
+        grad_q += jnp.dot(grad_scores, keys[r][...], preferred_element_type=F32)
+        terms[r][:, key_columns] = (tn(grad_scores, q) * scale).astype(BF)
+        terms[r][:, value_columns] = tn(low[r], ga).astype(BF)
+    grad_q = turn(grad_q * scale, cos[...], -front[...], -back[...])
+    dq[...] = grad_q.astype(BF)
+    dq_sum[...] = jnp.sum(grad_q, 0, keepdims=True)[None, None]
+
+
+def branch_body(info, att, act, *refs):
+    w_att, w_act, out = refs[:8], refs[8:16], refs[16]
+    for r in range(8):
+        start = pl.multiple_of((info[0] ^ r) * 256, 256)
+        part = nt(att[...], w_att[r][...]) + nt(act[...], w_act[r][...])
+        out[:, pl.ds(start, 256)] = part.astype(BF)
+
+
+def weight_send_body(places, info, x, h, out):
+    for i, r in enumerate(places):
+        out[i * 256 : (i + 1) * 256, :] = tn(columns(x, info, r), h[...]).astype(BF)
+
+
+def weight_add_body(places, info, x, h, received, send, keep):
+    for i, r in enumerate(places):
+        part = tn(columns(x, info, r), h[...]) + received[i * 256 : (i + 1) * 256, :].astype(F32)
+        if i < 2:
+            keep[i * 256 : (i + 1) * 256, :] = part.astype(BF)
+        else:
+            send[(i - 2) * 256 : (i - 1) * 256, :] = part.astype(BF)
+
+
+def weight_gradient(info, x, h, start, width, x_first):
+    rows = x.shape[0]
+    order = (0, 1, 4, 5) if x_first else (0, 4, 1, 5)
+    tile = 512
+    steps = width // tile
+    base = start // tile
+    cost = dict(flops=2 * rows * 1024 * width, moved=2 * (rows * (2048 + width) + 1024 * width))
+    ins = [
+        (smem(), info),
+        (whole(x), x),
+        (block((rows, tile), lambda j: (0, base + j)), h),
+    ]
+    column = lambda j: (0, j)
+    sent = call(
+        lambda *refs: weight_send_body([r ^ 2 for r in order], *refs),
+        (steps,),
+        ins,
+        [(block((1024, tile), column), struct((1024, width), BF))],
+        **cost,
+    )[0]
+    received = exchange(sent, "seq", 1)
+    send, keep = call(
+        lambda *refs: weight_add_body(order, *refs),
+        (steps,),
+        ins + [(block((1024, tile), column), received)],
+        [(block((512, tile), column), struct((512, width), BF))] * 2,
+        **cost,
+    )
+    first, second = (("seq", 2), ("batch", 1)) if x_first else (("batch", 1), ("seq", 2))
+    got = exchange(send, *first)
+    summed = keep.astype(F32) + got.astype(F32)
+    last = exchange(summed[256:].astype(BF), *second)
+    return summed[:256] + last.astype(F32)
+
+
+def input_body(seqs, info, q_low, own, core, far, hid, tok, cos, front, back, gain_a, gain_m, *refs):
+    w_qkv, w_up = refs[:8], refs[8:16]
+    part, low, kv_sum, sums, gx, xh = refs[16:]
+    step = pl.program_id(0)
+    t = tok[...].astype(F32)
+    centered = t - jnp.mean(t, -1, keepdims=True)
+    inverse = lax.rsqrt(jnp.mean(centered * centered, -1, keepdims=True) + EPS)
+    xh[...] = centered * inverse
+    terms = own[...].astype(F32) + core[...].astype(F32) + far[...].astype(F32)
+    pieces = []
+    kv_sums = []
+    for head in range(2):
+        grad_k = turn(terms[:, head * 256 : head * 256 + 256], cos[...], -front[...], -back[...])
+        grad_v = terms[:, 512 + head * 256 : 768 + head * 256]
+        kv_sums += [jnp.sum(grad_k, 0, keepdims=True), jnp.sum(grad_v, 0, keepdims=True)]
+        pieces += [q_low[:, head * 256 : head * 256 + 256], grad_k.astype(BF), grad_v.astype(BF)]
+    low[...] = jnp.concatenate(pieces, 1)
+    kv_sum[...] = jnp.concatenate(kv_sums, 1)[None]
+
+    @pl.when(step == 0)
+    def _():
+        sums[...] = jnp.zeros_like(sums)
+
+    for r in range(8):
+        there = pl.ds(pl.multiple_of((info[0] ^ r) * 256, 256), 256)
+        from_attn = nt(low[...], w_qkv[r][:, :1536])
+        from_mlp = nt(hid[...], w_up[r][...])
+        xhat = xh[:, there]
+        sums[0:1, there] += jnp.sum(from_attn * xhat, 0, keepdims=True)
+        sums[1:2, there] += jnp.sum(from_attn, 0, keepdims=True)
+        sums[2:3, there] += jnp.sum(from_mlp * xhat, 0, keepdims=True)
+        sums[3:4, there] += jnp.sum(from_mlp, 0, keepdims=True)
+        gx[:, there] = from_attn * gain_a[:, there] + from_mlp * gain_m[:, there]
+    grad = gx[...]
+    xhat = xh[...]
+    mean = jnp.mean(grad, -1, keepdims=True)
+    along = jnp.mean(grad * xhat, -1, keepdims=True)
+    part[...] = (inverse * (grad - mean - xhat * along)).astype(BF)
+
+
+def per_device_links(
+    tokens,
+    cotangent,
+    lengths,
+    block_slot,
+    gain_attn,
+    shift_attn,
+    gain_mlp,
+    shift_mlp,
+    w_qkv,
+    b_qkv,
+    w_out,
+    b_out,
+    w_up,
+    b_up,
+    w_down,
+    b_down,
+):
+    rows = 1024
+    seq_id = lax.axis_index("seq")
+    slots = [jnp.sum(jnp.where(jnp.arange(4) == (seq_id ^ r), block_slot, 0)) for r in range(4)]
+    info = jnp.concatenate(
+        [jnp.stack([seq_id * 2 + lax.axis_index("batch"), *slots]), lengths]
+    ).astype(jnp.int32)
+    tok = tokens.reshape(rows, D)
+    cot = cotangent.reshape(rows, D)
+    cosine, sine = rotation(slots[0] * 256 + jnp.arange(256, dtype=jnp.int32))
+    cosine, sine = cosine[:, 0], sine[:, 0]
+    zero = jnp.zeros_like(sine)
+    cos_t = jnp.concatenate([cosine, cosine, zero + 1.0, zero + 1.0], 1)
+    front_t = jnp.concatenate([-sine, zero, zero, zero], 1)
+    back_t = jnp.concatenate([zero, sine, zero, zero], 1)
+    tables = [(whole(t), t) for t in (cos_t, front_t, back_t)]
+    info_in = (smem(), info)
+    gains = [v.reshape(1, D) for v in (gain_attn, shift_attn, gain_mlp, shift_mlp)]
+
+    attn_shard = jnp.concatenate([w_qkv.reshape(256, 1536), w_out.T], 1)
+    attn_blocks, mark = gather_blocks(attn_shard)
+    up_blocks, mark = gather_blocks(after(w_up, mark))
+    down_blocks, mark = gather_blocks(after(w_down.T, mark))
+
+    row_block = lambda n: block((256, n), lambda i: (i, 0))
+    row_struct = lambda n, kind=BF: struct((rows, n), kind)
+    in_a, in_m, grad_low, grad_sum = call(
+        norm_body,
+        (4,),
+        [info_in, (row_block(D), tok), (row_block(D), cot)] + [(whole(v), v) for v in gains],
+        [(row_block(D), row_struct(D))] * 3 + [(block((1, D), lambda i: (0, 0)), struct((1, D), F32))],
+        moved=5 * rows * D * 2,
+    )
+
+    bias = b_qkv.reshape(1, 1536)
+    place = lambda j: (j % 2) * 3 + j // 2
+    tall = lambda index: block((256, 256), index)
+    q, kv_a, kv_b = call(
+        qkv_body,
+        (6,),
+        [info_in, (whole(in_a), in_a), (block((1, 256), lambda j: (0, place(j))), bias)]
+        + tables
+        + [(tall(lambda j: (0, place(j))), b) for b in attn_blocks],
+        [
+            (block((rows, 256), lambda j: (0, jnp.minimum(j, 1))), row_struct(512)),
+            (block((512, 256), lambda j: (0, jnp.maximum(j - 2, 0))), struct((512, 1024), BF)),
+            (block((512, 256), lambda j: (0, jnp.maximum(j - 2, 0))), struct((512, 1024), BF)),
+        ],
+        flops=2 * rows * D * 1536,
+        moved=2 * (rows * D + D * 1536 + rows * 1536),
+    )
+    grad_att = call(
+        grad_att_body,
+        (2,),
+        [info_in, (whole(grad_low), grad_low)] + [(tall(lambda j: (0, 6 + j)), b) for b in attn_blocks],
+        [(block((rows, 256), lambda j: (0, j)), row_struct(512))],
+        flops=2 * rows * D * 512,
+        moved=2 * (rows * D + D * 512 + rows * 512),
+    )[0]
+
+    def spread(own):
+        far = exchange(own, "seq", 2)
+        return [own, exchange(own, "seq", 1), far, exchange(far, "seq", 1)]
+
+    kv = [spread(kv_a), spread(kv_b)]
+
+    act, slope = call(
+        up_body,
+        (8,),
+        [info_in, (whole(in_m), in_m), (block((1, 256), lambda j: (0, j)), b_up.reshape(1, -1))]
+        + [(tall(lambda j: (0, j)), b) for b in up_blocks],
+        [(block((rows, 256), lambda j: (0, j)), row_struct(2048))] * 2,
+        flops=2 * rows * D * 2048,
+        moved=2 * (rows * D + D * 2048 + 2 * rows * 2048),
+    )
+
+    def attention(part):
+        base = part * 2
+        spot = lambda offset: block((256, 256), lambda s, h: (s + base, h + offset))
+        local = lambda offset: block((256, 256), lambda s, h: (s, h + offset))
+        return call(
+            lambda *refs: attention_body(base, *refs),
+            (2, 2),
+            [info_in, (spot(0), q), (spot(0), grad_att)]
+            + tables
+            + [(local(0), b) for b in kv[part]]
+            + [(local(2), b) for b in kv[part]],
+            [
+                (local(0), struct((512, 512), BF)),
+                (local(0), struct((512, 512), BF)),
+                (block((1, 1, 1, 256), lambda s, h: (s, h, 0, 0)), struct((2, 2, 1, 256), F32)),
+            ]
+            + [(block((256, 1024), lambda s, h: (s, 0)), struct((512, 1024), BF))] * 4,
+            flops=4 * 6 * 2 * 256 * 1024 * 256,
+            moved=4 * 2 * 256 * 256 * 24,
+        )
+
+    att = []
+    dq = []
+    dq_sums = []
+    branch = []
+    kv_terms = []
+    for part in range(2):
+        att_p, dq_p, dq_sum, *terms = attention(part)
+        att.append(att_p)
+        dq.append(dq_p)
+        dq_sums.append(dq_sum)
+        branch.append(
+            call(
+                branch_body,
+                (2,),
+                [info_in, (row_block(512), att_p), (block((256, 2048), lambda i, part=part: (i + 2 * part, 0)), act)]
+                + [(block((256, 512), lambda i: (0, 3)), b) for b in attn_blocks]
+                + [(whole(b), b) for b in down_blocks],
+                [(row_block(D), struct((512, D), BF))],
+                flops=2 * 512 * D * 2560,
+                moved=2 * (512 * 2560 + D * 2560 + 512 * D),
+            )[0]
+        )
+        from_core = exchange(terms[1], "seq", 1)
+        far_core = exchange(terms[3], "seq", 1)
+        far = exchange((terms[2].astype(F32) + far_core.astype(F32)).astype(BF), "seq", 2)
+        kv_terms.append((terms[0], from_core, far))
+
+    hidden_low, b_up_sum = call(
+        hidden_body,
+        (8,),
+        [info_in, (whole(grad_low), grad_low), (block((rows, 256), lambda j: (0, j)), slope)]
+        + [(tall(lambda j: (0, j)), b) for b in down_blocks],
+        [
+            (block((rows, 256), lambda j: (0, j)), row_struct(2048)),
+            (block((1, 256), lambda j: (0, j)), struct((1, 2048), F32)),
+        ],
+        flops=2 * rows * D * 2048,
+        moved=2 * (rows * D + D * 2048 + 2 * rows * 2048),
+    )
+
+    branch_sum = lax.psum(jnp.concatenate(branch, 0), "tensor")
+
+    parts = []
+    lows = []
+    kv_sums = []
+    norm_sums = []
+    for part in range(2):
+        shifted = lambda n, part=part: block((256, n), lambda i: (i + 2 * part, 0))
+        own, core, far = kv_terms[part]
+        part_p, low_p, kv_sum, sums = call(
+            lambda *refs: input_body(2, *refs),
+            (2,),
+            [
+                info_in,
+                (row_block(512), dq[part]),
+                (row_block(1024), own),
+                (row_block(1024), core),
+                (row_block(1024), far),
+                (shifted(2048), hidden_low),
+                (shifted(D), tok),
+            ]
+            + tables
+            + [(whole(v), v) for v in (gains[0], gains[2])]
+            + [(whole(b), b) for b in attn_blocks]
+            + [(whole(b), b) for b in up_blocks],
+            [
+                (row_block(D), struct((512, D), BF)),
+                (row_block(1536), struct((512, 1536), BF)),
+                (block((1, 1, 1024), lambda i: (i, 0, 0)), struct((2, 1, 1024), F32)),
+                (block((8, D), lambda i: (0, 0)), struct((8, D), F32)),
+            ],
+            scratch=[pltpu.VMEM((256, D), F32), pltpu.VMEM((256, D), F32)],
+            flops=2 * 512 * D * 3584,
+            moved=2 * (512 * 8192 + D * 3584),
+        )
+        parts.append(part_p)
+        lows.append(low_p)
+        kv_sums.append(kv_sum)
+        norm_sums.append(sums)
+
+    project_low = jnp.concatenate(lows, 0)
+    attended = jnp.concatenate(att, 0)
+    down_grad = weight_gradient(info, grad_low, act, 0, 2048, False)
+    up_grad = weight_gradient(info, in_m, hidden_low, 0, 2048, True)
+    qkv_grad_a = weight_gradient(info, in_a, project_low, 0, 1024, True)
+    qkv_grad_b = weight_gradient(info, in_a, project_low, 1024, 512, False)
+    out_grad = weight_gradient(info, grad_low, attended, 0, 512, False)
+
+    input_part = after(jnp.concatenate(parts, 0), branch_sum)
+    input_sum = lax.psum(input_part, "tensor")
+
+    q_sums = (dq_sums[0] + dq_sums[1]).sum(0).reshape(2, 1, 256)
+    kv_total = (kv_sums[0] + kv_sums[1]).sum(0).reshape(2, 2, 256)
+    bias_qkv = jnp.concatenate([q_sums, kv_total], 1).reshape(-1)
+    norm_total = (norm_sums[0] + norm_sums[1])[:4].reshape(-1)
+    small = jnp.concatenate([norm_total, bias_qkv, grad_sum[0], b_up_sum[0]]).reshape(-1, 128)
+    for axis, flip in (("seq", 1), ("seq", 2), ("batch", 1)):
+        small = small + exchange(small, axis, flip)
+    norms = small[:64]
+    for flip in (1, 2):
+        norms = norms + exchange(norms, "tensor", flip)
+    norms = norms.reshape(4, D)
+    small = small[64:].reshape(-1)
+
+    mixed = (tok.astype(F32) + branch_sum.astype(F32) + b_out + b_down).astype(BF)
+    tokens_grad = grad_low.astype(F32) + input_sum.astype(F32)
+    bias_out = small[1536 : 1536 + D]
+    return (
+        mixed.reshape(tokens.shape),
+        tokens_grad.reshape(tokens.shape),
+        norms[0],
+        norms[1],
+        norms[2],
+        norms[3],
+        jnp.concatenate([qkv_grad_a, qkv_grad_b], 1).reshape(w_qkv.shape),
+        small[:1536].reshape(b_qkv.shape),
+        out_grad.T,
+        bias_out,
+        up_grad,
+        small[1536 + D :],
+        down_grad.T,
+        bias_out,
+    )
+
+
 def solution(mesh):
     in_specs = (
         P("batch", "seq", None),
@@ -247,6 +797,8 @@
         P("tensor", ("seq", "batch")),
         P(),
     )
+    links = tuple(mesh.shape[axis] for axis in ("seq", "batch", "tensor"))
+    per_device = per_device_links if links == (4, 2, 4) else per_device_any
     return jax.shard_map(
         per_device, mesh=mesh, in_specs=in_specs, out_specs=out_specs, check_vma=False
     )

time: 936 us -> 615 us (0.66)
  waiting for transfers between devices: 509 us -> 237 us
  Pallas kernels: 0 us -> 226 us
  matrix products: 177 us -> 0 us
  other arithmetic: 120 us -> 46.8 us
  blocking collectives: 46.1 us -> 0 us
  starting transfers between devices: 0.59 us -> 42.9 us
  local copies, waits for them, and re-layouts: 58 us -> 43 us
    reduce_scatter x3 -> x0, waiting for transfers between devices: 243 us -> none  [the longest x1 109 us: per_device(): lax.psum_scatter(grad_mlp_weights, fsdp, scatter_dimension=0, tiled=True)]
    pallas_call x0 -> x21, Pallas kernels: none -> 226 us  [call(): pl.pallas_call(body, grid=grid, in_specs=[spec for spec, _ in ins], out_s...]
    dot_general x18 -> x0, matrix products: 177 us -> none  [the longest x12 141 us: dot(): return lax.dot_general(a, b, (dims, ((), ())), preferred_element_type=F32)]
    ppermute x0 -> x56, waiting for transfers between devices: none -> 172 us  [exchange(): return lax.ppermute(array, axis, [(i, i ^ flip) for i in range(size)])]
    all_gather x3 -> x0, waiting for transfers between devices: 137 us -> none  [the longest x1 56.1 us: per_device(): mlp_full = lax.all_gather(mlp_shard, fsdp, axis=0, tiled=True)]
    psum x2, waiting for transfers between devices: 128 us -> 65.2 us  [the longest x1 65.2 us: per_device_links(): input_sum = lax.psum(input_part, 'tensor')]
    psum x2 -> x0, blocking collectives: 46.1 us -> none  [the longest x1 25.2 us: per_device(): lax.psum(jnp.concatenate([norm_sums, bias_qkv_sum, jnp.sum(grad_rows, 0),...]
    ppermute x0 -> x56, starting transfers between devices: none -> 42.8 us  [exchange(): return lax.ppermute(array, axis, [(i, i ^ flip) for i in range(size)])]
  transfers between devices with their start and end apart: 8 -> 58, of which waited for: 8 -> 18; matrix products, arithmetic and copies ran while one was open for 25% -> 12% of each run, Pallas kernels for 0% -> 37%
where the time goes in v2:
time: 615 us; the launch traced here: 611 us
  waiting for transfers between devices  237 us (39%)
  Pallas kernels  226 us (37%)
  other arithmetic  46.8 us (8%)
  local copies, waits for them, and re-layouts  43 us (7%)
  starting transfers between devices  42.9 us (7%)
  between operations  15.6 us (3%)
    pallas_call x21, Pallas kernels, call(): pl.pallas_call(body, grid=grid, in_specs=[spec for spec, _ in ins], out_s...  226 us
    ppermute x56, waiting for transfers between devices, exchange(): return lax.ppermute(array, axis, [(i, i ^ flip) for i in range(size)])  172 us
    psum x1, waiting for transfers between devices, per_device_links(): input_sum = lax.psum(input_part, 'tensor')  65.2 us
    ppermute x56, starting transfers between devices, exchange(): return lax.ppermute(array, axis, [(i, i ^ flip) for i in range(size)])  42.8 us
    unnamed x85, local copies, waits for them, and re-layouts  20.7 us
  transfers between devices with their start and end apart: 58, of which 18 were waited for; matrix products, arithmetic and copies ran while one was open for 12% of the time, Pallas kernels for 37%

profile of v2, /device:TPU:0, one launch (start us, length us, event | category | flops | bytes accessed | tf_op | source)
XLA Modules:
  0.0 611.0 jit_solution(5649283730404876474)
XLA Ops:
  14.2 21.6 %collective-permute-done.3.refs_4_.refs_16_ = bf16[256,2048]{1,0:T(8,128)(2,1)S(1)} collective-permute-done((bf16[256,2048]{1,0:T(8,128)(2,1)S(1)}, bf16[256,2048]{1,0:T(8,128)(2,1)S(1)}, u32[]{:S(2)}, u32[]{:S(2)}) %collective-permute-start.3) | collective-permute-done | bytes 1048608 | tf_op jit(solution)/shard_map/ppermute | solution.py:219
  39.4 9.7 %collective-permute-done.4 = bf16[128,2048]{1,0:T(8,128)(2,1)S(1)} collective-permute-done((bf16[128,2048]{1,0:T(8,128)(2,1)S(1)}, bf16[128,2048]{1,0:T(8,128)(2,1)S(1)}, u32[]{:S(2)}, u32[]{:S(2)}) %collective-permute-start.4) | collective-permute-done | bytes 524320 | tf_op jit(solution)/shard_map/ppermute | solution.py:219
  55.3 18.4 %collective-permute-done.14.refs_4_.refs_24_ = bf16[256,2048]{1,0:T(8,128)(2,1)} collective-permute-done((bf16[256,2048]{1,0:T(8,128)(2,1)}, bf16[256,2048]{1,0:T(8,128)(2,1)}, u32[]{:S(2)}, u32[]{:S(2)}) %collective-permute-start.14) | collective-permute-done | bytes 1048608 | tf_op jit(solution)/shard_map/ppermute | solution.py:219
  85.6 11.4 %shard_map.263 = (bf16[1024,2048]{1,0:T(8,128)(2,1)}, bf16[1024,2048]{1,0:T(8,128)(2,1)}, bf16[1024,2048]{1,0:T(8,128)(2,1)}, f32[1,2048]{1,0:T(1,128)}) custom-call(s32[9]{0:T(128)} %concatenate.52.info.refs_0_, bf16[1024,2048]{1,0:T(8,128)(2,1)} %bitcast.49, bf16[1024,2048]{1,0:T(8,128)(2,1)} %bitcast.59, f32[1,2048]{1,0:T(1,128)} %bitcast.73, ...), custom_call_target="tpu_custom_call" | custom-call | bytes 20971520 | tf_op jit(solution)/shard_map/pallas_call | solution.py:239
  103.3 13.5 %shard_map.264 = (bf16[1024,512]{1,0:T(8,128)(2,1)}, bf16[512,1024]{1,0:T(8,128)(2,1)}, bf16[512,1024]{1,0:T(8,128)(2,1)}) custom-call(s32[9]{0:T(128)} %concatenate.52.info.refs_0_, bf16[1024,2048]{1,0:T(8,128)(2,1)} %get-tuple-element.60.x.refs_1_, f32[1,1536]{1,0:T(1,128)} %bitcast.82, f32[256,128]{1,0:T(8,128)} %get-tuple-element.147.cos.refs_3_.refs_7_, ...), custom_call_target="tpu_custom_call" | custom-call | flops 6442450944 | bytes 13631488 | tf_op jit(solution)/shard_map/pallas_call | solution.py:239
  118.9 9.3 %collective-permute-done.22.refs_12_.refs_4_ = bf16[256,2048]{1,0:T(8,128)(2,1)S(1)} collective-permute-done((bf16[256,2048]{1,0:T(8,128)(2,1)S(1)}, bf16[256,2048]{1,0:T(8,128)(2,1)S(1)}, u32[]{:S(2)}, u32[]{:S(2)}) %collective-permute-start.22) | collective-permute-done | bytes 1048608 | tf_op jit(solution)/shard_map/ppermute | solution.py:219
  129.7 6.3 %shard_map.265.refs_2_ = bf16[1024,512]{1,0:T(8,128)(2,1)} custom-call(s32[9]{0:T(128)} %concatenate.52.info.refs_0_, bf16[1024,2048]{1,0:T(8,128)(2,1)} %get-tuple-element.62.g.refs_1_, bf16[256,2048]{1,0:T(8,128)(2,1)} %copy-done.2, bf16[256,2048]{1,0:T(8,128)(2,1)} %copy-done.4, bf16[256,2048]{1,0:T(8,128)(2,1)} %collective-permute-done.1.refs_2_.refs_14_, ...), custom_call_target="tpu_custom_call" | custom-call | flops 2147483648 | bytes 7340032 | tf_op jit(solution)/shard_map/pallas_call | solution.py:239
  136.1 14.7 %collective-permute-done.9.refs_8_.refs_12_ = bf16[512,1024]{1,0:T(8,128)(2,1)} collective-permute-done((bf16[512,1024]{1,0:T(8,128)(2,1)}, bf16[512,1024]{1,0:T(8,128)(2,1)}, u32[]{:S(2)}, u32[]{:S(2)}) %collective-permute-start.9) | collective-permute-done | bytes 1048608 | tf_op jit(solution)/shard_map/ppermute | solution.py:219
  150.8 22.0 %collective-permute-done.28.refs_8_.refs_12_ = bf16[512,1024]{1,0:T(8,128)(2,1)} collective-permute-done((bf16[512,1024]{1,0:T(8,128)(2,1)}, bf16[512,1024]{1,0:T(8,128)(2,1)}, u32[]{:S(2)}, u32[]{:S(2)}) %collective-permute-start.28) | collective-permute-done | bytes 1048608 | tf_op jit(solution)/shard_map/ppermute | solution.py:219
  174.3 23.6 %shard_map.267 = (bf16[1024,2048]{1,0:T(8,128)(2,1)}, bf16[1024,2048]{1,0:T(8,128)(2,1)}) custom-call(s32[9]{0:T(128)} %concatenate.52.info.refs_0_, bf16[1024,2048]{1,0:T(8,128)(2,1)} %get-tuple-element.65.x.refs_1_, f32[1,2048]{1,0:T(1,128)} %bitcast.83, bf16[256,2048]{1,0:T(8,128)(2,1)} %refs_20_.1, ...), custom_call_target="tpu_custom_call" | custom-call | flops 8589934592 | bytes 20971520 | tf_op jit(solution)/shard_map/pallas_call | solution.py:239
  199.6 9.2 %shard_map.282 = bf16[1024,2048]{1,0:T(8,128)(2,1)} custom-call(s32[9]{0:T(128)} %concatenate.52.info.refs_0_, bf16[1024,2048]{1,0:T(8,128)(2,1)} %get-tuple-element.62.g.refs_1_, bf16[1024,2048]{1,0:T(8,128)(2,1)} %get-tuple-element.67.act.refs_2_), custom_call_target="tpu_custom_call" | custom-call | flops 4294967296 | bytes 12582912 | tf_op jit(solution)/shard_map/pallas_call | solution.py:239
  215.3 10.0 %shard_map.266 = (bf16[512,512]{1,0:T(8,128)(2,1)}, bf16[512,512]{1,0:T(8,128)(2,1)}, f32[2,2,1,256]{3,2,1,0:T(1,128)}, bf16[512,1024]{1,0:T(8,128)(2,1)}, bf16[...) custom-call(s32[9]{0:T(128)} %concatenate.52.info.refs_0_, ...), custom_call_target="tpu_custom_call" | custom-call | flops 3221225472 | bytes 12582912 | tf_op jit(solution)/shard_map/pallas_call | solution.py:239
  225.5 10.0 %shard_map.269 = (bf16[512,512]{1,0:T(8,128)(2,1)}, bf16[512,512]{1,0:T(8,128)(2,1)}, f32[2,2,1,256]{3,2,1,0:T(1,128)}, bf16[512,1024]{1,0:T(8,128)(2,1)}, bf16[...) custom-call(s32[9]{0:T(128)} %concatenate.52.info.refs_0_, ...), custom_call_target="tpu_custom_call" | custom-call | flops 3221225472 | bytes 12582912 | tf_op jit(solution)/shard_map/pallas_call | solution.py:239
  239.0 4.8 shard_map.278
  244.8 11.4 %shard_map.270 = bf16[512,2048]{1,0:T(8,128)(2,1)} custom-call(s32[9]{0:T(128)} %concatenate.52.info.refs_0_, bf16[512,512]{1,0:T(8,128)(2,1)} %get-tuple-element.70.att, bf16[1024,2048]{1,0:T(8,128)(2,1)} %get-tuple-element.67.act.refs_2_, bf16[256,2048]{1,0:T(8,128)(2,1)} %copy-done.2, bf16[256,2048]{1,0:T(8,128)(2,1)} %copy-done.4, ...), custom_call_target="tpu_custom_call" | custom-call | flops 5368709120 | bytes 15204352 | tf_op jit(solution)/shard_map/pallas_call | solution.py:239
  256.3 11.6 %shard_map.268 = bf16[512,2048]{1,0:T(8,128)(2,1)} custom-call(s32[9]{0:T(128)} %concatenate.52.info.refs_0_, bf16[512,512]{1,0:T(8,128)(2,1)} %get-tuple-element.64.att, bf16[1024,2048]{1,0:T(8,128)(2,1)} %get-tuple-element.67.act.refs_2_, bf16[256,2048]{1,0:T(8,128)(2,1)} %copy-done.2, bf16[256,2048]{1,0:T(8,128)(2,1)} %copy-done.4, ...), custom_call_target="tpu_custom_call" | custom-call | flops 5368709120 | bytes 15204352 | tf_op jit(solution)/shard_map/pallas_call | solution.py:239
  272.1 16.1 %shard_map.271 = (bf16[1024,2048]{1,0:T(8,128)(2,1)}, f32[1,2048]{1,0:T(1,128)}) custom-call(s32[9]{0:T(128)} %concatenate.52.info.refs_0_, bf16[1024,2048]{1,0:T(8,128)(2,1)} %get-tuple-element.62.g.refs_1_, bf16[1024,2048]{1,0:T(8,128)(2,1)} %get-tuple-element.76.slope, bf16[256,2048]{1,0:T(8,128)(2,1)} %bitcast.57, bf16[256,2048]{1,0:T(8,128)(2,1)} %copy-done.11, ...), custom_call_target="tpu_custom_call" | custom-call | flops 8589934592 | bytes 20971520 | tf_op jit(solution)/shard_map/pallas_call | solution.py:239
  291.4 5.0 shard_map.279
  301.0 9.3 %shard_map.280 = bf16[1024,2048]{1,0:T(8,128)(2,1)} custom-call(s32[9]{0:T(128)} %concatenate.52.info.refs_0_, bf16[1024,2048]{1,0:T(8,128)(2,1)} %get-tuple-element.65.x.refs_1_, bf16[1024,2048]{1,0:T(8,128)(2,1)} %get-tuple-element.77.refs_5_.refs_2_), custom_call_target="tpu_custom_call" | custom-call | flops 4294967296 | bytes 12582912 | tf_op jit(solution)/shard_map/pallas_call | solution.py:239
  318.1 20.8 %shard_map.273 = (bf16[512,2048]{1,0:T(8,128)(2,1)}, bf16[512,1536]{1,0:T(8,128)(2,1)}, f32[2,1,1024]{2,1,0:T(1,128)}, f32[8,2048]{1,0:T(8,128)}) custom-call(s32[9]{0:T(128)} %concatenate.52.info.refs_0_, bf16[512,512]{1,0:T(8,128)(2,1)} %get-tuple-element.79.refs_1_, bf16[512,1024]{1,0:T(8,128)(2,1)} %get-tuple-element.80.refs_2_, ...), custom_call_target="tpu_custom_call" | custom-call | flops 7516192768 | bytes 23068672 | tf_op jit(solution)/shard_map/pallas_call | solution.py:239
  340.5 21.0 %shard_map.272 = (bf16[512,2048]{1,0:T(8,128)(2,1)}, bf16[512,1536]{1,0:T(8,128)(2,1)}, f32[2,1,1024]{2,1,0:T(1,128)}, f32[8,2048]{1,0:T(8,128)}) custom-call(s32[9]{0:T(128)} %concatenate.52.info.refs_0_, bf16[512,512]{1,0:T(8,128)(2,1)} %get-tuple-element.71.refs_1_, bf16[512,1024]{1,0:T(8,128)(2,1)} %get-tuple-element.72.refs_2_, ...), custom_call_target="tpu_custom_call" | custom-call | flops 7516192768 | bytes 23068672 | tf_op jit(solution)/shard_map/pallas_call | solution.py:239
  368.0 6.3 %shard_map.274 = bf16[1024,1024]{1,0:T(8,128)(2,1)} custom-call(s32[9]{0:T(128)} %concatenate.52.info.refs_0_, bf16[1024,2048]{1,0:T(8,128)(2,1)} %get-tuple-element.60.x.refs_1_, bf16[1024,1536]{1,0:T(8,128)(2,1)} %copy-done.1), custom_call_target="tpu_custom_call" | custom-call | flops 2147483648 | bytes 8388608 | tf_op jit(solution)/shard_map/pallas_call | solution.py:239
  399.2 4.9 shard_map.277
  405.5 9.6 %shard_map.283 = (bf16[512,2048]{1,0:T(8,128)(2,1)}, bf16[512,2048]{1,0:T(8,128)(2,1)}) custom-call(s32[9]{0:T(128)} %concatenate.52.info.refs_0_, bf16[1024,2048]{1,0:T(8,128)(2,1)} %get-tuple-element.62.g.refs_1_, bf16[1024,2048]{1,0:T(8,128)(2,1)} %get-tuple-element.67.act.refs_2_, bf16[1024,2048]{1,0:T(8,128)(2,1)} %collective-permute-done.53.refs_3_), custom_call_target="tpu_custom_call" | custom-call | flops 4294967296 | bytes 12582912 | tf_op jit(solution)/shard_map/pallas_call | solution.py:239
  417.2 6.5 %shard_map.275 = (bf16[512,1024]{1,0:T(8,128)(2,1)}, bf16[512,1024]{1,0:T(8,128)(2,1)}) custom-call(s32[9]{0:T(128)} %concatenate.52.info.refs_0_, bf16[1024,2048]{1,0:T(8,128)(2,1)} %get-tuple-element.60.x.refs_1_, bf16[1024,1536]{1,0:T(8,128)(2,1)} %copy-done.1, bf16[1024,1024]{1,0:T(8,128)(2,1)} %copy-done.14), custom_call_target="tpu_custom_call" | custom-call | flops 2147483648 | bytes 8388608 | tf_op jit(solution)/shard_map/pallas_call | solution.py:239
  426.7 9.5 %shard_map.281 = (bf16[512,2048]{1,0:T(8,128)(2,1)}, bf16[512,2048]{1,0:T(8,128)(2,1)}) custom-call(s32[9]{0:T(128)} %concatenate.52.info.refs_0_, bf16[1024,2048]{1,0:T(8,128)(2,1)} %get-tuple-element.65.x.refs_1_, bf16[1024,2048]{1,0:T(8,128)(2,1)} %get-tuple-element.77.refs_5_.refs_2_, bf16[1024,2048]{1,0:T(8,128)(2,1)} %collective-permute-done.50.refs_3_), custom_call_target="tpu_custom_call" | custom-call | flops 4294967296 | bytes 12582912 | tf_op jit(solution)/shard_map/pallas_call | solution.py:239
  438.4 17.3 %collective-permute-done.46 = bf16[256,512]{1,0:T(8,128)(2,1)S(1)} collective-permute-done((bf16[256,512]{1,0:T(8,128)(2,1)}, bf16[256,512]{1,0:T(8,128)(2,1)S(1)}, u32[]{:S(2)}, u32[]{:S(2)}) %collective-permute-start.46) | collective-permute-done | bytes 262176 | tf_op jit(solution)/shard_map/ppermute | solution.py:219
  459.1 6.7 %add_convert_fusion = bf16[1024,2048]{1,0:T(8,128)(2,1)} fusion(bf16[1024,2048]{1,0:T(8,128)(2,1)} %all-reduce.4.cloned.1.call-done, f32[2048]{0:T(1024)S(1)} %copy-done.29, f32[2048]{0:T(1024)S(1)} %copy-done.30, bf16[4,256,2048]{2,1,0:T(8,128)(2,1)S(1)} %copy-done), kind=kLoop, calls=%fused_computation.1 | loop fusion | flops 12582912 | bytes 12599296 | tf_op jit(solution)/shard_map/convert_element_type | solution.py:744
  470.9 29.7 %collective-permute-done.51 = bf16[512,2048]{1,0:T(8,128)(2,1)S(1)} collective-permute-done((bf16[512,2048]{1,0:T(8,128)(2,1)}, bf16[512,2048]{1,0:T(8,128)(2,1)S(1)}, u32[]{:S(2)}, u32[]{:S(2)}) %collective-permute-start.51) | collective-permute-done | bytes 2097184 | tf_op jit(solution)/shard_map/ppermute | solution.py:219
  507.6 14.0 %collective-permute-done.55 = bf16[256,2048]{1,0:T(8,128)(2,1)} collective-permute-done((bf16[256,2048]{1,0:T(8,128)(2,1)}, bf16[256,2048]{1,0:T(8,128)(2,1)}, u32[]{:S(2)}, u32[]{:S(2)}) %collective-permute-start.55) | collective-permute-done | bytes 1048608 | tf_op jit(solution)/shard_map/ppermute | solution.py:219
  529.3 65.2 %all-reduce.6.cloned.1.call-done = bf16[1024,2048]{1,0:T(8,128)(2,1)} async-done(((bf16[1024,2048]{1,0:T(8,128)(2,1)}), bf16[1024,2048]{1,0:T(8,128)(2,1)}) %all-reduce.6.cloned.1.call-update) | async-done | bytes 4194320 | tf_op jit(solution)/shard_map/psum | solution.py:729
  594.5 8.8 %convert_add_fusion = f32[1024,2048]{1,0:T(8,128)} fusion(bf16[1024,2048]{1,0:T(8,128)(2,1)} %all-reduce.6.cloned.1.call-done, bf16[1024,2048]{1,0:T(8,128)(2,1)} %get-tuple-element.62.g.refs_1_), kind=kLoop, calls=%fused_computation | loop fusion | flops 6291456 | bytes 16777216 | tf_op jit(solution)/shard_map/add | solution.py:745
  (258 shorter events, 137.1 us)
Async XLA Ops:
  7.2 431.1 %all-reduce.4.cloned.1.call-start = ((), (), s32[]{:S(2)}) async-start(), calls=%async_computation | async-start | bytes 8388608 | tf_op jit(solution)/shard_map/psum | solution.py:680
  54.6 47.5 %collective-permute-start.6 = (bf16[256,2048]{1,0:T(8,128)(2,1)S(1)}, bf16[256,2048]{1,0:T(8,128)(2,1)}, u32[]{:S(2)}, u32[]{:S(2)}) collective-permute-start(bf16[256,2048]{1,0:T(8,128)(2,1)S(1)} %collective-permute-done.3.refs_4_.refs_16_), channel_id=1, source_target_pairs={{0,8},{8,0},{16,24},{24,16},{1,9},{9,1},{17,25},{25,17},{2,10},{10... | collective-permute-start | bytes 3145736 | tf_op jit(solution)/shard_map/ppermute | solution.py:219
  55.2 47.0 %collective-permute-start.2 = (bf16[256,2048]{1,0:T(8,128)(2,1)S(1)}, bf16[256,2048]{1,0:T(8,128)(2,1)}, u32[]{:S(2)}, u32[]{:S(2)}) collective-permute-start(bf16[256,2048]{1,0:T(8,128)(2,1)S(1)} %collective-permute-done.refs_1_.refs_13_), channel_id=1, source_target_pairs={{0,8},{8,0},{16,24},{24,16},{1,9},{9,1},{17,25},{25,17},{2,10},{10... | collective-permute-start | bytes 3145736 | tf_op jit(solution)/shard_map/ppermute | solution.py:219
  73.6 29.6 %collective-permute-start.7 = (bf16[256,2048]{1,0:T(8,128)(2,1)}, bf16[256,2048]{1,0:T(8,128)(2,1)}, u32[]{:S(2)}, u32[]{:S(2)}) collective-permute-start(bf16[256,2048]{1,0:T(8,128)(2,1)} %copy-done.5), channel_id=1, source_target_pairs={{0,8},{8,0},{16,24},{24,16},{1,9},{9,1},{17,25},{25,17},{2,10},{10... | collective-permute-start | bytes 3145736 | tf_op jit(solution)/shard_map/ppermute | solution.py:219
  102.2 33.9 %collective-permute-start.13 = (bf16[256,2048]{1,0:T(8,128)(2,1)}, bf16[256,2048]{1,0:T(8,128)(2,1)}, u32[]{:S(2)}, u32[]{:S(2)}) collective-permute-start(bf16[256,2048]{1,0:T(8,128)(2,1)} %collective-permute-done.11.refs_1_.refs_21_), channel_id=1, source_target_pairs={{0,8},{8,0},{16,24},{24,16},{1,9},{9,1},{17,25},{25,17},{2,10},{10... | collective-permute-start | bytes 3145736 | tf_op jit(solution)/shard_map/ppermute | solution.py:219
  116.8 34.0 %collective-permute-start.9 = (bf16[512,1024]{1,0:T(8,128)(2,1)}, bf16[512,1024]{1,0:T(8,128)(2,1)}, u32[]{:S(2)}, u32[]{:S(2)}) collective-permute-start(bf16[512,1024]{1,0:T(8,128)(2,1)} %get-tuple-element.63.refs_6_.refs_10_), channel_id=1, source_target_pairs={{0,16},{8,24},{16,0},{24,8},{1,17},{9,25},{17,1},{25,9},{2,18},{10... | collective-permute-start | bytes 3145736 | tf_op jit(solution)/shard_map/ppermute | solution.py:219
  117.8 55.0 %collective-permute-start.28 = (bf16[512,1024]{1,0:T(8,128)(2,1)}, bf16[512,1024]{1,0:T(8,128)(2,1)}, u32[]{:S(2)}, u32[]{:S(2)}) collective-permute-start(bf16[512,1024]{1,0:T(8,128)(2,1)} %get-tuple-element.69.refs_6_.refs_10_), channel_id=1, source_target_pairs={{0,16},{8,24},{16,0},{24,8},{1,17},{9,25},{17,1},{25,9},{2,18},{10... | collective-permute-start | bytes 3145736 | tf_op jit(solution)/shard_map/ppermute | solution.py:219
  118.9 53.9 %collective-permute-start.18 = (bf16[256,2048]{1,0:T(8,128)(2,1)}, bf16[256,2048]{1,0:T(8,128)(2,1)}, u32[]{:S(2)}, u32[]{:S(2)}) collective-permute-start(bf16[256,2048]{1,0:T(8,128)(2,1)} %constant_dynamic-update-slice_fusion.2.refs_5_.refs_25_), channel_id=1, source_target_pairs={{0,8},{8,0},{16,24},{24,16},{1,9},{9,1},{17,25},{25,17},{2,10},{10... | collective-permute-start | bytes 3145736 | tf_op jit(solution)/shard_map/ppermute | solution.py:219
  128.2 69.7 %collective-permute-start.19 = (bf16[256,2048]{1,0:T(8,128)(2,1)S(1)}, bf16[256,2048]{1,0:T(8,128)(2,1)S(1)}, u32[]{:S(2)}, u32[]{:S(2)}) collective-permute-start(bf16[256,2048]{1,0:T(8,128)(2,1)S(1)} %bitcast.53), channel_id=1, source_target_pairs={{0,4},{4,0},{1,5},{5,1},{2,6},{6,2},{3,7},{7,3},{8,12},{12,8},{9,1... | collective-permute-start | bytes 3145736 | tf_op jit(solution)/shard_map/ppermute | solution.py:219
  136.0 78.2 %collective-permute-start.8 = (bf16[512,1024]{1,0:T(8,128)(2,1)}, bf16[512,1024]{1,0:T(8,128)(2,1)}, u32[]{:S(2)}, u32[]{:S(2)}) collective-permute-start(bf16[512,1024]{1,0:T(8,128)(2,1)} %get-tuple-element.63.refs_6_.refs_10_), channel_id=1, source_target_pairs={{0,8},{8,0},{16,24},{24,16},{1,9},{9,1},{17,25},{25,17},{2,10},{10... | collective-permute-start | bytes 3145736 | tf_op jit(solution)/shard_map/ppermute | solution.py:219
  150.8 64.0 %collective-permute-start.27 = (bf16[512,1024]{1,0:T(8,128)(2,1)}, bf16[512,1024]{1,0:T(8,128)(2,1)}, u32[]{:S(2)}, u32[]{:S(2)}) collective-permute-start(bf16[512,1024]{1,0:T(8,128)(2,1)} %get-tuple-element.69.refs_6_.refs_10_), channel_id=1, source_target_pairs={{0,8},{8,0},{16,24},{24,16},{1,9},{9,1},{17,25},{25,17},{2,10},{10... | collective-permute-start | bytes 3145736 | tf_op jit(solution)/shard_map/ppermute | solution.py:219
  172.8 42.1 %collective-permute-start.10 = (bf16[512,1024]{1,0:T(8,128)(2,1)}, bf16[512,1024]{1,0:T(8,128)(2,1)}, u32[]{:S(2)}, u32[]{:S(2)}) collective-permute-start(bf16[512,1024]{1,0:T(8,128)(2,1)} %collective-permute-done.9.refs_8_.refs_12_), channel_id=1, source_target_pairs={{0,8},{8,0},{16,24},{24,16},{1,9},{9,1},{17,25},{25,17},{2,10},{10... | collective-permute-start | bytes 3145736 | tf_op jit(solution)/shard_map/ppermute | solution.py:219
  213.4 30.4 %collective-permute-start.20 = (bf16[256,2048]{1,0:T(8,128)(2,1)S(1)}, bf16[256,2048]{1,0:T(8,128)(2,1)}, u32[]{:S(2)}, u32[]{:S(2)}) collective-permute-start(bf16[256,2048]{1,0:T(8,128)(2,1)S(1)} %bitcast.54), channel_id=1, source_target_pairs={{0,8},{8,0},{16,24},{24,16},{1,9},{9,1},{17,25},{25,17},{2,10},{10... | collective-permute-start | bytes 3145736 | tf_op jit(solution)/shard_map/ppermute | solution.py:219
  214.3 30.0 %collective-permute-start.25 = (bf16[256,2048]{1,0:T(8,128)(2,1)S(1)}, bf16[256,2048]{1,0:T(8,128)(2,1)}, u32[]{:S(2)}, u32[]{:S(2)}) collective-permute-start(bf16[256,2048]{1,0:T(8,128)(2,1)S(1)} %collective-permute-done.22.refs_12_.refs_4_), channel_id=1, source_target_pairs={{0,8},{8,0},{16,24},{24,16},{1,9},{9,1},{17,25},{25,17},{2,10},{10... | collective-permute-start | bytes 3145736 | tf_op jit(solution)/shard_map/ppermute | solution.py:219
  214.8 29.5 %collective-permute-start.21 = (bf16[256,2048]{1,0:T(8,128)(2,1)S(1)}, bf16[256,2048]{1,0:T(8,128)(2,1)}, u32[]{:S(2)}, u32[]{:S(2)}) collective-permute-start(bf16[256,2048]{1,0:T(8,128)(2,1)S(1)} %collective-permute-done.19.refs_9_.refs_1_), channel_id=1, source_target_pairs={{0,8},{8,0},{16,24},{24,16},{1,9},{9,1},{17,25},{25,17},{2,10},{10... | collective-permute-start | bytes 3145736 | tf_op jit(solution)/shard_map/ppermute | solution.py:219
  214.9 29.9 %collective-permute-start.26 = (bf16[256,2048]{1,0:T(8,128)(2,1)}, bf16[256,2048]{1,0:T(8,128)(2,1)}, u32[]{:S(2)}, u32[]{:S(2)}) collective-permute-start(bf16[256,2048]{1,0:T(8,128)(2,1)} %constant_dynamic-update-slice_fusion.4.refs_13_.refs_5_), channel_id=1, source_target_pairs={{0,8},{8,0},{16,24},{24,16},{1,9},{9,1},{17,25},{25,17},{2,10},{10... | collective-permute-start | bytes 3145736 | tf_op jit(solution)/shard_map/ppermute | solution.py:219
  225.3 113.5 %collective-permute-start.30 = (bf16[512,1024]{1,0:T(8,128)(2,1)}, bf16[512,1024]{1,0:T(8,128)(2,1)}, u32[]{:S(2)}, u32[]{:S(2)}) collective-permute-start(bf16[512,1024]{1,0:T(8,128)(2,1)} %get-tuple-element.73), channel_id=1, source_target_pairs={{0,8},{8,0},{16,24},{24,16},{1,9},{9,1},{17,25},{25,17},{2,10},{10... | collective-permute-start | bytes 3145736 | tf_op jit(solution)/shard_map/ppermute | solution.py:219
  243.8 53.7 %collective-permute-start.31 = (bf16[512,1024]{1,0:T(8,128)(2,1)}, bf16[512,1024]{1,0:T(8,128)(2,1)}, u32[]{:S(2)}, u32[]{:S(2)}) collective-permute-start(bf16[512,1024]{1,0:T(8,128)(2,1)} %get-tuple-element.75), channel_id=1, source_target_pairs={{0,8},{8,0},{16,24},{24,16},{1,9},{9,1},{17,25},{25,17},{2,10},{10... | collective-permute-start | bytes 3145736 | tf_op jit(solution)/shard_map/ppermute | solution.py:219
  244.2 47.2 %collective-permute-start.47 = (bf16[1024,512]{1,0:T(8,128)(2,1)}, bf16[1024,512]{1,0:T(8,128)(2,1)}, u32[]{:S(2)}, u32[]{:S(2)}) collective-permute-start(bf16[1024,512]{1,0:T(8,128)(2,1)} %shard_map.278), channel_id=1, source_target_pairs={{0,8},{8,0},{16,24},{24,16},{1,9},{9,1},{17,25},{25,17},{2,10},{10... | collective-permute-start | bytes 3145736 | tf_op jit(solution)/shard_map/ppermute | solution.py:219
  244.3 68.5 %collective-permute-start.33 = (bf16[512,1024]{1,0:T(8,128)(2,1)}, bf16[512,1024]{1,0:T(8,128)(2,1)S(1)}, u32[]{:S(2)}, u32[]{:S(2)}) collective-permute-start(bf16[512,1024]{1,0:T(8,128)(2,1)} %get-tuple-element.81), channel_id=1, source_target_pairs={{0,8},{8,0},{16,24},{24,16},{1,9},{9,1},{17,25},{25,17},{2,10},{10... | collective-permute-start | bytes 3145736 | tf_op jit(solution)/shard_map/ppermute | solution.py:219
  244.8 43.5 %collective-permute-start.34 = (bf16[512,1024]{1,0:T(8,128)(2,1)}, bf16[512,1024]{1,0:T(8,128)(2,1)}, u32[]{:S(2)}, u32[]{:S(2)}) collective-permute-start(bf16[512,1024]{1,0:T(8,128)(2,1)} %get-tuple-element.83), channel_id=1, source_target_pairs={{0,8},{8,0},{16,24},{24,16},{1,9},{9,1},{17,25},{25,17},{2,10},{10... | collective-permute-start | bytes 3145736 | tf_op jit(solution)/shard_map/ppermute | solution.py:219
  272.1 322.5 %all-reduce.6.cloned.1.call-start = ((), (), s32[]{:S(2)}) async-start(), calls=%async_computation.1 | async-start | bytes 8388608 | tf_op jit(solution)/shard_map/psum | solution.py:729
  300.1 39.5 %collective-permute-start.32 = (bf16[512,1024]{1,0:T(8,128)(2,1)}, bf16[512,1024]{1,0:T(8,128)(2,1)S(1)}, u32[]{:S(2)}, u32[]{:S(2)}) collective-permute-start(bf16[512,1024]{1,0:T(8,128)(2,1)} %add_convert_fusion.2), channel_id=1, source_target_pairs={{0,16},{8,24},{16,0},{24,8},{1,17},{9,25},{17,1},{25,9},{2,18},{10... | collective-permute-start | bytes 3145736 | tf_op jit(solution)/shard_map/ppermute | solution.py:219
  310.6 94.8 %collective-permute-start.53 = (bf16[1024,2048]{1,0:T(8,128)(2,1)}, bf16[1024,2048]{1,0:T(8,128)(2,1)}, u32[]{:S(2)}, u32[]{:S(2)}) collective-permute-start(bf16[1024,2048]{1,0:T(8,128)(2,1)} %shard_map.282), channel_id=1, source_target_pairs={{0,8},{8,0},{16,24},{24,16},{1,9},{9,1},{17,25},{25,17},{2,10},{10... | collective-permute-start | bytes 12582920 | tf_op jit(solution)/shard_map/ppermute | solution.py:219
  312.9 113.8 %collective-permute-start.50 = (bf16[1024,2048]{1,0:T(8,128)(2,1)}, bf16[1024,2048]{1,0:T(8,128)(2,1)}, u32[]{:S(2)}, u32[]{:S(2)}) collective-permute-start(bf16[1024,2048]{1,0:T(8,128)(2,1)} %shard_map.280), channel_id=1, source_target_pairs={{0,8},{8,0},{16,24},{24,16},{1,9},{9,1},{17,25},{25,17},{2,10},{10... | collective-permute-start | bytes 12582920 | tf_op jit(solution)/shard_map/ppermute | solution.py:219
  317.1 63.1 %collective-permute-start.49 = (bf16[256,512]{1,0:T(8,128)(2,1)S(1)}, bf16[256,512]{1,0:T(8,128)(2,1)S(1)}, u32[]{:S(2)}, u32[]{:S(2)}) collective-permute-start(bf16[256,512]{1,0:T(8,128)(2,1)S(1)} %slice.176), channel_id=1, source_target_pairs={{0,16},{8,24},{16,0},{24,8},{1,17},{9,25},{17,1},{25,9},{2,18},{10... | collective-permute-start | bytes 786440 | tf_op jit(solution)/shard_map/ppermute | solution.py:219
  374.2 41.6 %collective-permute-start.41 = (bf16[1024,1024]{1,0:T(8,128)(2,1)}, bf16[1024,1024]{1,0:T(8,128)(2,1)S(1)}, u32[]{:S(2)}, u32[]{:S(2)}) collective-permute-start(bf16[1024,1024]{1,0:T(8,128)(2,1)} %shard_map.274), channel_id=1, source_target_pairs={{0,8},{8,0},{16,24},{24,16},{1,9},{9,1},{17,25},{25,17},{2,10},{10... | collective-permute-start | bytes 6291464 | tf_op jit(solution)/shard_map/ppermute | solution.py:219
  415.1 50.8 %collective-permute-start.54 = (bf16[512,2048]{1,0:T(8,128)(2,1)}, bf16[512,2048]{1,0:T(8,128)(2,1)}, u32[]{:S(2)}, u32[]{:S(2)}) collective-permute-start(bf16[512,2048]{1,0:T(8,128)(2,1)} %get-tuple-element.105), channel_id=1, source_target_pairs={{0,4},{4,0},{1,5},{5,1},{2,6},{6,2},{3,7},{7,3},{8,12},{12,8},{9,1... | collective-permute-start | bytes 6291464 | tf_op jit(solution)/shard_map/ppermute | solution.py:219
  423.7 32.0 %collective-permute-start.42 = (bf16[512,1024]{1,0:T(8,128)(2,1)}, bf16[512,1024]{1,0:T(8,128)(2,1)}, u32[]{:S(2)}, u32[]{:S(2)}) collective-permute-start(bf16[512,1024]{1,0:T(8,128)(2,1)} %get-tuple-element.97), channel_id=1, source_target_pairs={{0,16},{8,24},{16,0},{24,8},{1,17},{9,25},{17,1},{25,9},{2,18},{10... | collective-permute-start | bytes 3145736 | tf_op jit(solution)/shard_map/ppermute | solution.py:219
  436.2 64.4 %collective-permute-start.51 = (bf16[512,2048]{1,0:T(8,128)(2,1)}, bf16[512,2048]{1,0:T(8,128)(2,1)S(1)}, u32[]{:S(2)}, u32[]{:S(2)}) collective-permute-start(bf16[512,2048]{1,0:T(8,128)(2,1)} %get-tuple-element.103), channel_id=1, source_target_pairs={{0,16},{8,24},{16,0},{24,8},{1,17},{9,25},{17,1},{25,9},{2,18},{10... | collective-permute-start | bytes 6291464 | tf_op jit(solution)/shard_map/ppermute | solution.py:219
  457.8 47.3 %collective-permute-start.43 = (bf16[256,1024]{1,0:T(8,128)(2,1)S(1)}, bf16[256,1024]{1,0:T(8,128)(2,1)S(1)}, u32[]{:S(2)}, u32[]{:S(2)}) collective-permute-start(bf16[256,1024]{1,0:T(8,128)(2,1)S(1)} %slice.175), channel_id=1, source_target_pairs={{0,4},{4,0},{1,5},{5,1},{2,6},{6,2},{3,7},{7,3},{8,12},{12,8},{9,1... | collective-permute-start | bytes 1572872 | tf_op jit(solution)/shard_map/ppermute | solution.py:219
  469.4 52.1 %collective-permute-start.55 = (bf16[256,2048]{1,0:T(8,128)(2,1)}, bf16[256,2048]{1,0:T(8,128)(2,1)}, u32[]{:S(2)}, u32[]{:S(2)}) collective-permute-start(bf16[256,2048]{1,0:T(8,128)(2,1)} %slice.173), channel_id=1, source_target_pairs={{0,16},{8,24},{16,0},{24,8},{1,17},{9,25},{17,1},{25,9},{2,18},{10... | collective-permute-start | bytes 3145736 | tf_op jit(solution)/shard_map/ppermute | solution.py:219
  (62 other events, 1533.8 us)
Sparse Core Ops, SparseCore 0:
  272.2 156.1 all-reduce.3
  438.5 156.0 all-reduce.5

commit v3 on v1

--- a/solution.py
+++ b/solution.py
@@ -1,6 +1,8 @@
 import jax
 import jax.numpy as jnp
 from jax import lax
+from jax.experimental import pallas as pl
+from jax.experimental.pallas import tpu as pltpu
 from jax.sharding import PartitionSpec as P
 
 D = 2048
@@ -38,7 +40,7 @@
     return z * phi_cdf, phi_cdf + z * density
 
 
-def per_device(
+def per_device_any(
     tokens,
     cotangent,
     lengths,
@@ -212,6 +214,771 @@
     )
 
 
+def exchange(array, axis, flip):
+    size = lax.axis_size(axis)
+    return lax.ppermute(array, axis, [(i, i ^ flip) for i in range(size)])
+
+
+def after(array, *others):
+    return lax.optimization_barrier((array, *others))[0]
+
+
+def along_x(array):
+    return exchange(array, "seq", 2)
+
+
+def along_y(array):
+    return exchange(array, "batch", 1)
+
+
+def to_core(array):
+    return exchange(array, "seq", 1)
+
+
+ORDER = (0, 2, 4, 6, 1, 3, 5, 7)
+
+
+def block_ins(blocks, width, column):
+    return [(pl.BlockSpec((256, width), lambda j: (0, column(j))), b) for b in blocks]
+
+
+def both_cores(own, by_x, by_y, far, *others):
+    own_c, by_x_c, by_y_c, far_c = others
+    return (own, by_y, own_c, by_y_c, by_x, far, by_x_c, far_c)
+
+
+def call(body, grid, ins, outs, scratch=(), flops=0, moved=0, vmem=60, aliases={}):
+    return pl.pallas_call(
+        body,
+        grid=grid,
+        in_specs=[spec for spec, _ in ins],
+        out_specs=[spec for spec, _ in outs],
+        out_shape=[shape for _, shape in outs],
+        scratch_shapes=list(scratch),
+        input_output_aliases=aliases,
+        compiler_params=pltpu.CompilerParams(vmem_limit_bytes=vmem * 1024 * 1024),
+        cost_estimate=pl.CostEstimate(flops=flops, bytes_accessed=moved, transcendentals=0),
+    )(*[array for _, array in ins])
+
+
+def call_placed(body, grid, info, ins, outs, scratch=(), flops=0, moved=0, vmem=60):
+    return pl.pallas_call(
+        body,
+        grid_spec=pltpu.PrefetchScalarGridSpec(
+            num_scalar_prefetch=1,
+            grid=grid,
+            in_specs=[spec for spec, _ in ins],
+            out_specs=[spec for spec, _ in outs],
+            scratch_shapes=list(scratch),
+        ),
+        out_shape=[shape for _, shape in outs],
+        compiler_params=pltpu.CompilerParams(vmem_limit_bytes=vmem * 1024 * 1024),
+        cost_estimate=pl.CostEstimate(flops=flops, bytes_accessed=moved, transcendentals=0),
+    )(info, *[array for _, array in ins])
+
+
+def smem():
+    return pl.BlockSpec(memory_space=pltpu.SMEM)
+
+
+def any_place():
+    return pl.BlockSpec(memory_space=pl.ANY)
+
+
+def whole(array):
+    dims = len(array.shape)
+    return pl.BlockSpec(array.shape, lambda *_: (0,) * dims, pipeline_mode=pl.Buffered(1))
+
+
+def block(shape, index):
+    return pl.BlockSpec(shape, index)
+
+
+def struct(shape, dtype):
+    return jax.ShapeDtypeStruct(shape, dtype)
+
+
+def columns(ref, info, place):
+    start = pl.multiple_of((info[0] ^ place) * 256, 256)
+    return ref[:, pl.ds(start, 256)]
+
+
+def norm_body(info, tok, cot, gain_a, shift_a, gain_m, shift_m, in_a, in_m, grad, grad_sum):
+    step = pl.program_id(0)
+    t = tok[...].astype(F32)
+    centered = t - jnp.mean(t, -1, keepdims=True)
+    xhat = centered * lax.rsqrt(jnp.mean(centered * centered, -1, keepdims=True) + EPS)
+    in_a[...] = (xhat * gain_a[...] + shift_a[...]).astype(BF)
+    in_m[...] = (xhat * gain_m[...] + shift_m[...]).astype(BF)
+    place = info[1] * 256 + lax.broadcasted_iota(jnp.int32, t.shape, 0)
+    g = jnp.where(place < info[5 + step], cot[...].astype(F32), 0.0)
+    grad[...] = g.astype(BF)
+
+    @pl.when(step == 0)
+    def _():
+        grad_sum[...] = jnp.zeros_like(grad_sum)
+
+    grad_sum[...] += jnp.sum(g, 0, keepdims=True)
+
+
+def matched(x, blocks, info):
+    left = jnp.concatenate([columns(x, info, r) for r in range(8)], 1)
+    right = jnp.concatenate([b[...] for b in blocks], 0)
+    return jnp.dot(left, right, preferred_element_type=F32)
+
+
+def turn(z, cos, front, back):
+    first = z[:, :128]
+    first = (
+        first * cos
+        + pltpu.roll(first, 96, 1) * front
+        + pltpu.roll(first, 32, 1) * back
+    )
+    return jnp.concatenate([first, z[:, 128:]], 1)
+
+
+def qkv_body(info, x, bias, cos, front, back, *refs):
+    blocks, (q, kv_a, kv_b) = (refs[:8], refs[8:16]), refs[16:]
+    step = pl.program_id(0)
+    heads = [matched(x, blocks[h], info) + bias[h : h + 1] for h in range(2)]
+
+    def turned():
+        c, f, b = (jnp.concatenate([t[...]] * 4, 0) for t in (cos, front, back))
+        return jnp.concatenate([turn(z, c, f, b) for z in heads], 1).astype(BF)
+
+    @pl.when(step == 0)
+    def _():
+        q[...] = turned()
+
+    @pl.when(step == 1)
+    def _():
+        k = turned()
+        kv_a[...] = k[:512]
+        kv_b[...] = k[512:]
+
+    @pl.when(step == 2)
+    def _():
+        v = jnp.concatenate(heads, 1).astype(BF)
+        kv_a[...] = v[:512]
+        kv_b[...] = v[512:]
+
+
+def grad_att_body(info, g, *refs):
+    refs[16][...] = jnp.concatenate(
+        [matched(g, refs[:8], info), matched(g, refs[8:16], info)], 1
+    ).astype(BF)
+
+
+def up_body(info, x, bias, *refs):
+    blocks, (act, slope) = refs[:8], refs[8:]
+    z = matched(x, blocks, info) + bias[...]
+    gelu, steep = gelu_pair(z)
+    act[...] = gelu.astype(BF)
+    slope[...] = steep.astype(BF)
+
+
+def hidden_body(info, g, slope, *refs):
+    low, total = refs[8:]
+    grad = matched(g, refs[:8], info) * slope[...].astype(F32)
+    low[...] = grad.astype(BF)
+    total[...] = jnp.sum(grad, 0, keepdims=True)
+
+
+def nt(a, b):
+    return lax.dot_general(a, b, (((1,), (1,)), ((), ())), preferred_element_type=F32)
+
+
+def tn(a, b):
+    return lax.dot_general(a, b, (((0,), (0,)), ((), ())), preferred_element_type=F32)
+
+
+def attention_body(first_seq, info, q_ref, ga_ref, cos, front, back, *refs):
+    keys, values = refs[:4], refs[4:8]
+    att, dq, dq_sum, keep, send = refs[8:]
+    terms = (keep.at[0], send.at[0], keep.at[1], send.at[1])
+    seq = pl.program_id(0)
+    head = pl.program_id(1)
+    scale = HEAD_DIM ** (-0.5)
+    length = info[5 + first_seq + seq]
+    q = q_ref[...]
+    ga = ga_ref[...]
+    row_place = info[1] * 256 + lax.broadcasted_iota(jnp.int32, (256, 256), 0)
+    column = lax.broadcasted_iota(jnp.int32, (256, 256), 1)
+    scores = []
+    masks = []
+    for r in range(4):
+        key_place = info[1 + r] * 256 + column
+        allowed = (key_place <= row_place) & (key_place < length)
+        masks.append(allowed)
+        scores.append(jnp.where(allowed, nt(q, keys[r][...]) * scale, FLOOR))
+    top = jnp.max(jnp.maximum(jnp.maximum(scores[0], scores[1]), jnp.maximum(scores[2], scores[3])), -1, keepdims=True)
+    weights = [jnp.where(m, jnp.exp(s - top), 0.0) for s, m in zip(scores, masks)]
+    total = jnp.sum(weights[0] + weights[1] + weights[2] + weights[3], -1, keepdims=True)
+    inverse = 1.0 / total
+    probs = [w * inverse for w in weights]
+    low = [p.astype(BF) for p in probs]
+    out = jnp.zeros((256, 256), F32)
+    for r in range(4):
+        out += jnp.dot(low[r], values[r][...], preferred_element_type=F32)
+    att[...] = out.astype(BF)
+    grad_probs = [nt(ga, values[r][...]) for r in range(4)]
+    products = [p * g for p, g in zip(probs, grad_probs)]
+    delta = jnp.sum(products[0] + products[1] + products[2] + products[3], -1, keepdims=True)
+    grad_q = jnp.zeros((256, 256), F32)
+    key_columns = pl.ds(pl.multiple_of(head * 256, 256), 256)
+    value_columns = pl.ds(pl.multiple_of(head * 256 + 512, 256), 256)
+    for r in range(4):
+        grad_scores = (probs[r] * (grad_probs[r] - delta)).astype(BF)
+        grad_q += jnp.dot(grad_scores, keys[r][...], preferred_element_type=F32)
+        terms[r][:, key_columns] = (tn(grad_scores, q) * scale).astype(BF)
+        terms[r][:, value_columns] = tn(low[r], ga).astype(BF)
+    grad_q = turn(grad_q * scale, cos[...], -front[...], -back[...])
+    dq[...] = grad_q.astype(BF)
+    dq_sum[...] = jnp.sum(grad_q, 0, keepdims=True)[None, None]
+
+
+def streamed(blocks, width, column):
+    return [
+        (pl.BlockSpec((256, width), lambda *ids: (0, column), pipeline_mode=pl.Buffered(1)), blocks[r])
+        for r in ORDER
+    ]
+
+
+def branch_body(info, att, act, *refs):
+    w_att = (refs[:8], refs[8:16])
+    w_act, outs = refs[16:24], refs[24:]
+    for i, r in enumerate(ORDER):
+        there = pl.ds(pl.multiple_of((info[0] ^ r) * 256, 256), 256)
+        part = nt(att[:, :256], w_att[0][i][...]) + nt(att[:, 256:], w_att[1][i][...])
+        part = (part + nt(act[...], w_act[i][...])).astype(BF)
+        outs[0][:, there] = part[:256]
+        outs[1][:, there] = part[256:]
+
+
+def weight_part(refs):
+    products = [tn(refs[i][...], refs[i + 1][...]) for i in range(0, len(refs), 2)]
+    return products[0] if len(products) == 1 else jnp.concatenate(products, 1)
+
+
+def weight_send_body(info, *refs):
+    refs[-1][...] = weight_part(refs[:-1]).astype(BF)
+
+
+def weight_add_body(info, *refs):
+    received, outs = refs[-5], refs[-4:]
+    step = pl.program_id(0)
+    part = (weight_part(refs[:-5]) + received[...].astype(F32)).astype(BF)
+    for i, out in enumerate(outs):
+
+        @pl.when(step == i)
+        def _():
+            out[...] = part
+
+
+def weight_first(info, pairs, x_first):
+    width = 2048
+    last, first = (4, 1) if not x_first else (1, 4)
+    order = (first, first | last, 0, last)
+    cost = dict(flops=2 * 1024 * 1024 * width, moved=2 * (1024 * 1024 + 1024 * width * 2))
+
+    def places(flip):
+        def index(i, info):
+            place = jnp.where(
+                i == 0, order[0], jnp.where(i == 1, order[1], jnp.where(i == 2, order[2], order[3]))
+            )
+            return 0, info[0] ^ place ^ flip
+
+        return index
+
+    fixed = lambda array: pl.BlockSpec(array.shape, lambda i, info: (0, 0), pipeline_mode=pl.Buffered(1))
+
+    def left(flip):
+        return [
+            operand
+            for x, h in pairs
+            for operand in ((block((1024, 256), places(flip)), x), (fixed(h), h))
+        ]
+
+    row = lambda i, info: (i, 0)
+    sent = call_placed(
+        weight_send_body,
+        (4,),
+        info,
+        left(2),
+        [(block((256, width), row), struct((1024, width), BF))],
+        **cost,
+    )[0]
+
+    def second(received):
+        return call_placed(
+            weight_add_body,
+            (4,),
+            info,
+            left(0) + [(block((256, width), row), received)],
+            [(block((256, width), lambda i, info: (0, 0)), struct((256, width), BF))] * 4,
+            **cost,
+        )
+
+    return sent, second
+
+
+def project_body(info, q, own, core, far, cos, front, back, low, kv_sum):
+    c, f, b = (jnp.concatenate([t[...]] * 2, 0) for t in (cos, front, back))
+    for head in range(2):
+        mine = slice(head * 256, head * 256 + 256)
+        low[:, head * 768 : head * 768 + 256] = q[:, mine]
+        for kind in range(2):
+            cut = slice(kind * 512 + head * 256, kind * 512 + head * 256 + 256)
+            grad = own[:, cut].astype(F32) + core[:, cut].astype(F32) + far[:, cut].astype(F32)
+            if kind == 0:
+                grad = turn(grad, c, -f, -b)
+            kv_sum[:, head * 512 + kind * 256 : head * 512 + kind * 256 + 256] = jnp.sum(grad, 0, keepdims=True)
+            start = head * 768 + 256 + kind * 256
+            low[:, start : start + 256] = grad.astype(BF)
+
+
+def input_body(info, low, hid, tok, gain_a, gain_m, *refs):
+    w_qkv = (refs[:8], refs[8:16])
+    w_up, parts, sums, (gx, xh) = refs[16:24], refs[24:26], refs[26], refs[27:]
+    t = tok[...].astype(F32)
+    centered = t - jnp.mean(t, -1, keepdims=True)
+    inverse = lax.rsqrt(jnp.mean(centered * centered, -1, keepdims=True) + EPS)
+    xh[...] = centered * inverse
+    for i, r in enumerate(ORDER):
+        there = pl.ds(pl.multiple_of((info[0] ^ r) * 256, 256), 256)
+        from_attn = nt(low[:, :768], w_qkv[0][i][:, :768]) + nt(low[:, 768:], w_qkv[1][i][:, :768])
+        from_mlp = nt(hid[...], w_up[i][...])
+        xhat = xh[:, there]
+        sums[0:1, there] = jnp.sum(from_attn * xhat, 0, keepdims=True)
+        sums[1:2, there] = jnp.sum(from_attn, 0, keepdims=True)
+        sums[2:3, there] = jnp.sum(from_mlp * xhat, 0, keepdims=True)
+        sums[3:4, there] = jnp.sum(from_mlp, 0, keepdims=True)
+        gx[:, there] = from_attn * gain_a[:, there] + from_mlp * gain_m[:, there]
+    grad = gx[...]
+    xhat = xh[...]
+    mean = jnp.mean(grad, -1, keepdims=True)
+    along = jnp.mean(grad * xhat, -1, keepdims=True)
+    out = (inverse * (grad - mean - xhat * along)).astype(BF)
+    parts[0][...] = out[:256]
+    parts[1][...] = out[256:]
+
+
+ENDS_IN = [(0, 1), (3, 2)]
+MIDDLE = [(1, 2), (2, 1)]
+ENDS_OUT = [(1, 0), (2, 3)]
+
+
+def plus(a, b):
+    return (a.astype(F32) + b.astype(F32)).astype(BF)
+
+
+def bar(*arrays):
+    return lax.optimization_barrier(arrays)
+
+
+class Hops:
+    def __init__(self, info, rows_of, tok, grad, bias):
+        self.info = info
+        self.rows_of = rows_of
+        self.given = (tok, grad, bias)
+        self.mine, self.came, self.pair, self.crossed, self.total, self.back = ({} for _ in range(6))
+        self.out = [None, None]
+
+    def send(self, k, block):
+        self.mine[k] = block
+        self.came[k] = lax.ppermute(block, "tensor", ENDS_IN)
+
+    def flying(self, k):
+        return [group[i] for group, i in ((self.came, k), (self.crossed, k - 1), (self.back, k - 2)) if i in group]
+
+    def land(self, k, *arrived):
+        arrived = list(arrived)
+        tok, grad, bias = self.given
+        ins, outs, kinds, aliases = [(smem(), self.info)], [], [], {}
+        half = lambda array: (block((128, D), lambda i: (i, 0)), array)
+        for kind, (group, i) in enumerate(((self.came, k), (self.crossed, k - 1), (self.back, k - 2))):
+            if i not in group:
+                continue
+            came = arrived.pop(0)
+            if kind < 2:
+                ins += [half((self.mine, self.pair)[kind][i]), half(came)]
+                outs.append((block((128, D), lambda i: (i, 0)), struct((256, D), BF)))
+            else:
+                place, which = i % 4, i // 4
+                kept = (block((128, D), lambda i, place=place: (2 * place + i, 0)), grad if which else tok)
+                ins += [half(self.total[i]), half(came), kept]
+                if not which:
+                    ins.append((whole(bias), bias))
+                shape = struct((1024, D), F32 if which else BF)
+                outs.append((kept[0], shape))
+                kind += which
+            kinds.append(kind)
+        old = self.out[kinds[-1] - 2] if kinds[-1] >= 2 else None
+        if old is not None:
+            aliases[len(ins)] = len(outs) - 1
+            ins.append((any_place(), old))
+        made = call(lambda *refs: land_body(kinds, *refs), (2,), ins, outs, aliases=aliases)
+        for kind, array in zip(kinds, made):
+            if kind == 0:
+                self.pair[k] = array
+                self.crossed[k] = lax.ppermute(array, "tensor", MIDDLE)
+            elif kind == 1:
+                self.total[k - 1] = array
+                self.back[k - 1] = lax.ppermute(array, "tensor", ENDS_OUT)
+            else:
+                self.out[kind - 2] = array
+        return made
+
+
+def land_body(kinds, info, *refs):
+    refs = list(refs)
+    outs = refs[-len(kinds) :]
+    for kind, out in zip(kinds, outs):
+        if kind < 2:
+            a, b = refs.pop(0), refs.pop(0)
+            out[...] = (a[...].astype(F32) + b[...].astype(F32)).astype(BF)
+            continue
+        total, came, kept = refs.pop(0), refs.pop(0), refs.pop(0)
+        summed = jnp.where(info[9] > 0, total[...], came[...]).astype(F32) + kept[...].astype(F32)
+        out[...] = (summed + refs.pop(0)[...]).astype(BF) if kind == 2 else summed
+
+
+def per_device_links(
+    tokens,
+    cotangent,
+    lengths,
+    block_slot,
+    gain_attn,
+    shift_attn,
+    gain_mlp,
+    shift_mlp,
+    w_qkv,
+    b_qkv,
+    w_out,
+    b_out,
+    w_up,
+    b_up,
+    w_down,
+    b_down,
+):
+    rows = 1024
+    seq_id = lax.axis_index("seq")
+    slots = [jnp.sum(jnp.where(jnp.arange(4) == (seq_id ^ r), block_slot, 0)) for r in range(4)]
+    tensor_id = lax.axis_index("tensor")
+    inner = ((tensor_id == 1) | (tensor_id == 2)).astype(jnp.int32)
+    me = seq_id * 2 + lax.axis_index("batch")
+    info = jnp.concatenate([jnp.stack([me, *slots]), lengths, inner.reshape(1)]).astype(jnp.int32)
+    tok = tokens.reshape(rows, D)
+    cot = cotangent.reshape(rows, D)
+    cosine, sine = rotation(slots[0] * 256 + jnp.arange(256, dtype=jnp.int32))
+    cosine, sine = cosine[:, 0], sine[:, 0]
+    zero = jnp.zeros_like(sine)
+    cos_t = jnp.concatenate([cosine, cosine, zero + 1.0, zero + 1.0], 1)
+    front_t = jnp.concatenate([-sine, zero, zero, zero], 1)
+    back_t = jnp.concatenate([zero, sine, zero, zero], 1)
+    tables = [(whole(t), t) for t in (cos_t, front_t, back_t)]
+    gains = [v.reshape(1, D) for v in (gain_attn, shift_attn, gain_mlp, shift_mlp)]
+
+    def info_in(*tokens_before):
+        return (smem(), after(info, *tokens_before) if tokens_before else info)
+
+    row_block = lambda n: block((256, n), lambda i: (i, 0))
+    row_struct = lambda n, kind=BF: struct((rows, n), kind)
+    tall = lambda n, index: block((256, n), index)
+
+    head_own = jnp.concatenate(
+        [w for h in range(2) for w in (w_qkv[:, h], w_out[h * 256 : (h + 1) * 256].T)], 1
+    )
+    head_x, head_y = along_x(head_own), along_y(head_own)
+    head_c = to_core(head_own)
+    in_a, in_m, grad_low, grad_sum = call(
+        norm_body,
+        (4,),
+        [info_in(), (row_block(D), tok), (row_block(D), cot)] + [(whole(v), v) for v in gains],
+        [(row_block(D), row_struct(D))] * 3 + [(block((1, D), lambda i: (0, 0)), struct((1, D), F32))],
+        moved=5 * rows * D * 2,
+    )
+    down_own = w_down.T
+    head_x, head_y, head_c, in_a, in_m, grad_low, down_own = bar(
+        head_x, head_y, head_c, in_a, in_m, grad_low, down_own
+    )
+
+    far_y, far_x = along_y(head_x[:128]), along_x(head_y[128:])
+    others = [head_c, to_core(head_x), to_core(head_y)]
+    far_y, far_x, up_own, *others = bar(far_y, far_x, w_up, *others)
+
+    up_x, up_y = along_x(up_own), along_y(up_own)
+    far = jnp.concatenate([far_y, far_x], 0)
+    heads = both_cores(head_own, head_x, head_y, far, *others, to_core(far))
+    bias = jnp.swapaxes(b_qkv.reshape(2, 3, 256), 0, 1)
+    q, kv_a, kv_b = call(
+        lambda info, x, bias, *refs: qkv_body(info, x, bias.at[0], *refs),
+        (3,),
+        [info_in(), (whole(in_a), in_a), (block((1, 2, 256), lambda j: (j, 0, 0)), bias)]
+        + tables
+        + block_ins(heads, 256, lambda j: j)
+        + block_ins(heads, 256, lambda j: j + 4),
+        [
+            (block((rows, 512), lambda j: (0, 0)), row_struct(512)),
+            (block((512, 512), lambda j: (0, jnp.maximum(j - 1, 0))), struct((512, 1024), BF)),
+            (block((512, 512), lambda j: (0, jnp.maximum(j - 1, 0))), struct((512, 1024), BF)),
+        ],
+        flops=2 * rows * D * 1536,
+        moved=2 * (rows * D + D * 1536 + rows * 1536),
+    )
+    kv_x = along_x(kv_a)
+    grad_att = call(
+        grad_att_body,
+        (1,),
+        [info_in(q), (whole(grad_low), grad_low)]
+        + block_ins(heads, 256, lambda j: 3)
+        + block_ins(heads, 256, lambda j: 7),
+        [(block((rows, 512), lambda j: (0, 0)), row_struct(512))],
+        flops=2 * rows * D * 512,
+        moved=2 * (rows * D + D * 512 + rows * 512),
+    )[0]
+    up_c = to_core(after(up_own, q))
+    up_x, up_y, up_c, grad_att = bar(up_x, up_y, up_c, grad_att)
+
+    up_far = along_y(up_x)
+    others = [up_c, to_core(up_x), to_core(up_y)]
+    down_own = after(down_own, *others)
+    down_x, down_y = along_x(down_own), along_y(down_own)
+    up_far, kv_x, kv_a, *others = bar(up_far, kv_x, kv_a, *others)
+    ups = both_cores(up_own, up_x, up_y, up_far, *others, to_core(up_far))
+
+    def kv_refs(own, by_x):
+        both = to_core(jnp.concatenate([own, by_x], 0))
+        return [(own, 0), (both, 0), (by_x, 0), (both, 2)]
+
+    kv = [kv_refs(kv_a, kv_x)]
+    act, slope = call(
+        up_body,
+        (4,),
+        [info_in(grad_att), (whole(in_m), in_m), (block((1, 512), lambda j: (0, j)), b_up.reshape(1, -1))]
+        + block_ins(ups, 512, lambda j: j),
+        [(block((rows, 512), lambda j: (0, j)), row_struct(2048))] * 2,
+        flops=2 * rows * D * 2048,
+        moved=2 * (rows * D + D * 2048 + 2 * rows * 2048),
+    )
+    down_c = to_core(after(down_own, ups[7]))
+    down_x, down_y, down_c, act, slope = bar(down_x, down_y, down_c, act, slope)
+
+    def attention(part, *before):
+        base = part * 2
+        spot = lambda offset: block((256, 256), lambda s, h: (s + base, h + offset))
+        local = lambda offset, row=0: block((256, 256), lambda s, h: (s + row, h + offset))
+        return call(
+            lambda *refs: attention_body(base, *refs),
+            (2, 2),
+            [info_in(*before), (spot(0), q), (spot(0), grad_att)]
+            + tables
+            + [(local(0, row), b) for b, row in kv[part]]
+            + [(local(2, row), b) for b, row in kv[part]],
+            [
+                (local(0), struct((512, 512), BF)),
+                (local(0), struct((512, 512), BF)),
+                (block((1, 1, 1, 256), lambda s, h: (s, h, 0, 0)), struct((2, 2, 1, 256), F32)),
+            ]
+            + [(block((2, 256, 1024), lambda s, h: (0, s, 0)), struct((2, 512, 1024), BF))] * 2,
+            flops=4 * 6 * 2 * 256 * 1024 * 256,
+            moved=4 * 2 * 256 * 256 * 24,
+        )
+
+    def branch(part, att, *before):
+        return call(
+            branch_body,
+            (1,),
+            [info_in(*before), (whole(att), att), (block((512, 2048), lambda i: (part, 0)), act)]
+            + streamed(heads, 256, 3)
+            + streamed(heads, 256, 7)
+            + streamed(downs, 2048, 0),
+            [(block((256, D), lambda i: (0, 0)), struct((256, D), BF))] * 2,
+            flops=2 * 512 * D * 2560,
+            moved=2 * (512 * 2560 + D * 2560 + 512 * D),
+        )
+
+    far_y, far_x = along_y(down_x[:128]), along_x(down_y[128:])
+    others = [down_c, to_core(down_x), to_core(down_y)]
+    att_a, dq_a, dq_sum_a, keep_a, send_a = attention(0, down_x)
+    far_y, far_x, att_a, kv_b, send_a, *others = bar(far_y, far_x, att_a, kv_b, send_a, *others)
+
+    far = jnp.concatenate([far_y, far_x], 0)
+    downs = both_cores(down_own, down_x, down_y, far, *others, to_core(far))
+    kv_x = along_x(kv_b)
+    received_a = to_core(send_a)
+    branch_a = branch(0, att_a)
+    kv_x, received_a, *branch_a = bar(kv_x, received_a, *branch_a)
+
+    hops = Hops(info, 256, tok, grad_low, (b_out + b_down).reshape(1, D))
+    attended = None
+
+    def hidden_call(before):
+        return call(
+            hidden_body,
+            (4,),
+            [info_in(before), (whole(grad_low), grad_low), (block((rows, 512), lambda j: (0, j)), slope)]
+            + block_ins(downs, 512, lambda j: j),
+            [
+                (block((rows, 512), lambda j: (0, j)), row_struct(2048)),
+                (block((1, 512), lambda j: (0, j)), struct((1, 2048), F32)),
+            ],
+            flops=2 * rows * D * 2048,
+            moved=2 * (rows * D + D * 2048 + 2 * rows * 2048),
+        )
+
+    def project(dq, keep, came, far, before):
+        return call(
+            project_body,
+            (1,),
+            [info_in(before), (whole(dq), dq)]
+            + [(pl.BlockSpec((None, 512, 1024), lambda i: (0, 0, 0)), t) for t in (keep, came)]
+            + [(whole(far), far)]
+            + tables,
+            [
+                (block((512, 1536), lambda i: (0, 0)), struct((512, 1536), BF)),
+                (block((1, 1024), lambda i: (0, 0)), struct((1, 1024), F32)),
+            ],
+            moved=2 * 512 * 5000,
+        )
+
+    def input_part(half, low, before):
+        fixed = lambda shape, row=0: pl.BlockSpec(shape, lambda i: (row, 0), pipeline_mode=pl.Buffered(1))
+        return call(
+            input_body,
+            (1,),
+            [info_in(before), (whole(low), low)]
+            + [(fixed((512, 2048), half), t) for t in (hidden_low, tok)]
+            + [(whole(t), t) for t in (gains[0], gains[2])]
+            + streamed(heads, 1024, 0)
+            + streamed(heads, 1024, 1)
+            + streamed(ups, 2048, 0),
+            [(block((256, D), lambda i: (0, 0)), struct((256, D), BF))] * 2
+            + [(block((8, D), lambda i: (0, 0)), struct((8, D), F32))],
+            scratch=[pltpu.VMEM((512, D), F32), pltpu.VMEM((512, D), F32)],
+            flops=2 * 512 * D * 3584,
+            moved=2 * (512 * 6000 + D * 3584),
+        )
+
+    hops.send(0, branch_a[0])
+    kv.append(kv_refs(kv_b, kv_x))
+    far_a = along_x(plus(keep_a[1], received_a[1]))
+    hidden_low, b_up_sum = hidden_call(branch_a[0])
+    att_b, dq_b, dq_sum_b, keep_b, send_b = attention(1, hidden_low)
+    flown, far_a, att_b, send_b = bar(hops.flying(0), far_a, att_b, send_b)
+
+    pair, = hops.land(0, *flown)
+    hops.send(1, after(branch_a[1], pair))
+    received_b = to_core(after(send_b, pair))
+    branch_b = branch(1, att_b, pair)
+    down_sent, down_second = weight_first(after(info, branch_b[0]), [(grad_low, act)], False)
+    flown, received_b, down_sent, *branch_b = bar(hops.flying(1), received_b, down_sent, *branch_b)
+
+    pair, *_ = hops.land(1, *flown)
+    hops.send(2, after(branch_b[0], pair))
+    far_b = along_x(plus(after(keep_b[1], pair), received_b[1]))
+    down_received = to_core(after(down_sent, pair))
+    low_a, kv_sum_a = project(dq_a, keep_a, received_a, far_a, pair)
+    first, second, norm_sum_a = input_part(0, low_a, low_a)
+    flown, far_b, down_received, first, second = bar(hops.flying(2), far_b, down_received, first, second)
+
+    pair, *_ = hops.land(2, *flown)
+    hops.send(3, after(branch_b[1], pair))
+    low_b, kv_sum_b = project(dq_b, keep_b, received_b, far_b, pair)
+    third, fourth, norm_sum_b = input_part(1, low_b, low_b)
+    project_low = jnp.concatenate([low_a, after(low_b, third)], 0)
+    attended = jnp.concatenate([att_a, after(att_b, third)], 0)
+    q_sums = (dq_sum_a + dq_sum_b).sum(0).reshape(2, 1, 256)
+    kv_total = (kv_sum_a + kv_sum_b).reshape(2, 2, 256)
+    bias_qkv = jnp.concatenate([q_sums, kv_total], 1).reshape(-1)
+    norm_sums = (norm_sum_a + norm_sum_b)[:4].reshape(-1)
+    small = jnp.concatenate([norm_sums, bias_qkv, grad_sum[0], b_up_sum[0]]).reshape(-1, 128)
+    flown, third, fourth, small, project_low, attended = bar(
+        hops.flying(3), third, fourth, small, project_low, attended
+    )
+
+    pair, *_ = hops.land(3, *flown)
+    hops.send(4, after(first, pair))
+    small = after(small, pair)
+    small = small + to_core(small)
+    down = down_second(after(down_received, pair))
+    small = small + along_x(small)
+    up_sent, up_second = weight_first(after(info, down[0], small), [(in_m, hidden_low)], True)
+    flown, up_sent, small, *down = bar(hops.flying(4), up_sent, small, *down)
+
+    pair, *_ = hops.land(4, *flown)
+    hops.send(5, after(second, pair))
+    down_got = [along_y(after(down[0], pair))]
+    up_received = to_core(after(up_sent, pair))
+    attn_sent, attn_second = weight_first(
+        after(info, pair), [(in_a, project_low), (grad_low, attended)], False
+    )
+    up = up_second(after(up_received, attn_sent))
+    flown, down_got[0], attn_sent, *up = bar(hops.flying(5), down_got[0], attn_sent, *up)
+
+    pair, *_ = hops.land(5, *flown)
+    hops.send(6, after(third, pair))
+    attn_received = to_core(after(attn_sent, pair))
+    down_got.append(along_y(after(down[1], pair)))
+    up_got = [along_x(after(up[0], pair))]
+    attn = attn_second(after(attn_received, pair))
+    flown, down_got[1], up_got[0], *attn = bar(hops.flying(6), down_got[1], up_got[0], *attn)
+
+    pair, *_ = hops.land(6, *flown)
+    hops.send(7, after(fourth, pair))
+    up_got.append(along_x(after(up[1], pair)))
+    attn_got = [along_y(after(attn[0], pair))]
+    down_leaving = plus(after(down[3], pair), down_got[1])
+    flown, up_got[1], attn_got[0], down_leaving = bar(hops.flying(7), up_got[1], attn_got[0], down_leaving)
+
+    pair, *_ = hops.land(7, *flown)
+    down_last = along_x(after(down_leaving, pair))
+    attn_got.append(along_y(after(attn[1], pair)))
+    small = after(small, pair)
+    small = small + along_y(small)
+    up_leaving = plus(after(up[3], pair), up_got[1])
+    flown, down_last, attn_got[1], small, up_leaving = bar(
+        hops.flying(8), down_last, attn_got[1], small, up_leaving
+    )
+
+    sum_8, *_ = hops.land(8, *flown)
+    attn_last = along_x(plus(after(attn[3], sum_8), attn_got[1]))
+    up_last = along_y(after(up_leaving, sum_8))
+    norms = after(small[:64], sum_8)
+    for flip in (1, 2):
+        norms = norms + exchange(norms, "tensor", flip)
+
+    def total(keep, got, last):
+        return keep.astype(F32) + got.astype(F32) + last.astype(F32)
+
+    down_grad = total(after(down[2], sum_8), down_got[0], down_last).T
+    flown, attn_last, norms, up_last, down_grad = bar(hops.flying(9), attn_last, norms, up_last, down_grad)
+    hops.land(9, *flown)
+    mixed, tokens_grad = hops.out
+
+    norms = norms.reshape(4, D)
+    small = small[64:].reshape(-1)
+    bias_out = small[1536 : 1536 + D]
+
+    attn_grad = total(attn[2], attn_got[0], attn_last)
+    return (
+        mixed.reshape(tokens.shape),
+        tokens_grad.reshape(tokens.shape),
+        norms[0],
+        norms[1],
+        norms[2],
+        norms[3],
+        attn_grad[:, :1536].reshape(w_qkv.shape),
+        small[:1536].reshape(b_qkv.shape),
+        attn_grad[:, 1536:].T,
+        bias_out,
+        total(up[2], up_got[0], up_last),
+        small[1536 + D :],
+        down_grad,
+        bias_out,
+    )
+
+
 def solution(mesh):
     in_specs = (
         P("batch", "seq", None),
@@ -247,6 +1014,8 @@
         P("tensor", ("seq", "batch")),
         P(),
     )
+    links = tuple(mesh.shape[axis] for axis in ("seq", "batch", "tensor"))
+    per_device = per_device_links if links == (4, 2, 4) else per_device_any
     return jax.shard_map(
         per_device, mesh=mesh, in_specs=in_specs, out_specs=out_specs, check_vma=False
     )

time: 936 us -> 585 us (0.62)
  waiting for transfers between devices: 509 us -> 153 us
  Pallas kernels: 0 us -> 257 us
  matrix products: 177 us -> 0 us
  starting transfers between devices: 0.59 us -> 98.8 us
  other arithmetic: 120 us -> 27.9 us
  blocking collectives: 46.1 us -> 0 us
  local copies, waits for them, and re-layouts: 58 us -> 33.8 us
  between operations: 15.8 us -> 2.5 us
    pallas_call x0 -> x29, Pallas kernels: none -> 257 us  [the longest x23 195 us: call(): pl.pallas_call(body, grid=grid, in_specs=[spec for spec, _ in ins], out_s...]
    reduce_scatter x3 -> x0, waiting for transfers between devices: 243 us -> none  [the longest x1 109 us: per_device(): lax.psum_scatter(grad_mlp_weights, fsdp, scatter_dimension=0, tiled=True)]
    dot_general x18 -> x0, matrix products: 177 us -> none  [the longest x12 141 us: dot(): return lax.dot_general(a, b, (dims, ((), ())), preferred_element_type=F32)]
    ppermute x0 -> x72, waiting for transfers between devices: none -> 153 us  [the longest x48 131 us: exchange(): return lax.ppermute(array, axis, [(i, i ^ flip) for i in range(size)])]
    all_gather x3 -> x0, waiting for transfers between devices: 137 us -> none  [the longest x1 56.1 us: per_device(): mlp_full = lax.all_gather(mlp_shard, fsdp, axis=0, tiled=True)]
    psum x2 -> x0, waiting for transfers between devices: 128 us -> none  [the longest x1 82.7 us: per_device(): branch = lax.psum(partial.astype(BF), 'tensor').astype(F32)]
    ppermute x0 -> x72, starting transfers between devices: none -> 98.8 us  [the longest x8 44.6 us: send(): self.came[k] = lax.ppermute(block, 'tensor', ENDS_IN)]
    psum x2 -> x0, blocking collectives: 46.1 us -> none  [the longest x1 25.2 us: per_device(): lax.psum(jnp.concatenate([norm_sums, bias_qkv_sum, jnp.sum(grad_rows, 0),...]
  transfers between devices with their start and end apart: 8 -> 72, of which waited for: 8 -> 29; matrix products, arithmetic and copies ran while one was open for 25% -> 6% of each run, Pallas kernels for 0% -> 38%
where the time goes in v3:
time: 585 us; the launch traced here: 573 us
  Pallas kernels  257 us (44%)
  waiting for transfers between devices  153 us (26%)
  starting transfers between devices  98.8 us (17%)
  local copies, waits for them, and re-layouts  33.8 us (6%)
  other arithmetic  27.9 us (5%)
    pallas_call x23, Pallas kernels, call(): pl.pallas_call(body, grid=grid, in_specs=[spec for spec, _ in ins], out_s...  195 us
    ppermute x48, waiting for transfers between devices, exchange(): return lax.ppermute(array, axis, [(i, i ^ flip) for i in range(size)])  131 us
    pallas_call x6, Pallas kernels, call_placed(): pl.pallas_call(body, grid_spec=pltpu.PrefetchScalarGridSpec(num_scalar_pr...  62.1 us
    ppermute x8, starting transfers between devices, send(): self.came[k] = lax.ppermute(block, 'tensor', ENDS_IN)  44.6 us
    ppermute x48, starting transfers between devices, exchange(): return lax.ppermute(array, axis, [(i, i ^ flip) for i in range(size)])  33.2 us
    ppermute x8, waiting for transfers between devices, land(): self.back[k - 1] = lax.ppermute(array, 'tensor', ENDS_OUT)  18.7 us
    unnamed x133, local copies, waits for them, and re-layouts  14.2 us
  transfers between devices with their start and end apart: 72, of which 29 were waited for; matrix products, arithmetic and copies ran while one was open for 6% of the time, Pallas kernels for 38%

profile of v3, /device:TPU:0, one launch (start us, length us, event | category | flops | bytes accessed | tf_op | source)
XLA Modules:
  0.0 573.4 jit_solution(13350875388450515109)
XLA Ops:
  14.7 11.4 %shard_map.263 = (bf16[1024,2048]{1,0:T(8,128)(2,1)}, bf16[1024,2048]{1,0:T(8,128)(2,1)}, bf16[1024,2048]{1,0:T(8,128)(2,1)}, f32[1,2048]{1,0:T(1,128)}) custom-call(s32[10]{0:T(128)} %concatenate.46.info.refs_0_, bf16[1024,2048]{1,0:T(8,128)(2,1)} %bitcast.56, bf16[1024,2048]{1,0:T(8,128)(2,1)} %bitcast.71, f32[1,2048]{1,0:T(1,128)} %bitcast.79, ...), custom_call_target="tpu_custom_call" | custom-call | bytes 20971520 | tf_op jit(solution)/shard_map/pallas_call | solution.py:251
  34.3 11.8 %collective-permute-done.3 = bf16[128,2048]{1,0:T(8,128)(2,1)S(1)} collective-permute-done((bf16[128,2048]{1,0:T(8,128)(2,1)S(1)}, bf16[128,2048]{1,0:T(8,128)(2,1)S(1)}, u32[]{:S(2)}, u32[]{:S(2)}) %collective-permute-start.3) | collective-permute-done | bytes 524320 | tf_op jit(solution)/shard_map/ppermute | solution.py:219
  52.6 13.1 %shard_map.264 = (bf16[1024,512]{1,0:T(8,128)(2,1)}, bf16[512,1024]{1,0:T(8,128)(2,1)}, bf16[512,1024]{1,0:T(8,128)(2,1)}) custom-call(s32[10]{0:T(128)} %concatenate.46.info.refs_0_, bf16[1024,2048]{1,0:T(8,128)(2,1)} %get-tuple-element.248.x.refs_0_, f32[3,2,256]{2,1,0:T(2,128)} %bitcast.90, f32[256,128]{1,0:T(8,128)} %get-tuple-element.513.refs_0_.refs_3_.cos, ...), custom_call_target="tpu_custom_call" | custom-call | flops 6442450944 | bytes 13631488 | tf_op jit(solution)/shard_map/pallas_call | solution.py:251
  67.5 6.2 %shard_map.265.refs_2_ = bf16[1024,512]{1,0:T(8,128)(2,1)} custom-call(s32[10]{0:T(128)} %concatenate.46.info.refs_0_, bf16[1024,2048]{1,0:T(8,128)(2,1)} %get-tuple-element.257.g.refs_0_.refs_2_.refs_7_.refs_5_.refs_3_, bf16[256,2048]{1,0:T(8,128)(2,1)} %copy-done, bf16[256,2048]{1,0:T(8,128)(2,1)} %copy-done.2, ...), custom_call_target="tpu_custom_call" | custom-call | flops 2147483648 | bytes 7340032 | tf_op jit(solution)/shard_map/pallas_call | solution.py:251
  79.0 21.0 %collective-permute-done.16.refs_8_.refs_12_ = bf16[512,1024]{1,0:T(8,128)(2,1)S(1)} collective-permute-done((bf16[512,1024]{1,0:T(8,128)(2,1)}, bf16[512,1024]{1,0:T(8,128)(2,1)S(1)}, u32[]{:S(2)}, u32[]{:S(2)}) %collective-permute-start.16) | collective-permute-done | bytes 1048608 | tf_op jit(solution)/shard_map/ppermute | solution.py:219
  108.6 16.8 %shard_map.266 = (bf16[1024,2048]{1,0:T(8,128)(2,1)}, bf16[1024,2048]{1,0:T(8,128)(2,1)}) custom-call(s32[10]{0:T(128)} %concatenate.46.info.refs_0_, bf16[1024,2048]{1,0:T(8,128)(2,1)} %get-tuple-element.267.x.refs_0_, f32[1,2048]{1,0:T(1,128)} %bitcast.89, bf16[256,2048]{1,0:T(8,128)(2,1)} %refs_16_.1, ...), custom_call_target="tpu_custom_call" | custom-call | flops 8589934592 | bytes 20971520 | tf_op jit(solution)/shard_map/pallas_call | solution.py:251
  125.5 5.7 collective-permute-done.13.refs_18_.refs_4_
  139.0 10.7 %shard_map.267 = (bf16[512,512]{1,0:T(8,128)(2,1)}, bf16[512,512]{1,0:T(8,128)(2,1)}, f32[2,2,1,256]{3,2,1,0:T(1,128)}, bf16[2,512,1024]{2,1,0:T(8,128)(2,1)}, bf16[2,512,1024]{2,1,0:T(8,128)(2,1)}) custom-call(s32[10]{0:T(128)} %concatenate.46.info.refs_0_, bf16[1024,512]{1,0:T(8,128)(2,1)} %get-tuple-element.254.refs_1_, ...), custom_call_target="tpu_custom_call" | custom-call | flops 3221225472 | bytes 12582912 | tf_op jit(solution)/shard_map/pallas_call | solution.py:251
  156.7 11.7 %shard_map.268 = (bf16[256,2048]{1,0:T(8,128)(2,1)}, bf16[256,2048]{1,0:T(8,128)(2,1)}) custom-call(s32[10]{0:T(128)} %concatenate.46.info.refs_0_, bf16[512,512]{1,0:T(8,128)(2,1)} %get-tuple-element.284.att, bf16[1024,2048]{1,0:T(8,128)(2,1)} %get-tuple-element.285.act.refs_1_, bf16[256,2048]{1,0:T(8,128)(2,1)} %copy-done, ...), custom_call_target="tpu_custom_call" | custom-call | flops 5368709120 | bytes 15204352 | tf_op jit(solution)/shard_map/pallas_call | solution.py:251
  168.4 9.3 %collective-permute-done.24.refs_8_.refs_12_ = bf16[512,1024]{1,0:T(8,128)(2,1)S(1)} collective-permute-done((bf16[512,1024]{1,0:T(8,128)(2,1)S(1)}, bf16[512,1024]{1,0:T(8,128)(2,1)S(1)}, u32[]{:S(2)}, u32[]{:S(2)}) %collective-permute-start.24) | collective-permute-done | bytes 1048608 | tf_op jit(solution)/shard_map/ppermute | solution.py:219
  188.0 14.4 %shard_map.269 = (bf16[1024,2048]{1,0:T(8,128)(2,1)}, f32[1,2048]{1,0:T(1,128)}) custom-call(s32[10]{0:T(128)} %concatenate.46.info.refs_0_, bf16[1024,2048]{1,0:T(8,128)(2,1)} %get-tuple-element.257.g.refs_0_.refs_2_.refs_7_.refs_5_.refs_3_, bf16[1024,2048]{1,0:T(8,128)(2,1)} %get-tuple-element.298.slope, bf16[256,2048]{1,0:T(8,128)(2,1)} %bitcast.66, ...), custom_call_target="tpu_custom_call" | custom-call | flops 8589934592 | bytes 20971520 | tf_op jit(solution)/shard_map/pallas_call | solution.py:251
  203.7 10.3 %shard_map.270 = (bf16[512,512]{1,0:T(8,128)(2,1)}, bf16[512,512]{1,0:T(8,128)(2,1)}, f32[2,2,1,256]{3,2,1,0:T(1,128)}, bf16[2,512,1024]{2,1,0:T(8,128)(2,1)}, bf16[2,512,1024]{2,1,0:T(8,128)(2,1)}) custom-call(s32[10]{0:T(128)} %concatenate.46.info.refs_0_, bf16[1024,512]{1,0:T(8,128)(2,1)} %get-tuple-element.254.refs_1_, ...), custom_call_target="tpu_custom_call" | custom-call | flops 3221225472 | bytes 12582912 | tf_op jit(solution)/shard_map/pallas_call | solution.py:251
  220.8 11.7 %shard_map.272 = (bf16[256,2048]{1,0:T(8,128)(2,1)}, bf16[256,2048]{1,0:T(8,128)(2,1)}) custom-call(s32[10]{0:T(128)} %concatenate.46.info.refs_0_, bf16[512,512]{1,0:T(8,128)(2,1)} %get-tuple-element.356.att, bf16[1024,2048]{1,0:T(8,128)(2,1)} %get-tuple-element.285.act.refs_1_, bf16[256,2048]{1,0:T(8,128)(2,1)} %copy-done, ...), custom_call_target="tpu_custom_call" | custom-call | flops 5368709120 | bytes 15204352 | tf_op jit(solution)/shard_map/pallas_call | solution.py:251
  232.6 9.4 %shard_map.273 = bf16[1024,2048]{1,0:T(8,128)(2,1)} custom-call(s32[10]{0:T(128)} %concatenate.46.info.refs_0_, bf16[1024,2048]{1,0:T(8,128)(2,1)} %get-tuple-element.257.g.refs_0_.refs_2_.refs_7_.refs_5_.refs_3_, bf16[1024,2048]{1,0:T(8,128)(2,1)} %get-tuple-element.285.act.refs_1_), custom_call_target="tpu_custom_call" | custom-call | flops 4294967296 | bytes 10485760 | tf_op jit(solution)/shard_map/pallas_call | solution.py:265
  252.4 5.6 collective-permute-start.33
  264.3 19.5 %shard_map.276 = (bf16[256,2048]{1,0:T(8,128)(2,1)}, bf16[256,2048]{1,0:T(8,128)(2,1)}, f32[8,2048]{1,0:T(8,128)}) custom-call(s32[10]{0:T(128)} %concatenate.46.info.refs_0_, bf16[512,1536]{1,0:T(8,128)(2,1)} %get-tuple-element.327.low, bf16[1024,2048]{1,0:T(8,128)(2,1)} %get-tuple-element.299.hid.refs_1_, bf16[1024,2048]{1,0:T(8,128)(2,1)} %bitcast.57, ...), custom_call_target="tpu_custom_call" | custom-call | flops 7516192768 | bytes 20824064 | tf_op jit(solution)/shard_map/pallas_call | solution.py:251
  295.2 7.1 %collective-permute-start.38 = (bf16[256,2048]{1,0:T(8,128)(2,1)}, bf16[256,2048]{1,0:T(8,128)(2,1)}, u32[]{:S(2)}, u32[]{:S(2)}) collective-permute-start(bf16[256,2048]{1,0:T(8,128)(2,1)} %get-tuple-element.338.refs_1_), channel_id=1, source_target_pairs={{0,1},{3,2},{4,5},{7,6},{8,9},{11,10},{12,13},{15,14},{16,17},{19,... | collective-permute-start | bytes 3145736 | tf_op jit(solution)/shard_map/ppermute | solution.py:589
  304.0 19.6 %shard_map.279 = (bf16[256,2048]{1,0:T(8,128)(2,1)}, bf16[256,2048]{1,0:T(8,128)(2,1)}, f32[8,2048]{1,0:T(8,128)}) custom-call(s32[10]{0:T(128)} %concatenate.46.info.refs_0_, bf16[512,1536]{1,0:T(8,128)(2,1)} %get-tuple-element.355.low, bf16[1024,2048]{1,0:T(8,128)(2,1)} %get-tuple-element.299.hid.refs_1_, bf16[1024,2048]{1,0:T(8,128)(2,1)} %bitcast.59, ...), custom_call_target="tpu_custom_call" | custom-call | flops 7516192768 | bytes 20824064 | tf_op jit(solution)/shard_map/pallas_call | solution.py:251
  334.3 8.4 %collective-permute-start.41 = (bf16[256,2048]{1,0:T(8,128)(2,1)S(1)}, bf16[256,2048]{1,0:T(8,128)(2,1)S(1)}, u32[]{:S(2)}, u32[]{:S(2)}) collective-permute-start(bf16[256,2048]{1,0:T(8,128)(2,1)S(1)} %copy-done.42), channel_id=1, source_target_pairs={{0,1},{3,2},{4,5},{7,6},{8,9},{11,10},{12,13},{15,14},{16,17},{19,... | collective-permute-start | bytes 3145736 | tf_op jit(solution)/shard_map/ppermute | solution.py:589
  346.5 11.0 %shard_map.281 = (bf16[256,2048]{1,0:T(8,128)(2,1)}, bf16[256,2048]{1,0:T(8,128)(2,1)}, bf16[256,2048]{1,0:T(8,128)(2,1)}, bf16[256,2048]{1,0:T(8,128)(2,1)}) custom-call(s32[10]{0:T(128)} %concatenate.46.info.refs_0_, bf16[1024,2048]{1,0:T(8,128)(2,1)} %get-tuple-element.257.g.refs_0_.refs_2_.refs_7_.refs_5_.refs_3_, ...), custom_call_target="tpu_custom_call" | custom-call | flops 4294967296 | bytes 10485760 | tf_op jit(solution)/shard_map/pallas_call | solution.py:265
  357.6 9.4 %shard_map.282 = bf16[1024,2048]{1,0:T(8,128)(2,1)} custom-call(s32[10]{0:T(128)} %concatenate.46.info.refs_0_, bf16[1024,2048]{1,0:T(8,128)(2,1)} %get-tuple-element.267.x.refs_0_, bf16[1024,2048]{1,0:T(8,128)(2,1)} %get-tuple-element.299.hid.refs_1_), custom_call_target="tpu_custom_call" | custom-call | flops 4294967296 | bytes 10485760 | tf_op jit(solution)/shard_map/pallas_call | solution.py:265
  375.2 8.1 %collective-permute-start.46 = (bf16[256,2048]{1,0:T(8,128)(2,1)S(1)}, bf16[256,2048]{1,0:T(8,128)(2,1)}, u32[]{:S(2)}, u32[]{:S(2)}) collective-permute-start(bf16[256,2048]{1,0:T(8,128)(2,1)S(1)} %copy-done.41), channel_id=1, source_target_pairs={{0,1},{3,2},{4,5},{7,6},{8,9},{11,10},{12,13},{15,14},{16,17},{19,... | collective-permute-start | bytes 3145736 | tf_op jit(solution)/shard_map/ppermute | solution.py:589
  384.6 9.7 %shard_map.284 = bf16[1024,2048]{1,0:T(8,128)(2,1)} custom-call(s32[10]{0:T(128)} %concatenate.46.info.refs_0_, bf16[1024,2048]{1,0:T(8,128)(2,1)} %get-tuple-element.248.x.refs_0_, bf16[1024,1536]{1,0:T(8,128)(2,1)} %pad_maximum_fusion.refs_1_, bf16[1024,2048]{1,0:T(8,128)(2,1)} %get-tuple-element.257.g.refs_0_.refs_2_.refs_7_.refs_5_.refs_3_, ...), custom_call_target="tpu_custom_call" | custom-call | flops 4294967296 | bytes 10485760 | tf_op jit(solution)/shard_map/pallas_call | solution.py:265
  394.3 11.1 %shard_map.285 = (bf16[256,2048]{1,0:T(8,128)(2,1)}, bf16[256,2048]{1,0:T(8,128)(2,1)}, bf16[256,2048]{1,0:T(8,128)(2,1)}, bf16[256,2048]{1,0:T(8,128)(2,1)}) custom-call(s32[10]{0:T(128)} %concatenate.46.info.refs_0_, bf16[1024,2048]{1,0:T(8,128)(2,1)} %get-tuple-element.267.x.refs_0_, bf16[1024,2048]{1,0:T(8,128)(2,1)} %get-tuple-element.299.hid.refs_1_, ...), custom_call_target="tpu_custom_call" | custom-call | flops 4294967296 | bytes 10485760 | tf_op jit(solution)/shard_map/pallas_call | solution.py:265
  405.4 4.8 collective-permute-done.48.refs_6_
  424.0 11.6 %shard_map.287 = (bf16[256,2048]{1,0:T(8,128)(2,1)}, bf16[256,2048]{1,0:T(8,128)(2,1)}, bf16[256,2048]{1,0:T(8,128)(2,1)}, bf16[256,2048]{1,0:T(8,128)(2,1)}) custom-call(s32[10]{0:T(128)} %concatenate.46.info.refs_0_, bf16[1024,2048]{1,0:T(8,128)(2,1)} %get-tuple-element.248.x.refs_0_, bf16[1024,1536]{1,0:T(8,128)(2,1)} %pad_maximum_fusion.refs_1_, ...), custom_call_target="tpu_custom_call" | custom-call | flops 4294967296 | bytes 10485760 | tf_op jit(solution)/shard_map/pallas_call | solution.py:265
  435.6 6.5 %collective-permute-done.55 = bf16[256,2048]{1,0:T(8,128)(2,1)S(1)} collective-permute-done((bf16[256,2048]{1,0:T(8,128)(2,1)}, bf16[256,2048]{1,0:T(8,128)(2,1)S(1)}, u32[]{:S(2)}, u32[]{:S(2)}) %collective-permute-start.55) | collective-permute-done | bytes 1048608 | tf_op jit(solution)/shard_map/ppermute | solution.py:219
  444.2 5.4 collective-permute-done.53.refs_6_
  465.2 14.0 %collective-permute-done.61 = bf16[256,2048]{1,0:T(8,128)(2,1)S(1)} collective-permute-done((bf16[256,2048]{1,0:T(8,128)(2,1)}, bf16[256,2048]{1,0:T(8,128)(2,1)S(1)}, u32[]{:S(2)}, u32[]{:S(2)}) %collective-permute-start.61) | collective-permute-done | bytes 1048608 | tf_op jit(solution)/shard_map/ppermute | solution.py:219
  487.6 4.8 shard_map.289
  499.9 17.1 %collective-permute-done.66 = f32[108,128]{1,0:T(8,128)S(1)} collective-permute-done((f32[108,128]{1,0:T(8,128)S(1)}, f32[108,128]{1,0:T(8,128)S(1)}, u32[]{:S(2)}, u32[]{:S(2)}) %collective-permute-start.66) | collective-permute-done | bytes 55328 | tf_op jit(solution)/shard_map/ppermute | solution.py:219
  533.2 18.2 %collective-permute-done.69 = f32[64,128]{1,0:T(8,128)S(1)} collective-permute-done((f32[64,128]{1,0:T(8,128)S(1)}, f32[64,128]{1,0:T(8,128)S(1)}, u32[]{:S(2)}, u32[]{:S(2)}) %collective-permute-start.69) | collective-permute-done | bytes 32800 | tf_op jit(solution)/shard_map/ppermute | solution.py:219
  (332 shorter events, 215.3 us)
Async XLA Ops:
  4.0 26.2 %collective-permute-start = (bf16[256,2048]{1,0:T(8,128)(2,1)S(1)}, bf16[256,2048]{1,0:T(8,128)(2,1)S(1)}, u32[]{:S(2)}, u32[]{:S(2)}) collective-permute-start(bf16[256,2048]{1,0:T(8,128)(2,1)S(1)} %pad_maximum_fusion.3.refs_3_.refs_11_.refs_0_.refs_8_), channel_id=1, source_target_pairs={{0,16},{8,24},{16,0},{24,8},{1,17},{9,25},{17,1},{25,9},{2,18},{10... | collective-permute-start | bytes 3145736 | tf_op jit(solution)/shard_map/ppermute | solution.py:219
  51.7 26.3 %collective-permute-start.7 = (bf16[256,2048]{1,0:T(8,128)(2,1)}, bf16[256,2048]{1,0:T(8,128)(2,1)}, u32[]{:S(2)}, u32[]{:S(2)}) collective-permute-start(bf16[256,2048]{1,0:T(8,128)(2,1)} %refs_16_.1), channel_id=1, source_target_pairs={{0,16},{8,24},{16,0},{24,8},{1,17},{9,25},{17,1},{25,9},{2,18},{10... | collective-permute-start | bytes 3145736 | tf_op jit(solution)/shard_map/ppermute | solution.py:219
  52.2 25.7 %collective-permute-start.8 = (bf16[256,2048]{1,0:T(8,128)(2,1)}, bf16[256,2048]{1,0:T(8,128)(2,1)}, u32[]{:S(2)}, u32[]{:S(2)}) collective-permute-start(bf16[256,2048]{1,0:T(8,128)(2,1)} %refs_16_.1), channel_id=1, source_target_pairs={{0,4},{4,0},{1,5},{5,1},{2,6},{6,2},{3,7},{7,3},{8,12},{12,8},{9,1... | collective-permute-start | bytes 3145736 | tf_op jit(solution)/shard_map/ppermute | solution.py:219
  65.8 34.2 %collective-permute-start.16 = (bf16[512,1024]{1,0:T(8,128)(2,1)}, bf16[512,1024]{1,0:T(8,128)(2,1)S(1)}, u32[]{:S(2)}, u32[]{:S(2)}) collective-permute-start(bf16[512,1024]{1,0:T(8,128)(2,1)} %get-tuple-element.276.refs_6_.refs_10_), channel_id=1, source_target_pairs={{0,16},{8,24},{16,0},{24,8},{1,17},{9,25},{17,1},{25,9},{2,18},{10... | collective-permute-start | bytes 3145736 | tf_op jit(solution)/shard_map/ppermute | solution.py:219
  105.5 32.2 %collective-permute-start.21 = (bf16[1024,1024]{1,0:T(8,128)(2,1)}, bf16[1024,1024]{1,0:T(8,128)(2,1)S(1)}, u32[]{:S(2)}, u32[]{:S(2)}) collective-permute-start(bf16[1024,1024]{1,0:T(8,128)(2,1)} %pad_maximum_fusion.1), channel_id=1, source_target_pairs={{0,8},{8,0},{16,24},{24,16},{1,9},{9,1},{17,25},{25,17},{2,10},{10... | collective-permute-start | bytes 6291464 | tf_op jit(solution)/shard_map/ppermute | solution.py:219
  150.9 26.9 %collective-permute-start.25 = (bf16[2,512,1024]{2,1,0:T(8,128)(2,1)}, bf16[2,512,1024]{2,1,0:T(8,128)(2,1)}, u32[]{:S(2)}, u32[]{:S(2)}) collective-permute-start(bf16[2,512,1024]{2,1,0:T(8,128)(2,1)} %get-tuple-element.283), channel_id=1, source_target_pairs={{0,8},{8,0},{16,24},{24,16},{1,9},{9,1},{17,25},{25,17},{2,10},{10... | collective-permute-start | bytes 6291464 | tf_op jit(solution)/shard_map/ppermute | solution.py:219
  180.2 33.8 %collective-permute-start.27 = (bf16[256,2048]{1,0:T(8,128)(2,1)}, bf16[256,2048]{1,0:T(8,128)(2,1)}, u32[]{:S(2)}, u32[]{:S(2)}) collective-permute-start(bf16[256,2048]{1,0:T(8,128)(2,1)} %get-tuple-element.294.refs_1_), channel_id=1, source_target_pairs={{0,1},{3,2},{4,5},{7,6},{8,9},{11,10},{12,13},{15,14},{16,17},{19,... | collective-permute-start | bytes 3145736 | tf_op jit(solution)/shard_map/ppermute | solution.py:589
  187.3 26.7 %collective-permute-start.28 = (bf16[512,1024]{1,0:T(8,128)(2,1)}, bf16[512,1024]{1,0:T(8,128)(2,1)S(1)}, u32[]{:S(2)}, u32[]{:S(2)}) collective-permute-start(bf16[512,1024]{1,0:T(8,128)(2,1)} %fusion.1), channel_id=1, source_target_pairs={{0,16},{8,24},{16,0},{24,8},{1,17},{9,25},{17,1},{25,9},{2,18},{10... | collective-permute-start | bytes 3145736 | tf_op jit(solution)/shard_map/ppermute | solution.py:219
  246.0 39.0 %collective-permute-start.37 = (bf16[1024,2048]{1,0:T(8,128)(2,1)}, bf16[1024,2048]{1,0:T(8,128)(2,1)}, u32[]{:S(2)}, u32[]{:S(2)}) collective-permute-start(bf16[1024,2048]{1,0:T(8,128)(2,1)} %shard_map.273), channel_id=1, source_target_pairs={{0,8},{8,0},{16,24},{24,16},{1,9},{9,1},{17,25},{25,17},{2,10},{10... | collective-permute-start | bytes 12582920 | tf_op jit(solution)/shard_map/ppermute | solution.py:219
  247.9 36.0 %collective-permute-start.34 = (bf16[256,2048]{1,0:T(8,128)(2,1)}, bf16[256,2048]{1,0:T(8,128)(2,1)}, u32[]{:S(2)}, u32[]{:S(2)}) collective-permute-start(bf16[256,2048]{1,0:T(8,128)(2,1)} %get-tuple-element.316.refs_3_), channel_id=1, source_target_pairs={{1,2},{2,1},{5,6},{6,5},{9,10},{10,9},{13,14},{14,13},{17,18},{18,... | collective-permute-start | bytes 3145736 | tf_op jit(solution)/shard_map/ppermute | solution.py:624
  251.1 32.7 %collective-permute-start.36 = (bf16[512,1024]{1,0:T(8,128)(2,1)}, bf16[512,1024]{1,0:T(8,128)(2,1)S(1)}, u32[]{:S(2)}, u32[]{:S(2)}) collective-permute-start(bf16[512,1024]{1,0:T(8,128)(2,1)} %fusion), channel_id=1, source_target_pairs={{0,16},{8,24},{16,0},{24,8},{1,17},{9,25},{17,1},{25,9},{2,18},{10... | collective-permute-start | bytes 3145736 | tf_op jit(solution)/shard_map/ppermute | solution.py:219
  252.4 31.5 %collective-permute-start.33 = (bf16[256,2048]{1,0:T(8,128)(2,1)S(1)}, bf16[256,2048]{1,0:T(8,128)(2,1)S(1)}, u32[]{:S(2)}, u32[]{:S(2)}) collective-permute-start(bf16[256,2048]{1,0:T(8,128)(2,1)S(1)} %copy-done.29), channel_id=1, source_target_pairs={{0,1},{3,2},{4,5},{7,6},{8,9},{11,10},{12,13},{15,14},{16,17},{19,... | collective-permute-start | bytes 3145736 | tf_op jit(solution)/shard_map/ppermute | solution.py:589
  258.0 26.9 %collective-permute-start.35 = (bf16[256,2048]{1,0:T(8,128)(2,1)}, bf16[256,2048]{1,0:T(8,128)(2,1)}, u32[]{:S(2)}, u32[]{:S(2)}) collective-permute-start(bf16[256,2048]{1,0:T(8,128)(2,1)} %get-tuple-element.318.refs_5_), channel_id=1, source_target_pairs={{1,0},{2,3},{5,4},{6,7},{9,8},{10,11},{13,12},{14,15},{17,16},{18,... | collective-permute-start | bytes 3145736 | tf_op jit(solution)/shard_map/ppermute | solution.py:627
  289.5 39.5 %collective-permute-start.39 = (bf16[256,2048]{1,0:T(8,128)(2,1)}, bf16[256,2048]{1,0:T(8,128)(2,1)}, u32[]{:S(2)}, u32[]{:S(2)}) collective-permute-start(bf16[256,2048]{1,0:T(8,128)(2,1)} %get-tuple-element.337.refs_3_), channel_id=1, source_target_pairs={{1,2},{2,1},{5,6},{6,5},{9,10},{10,9},{13,14},{14,13},{17,18},{18,... | collective-permute-start | bytes 3145736 | tf_op jit(solution)/shard_map/ppermute | solution.py:624
  295.2 33.7 %collective-permute-start.38 = (bf16[256,2048]{1,0:T(8,128)(2,1)}, bf16[256,2048]{1,0:T(8,128)(2,1)}, u32[]{:S(2)}, u32[]{:S(2)}) collective-permute-start(bf16[256,2048]{1,0:T(8,128)(2,1)} %get-tuple-element.338.refs_1_), channel_id=1, source_target_pairs={{0,1},{3,2},{4,5},{7,6},{8,9},{11,10},{12,13},{15,14},{16,17},{19,... | collective-permute-start | bytes 3145736 | tf_op jit(solution)/shard_map/ppermute | solution.py:589
  302.4 26.6 %collective-permute-start.40 = (bf16[256,2048]{1,0:T(8,128)(2,1)}, bf16[256,2048]{1,0:T(8,128)(2,1)}, u32[]{:S(2)}, u32[]{:S(2)}) collective-permute-start(bf16[256,2048]{1,0:T(8,128)(2,1)} %get-tuple-element.339.refs_5_), channel_id=1, source_target_pairs={{1,0},{2,3},{5,4},{6,7},{9,8},{10,11},{13,12},{14,15},{17,16},{18,... | collective-permute-start | bytes 3145736 | tf_op jit(solution)/shard_map/ppermute | solution.py:627
  333.6 33.4 %collective-permute-start.42 = (bf16[256,2048]{1,0:T(8,128)(2,1)}, bf16[256,2048]{1,0:T(8,128)(2,1)S(1)}, u32[]{:S(2)}, u32[]{:S(2)}) collective-permute-start(bf16[256,2048]{1,0:T(8,128)(2,1)} %get-tuple-element.361.refs_3_), channel_id=1, source_target_pairs={{1,2},{2,1},{5,6},{6,5},{9,10},{10,9},{13,14},{14,13},{17,18},{18,... | collective-permute-start | bytes 3145736 | tf_op jit(solution)/shard_map/ppermute | solution.py:624
  334.3 32.7 %collective-permute-start.41 = (bf16[256,2048]{1,0:T(8,128)(2,1)S(1)}, bf16[256,2048]{1,0:T(8,128)(2,1)S(1)}, u32[]{:S(2)}, u32[]{:S(2)}) collective-permute-start(bf16[256,2048]{1,0:T(8,128)(2,1)S(1)} %copy-done.42), channel_id=1, source_target_pairs={{0,1},{3,2},{4,5},{7,6},{8,9},{11,10},{12,13},{15,14},{16,17},{19,... | collective-permute-start | bytes 3145736 | tf_op jit(solution)/shard_map/ppermute | solution.py:589
  372.9 32.5 %collective-permute-start.47 = (bf16[256,2048]{1,0:T(8,128)(2,1)}, bf16[256,2048]{1,0:T(8,128)(2,1)S(1)}, u32[]{:S(2)}, u32[]{:S(2)}) collective-permute-start(bf16[256,2048]{1,0:T(8,128)(2,1)} %get-tuple-element.377.refs_3_), channel_id=1, source_target_pairs={{1,2},{2,1},{5,6},{6,5},{9,10},{10,9},{13,14},{14,13},{17,18},{18,... | collective-permute-start | bytes 3145736 | tf_op jit(solution)/shard_map/ppermute | solution.py:624
  373.6 31.8 %collective-permute-start.49 = (bf16[256,2048]{1,0:T(8,128)(2,1)}, bf16[256,2048]{1,0:T(8,128)(2,1)S(1)}, u32[]{:S(2)}, u32[]{:S(2)}) collective-permute-start(bf16[256,2048]{1,0:T(8,128)(2,1)} %get-tuple-element.381), channel_id=1, source_target_pairs={{0,4},{4,0},{1,5},{5,1},{2,6},{6,2},{3,7},{7,3},{8,12},{12,8},{9,1... | collective-permute-start | bytes 3145736 | tf_op jit(solution)/shard_map/ppermute | solution.py:219
  375.2 30.2 %collective-permute-start.46 = (bf16[256,2048]{1,0:T(8,128)(2,1)S(1)}, bf16[256,2048]{1,0:T(8,128)(2,1)}, u32[]{:S(2)}, u32[]{:S(2)}) collective-permute-start(bf16[256,2048]{1,0:T(8,128)(2,1)S(1)} %copy-done.41), channel_id=1, source_target_pairs={{0,1},{3,2},{4,5},{7,6},{8,9},{11,10},{12,13},{15,14},{16,17},{19,... | collective-permute-start | bytes 3145736 | tf_op jit(solution)/shard_map/ppermute | solution.py:589
  383.3 26.9 %collective-permute-start.48 = (bf16[256,2048]{1,0:T(8,128)(2,1)}, bf16[256,2048]{1,0:T(8,128)(2,1)}, u32[]{:S(2)}, u32[]{:S(2)}) collective-permute-start(bf16[256,2048]{1,0:T(8,128)(2,1)} %get-tuple-element.379.refs_5_), channel_id=1, source_target_pairs={{1,0},{2,3},{5,4},{6,7},{9,8},{10,11},{13,12},{14,15},{17,16},{18,... | collective-permute-start | bytes 3145736 | tf_op jit(solution)/shard_map/ppermute | solution.py:627
  414.7 29.5 %collective-permute-start.52 = (bf16[256,2048]{1,0:T(8,128)(2,1)}, bf16[256,2048]{1,0:T(8,128)(2,1)}, u32[]{:S(2)}, u32[]{:S(2)}) collective-permute-start(bf16[256,2048]{1,0:T(8,128)(2,1)} %get-tuple-element.399.refs_3_), channel_id=1, source_target_pairs={{1,2},{2,1},{5,6},{6,5},{9,10},{10,9},{13,14},{14,13},{17,18},{18,... | collective-permute-start | bytes 3145736 | tf_op jit(solution)/shard_map/ppermute | solution.py:624
  416.4 25.8 %collective-permute-start.55 = (bf16[256,2048]{1,0:T(8,128)(2,1)}, bf16[256,2048]{1,0:T(8,128)(2,1)S(1)}, u32[]{:S(2)}, u32[]{:S(2)}) collective-permute-start(bf16[256,2048]{1,0:T(8,128)(2,1)} %get-tuple-element.405), channel_id=1, source_target_pairs={{0,16},{8,24},{16,0},{24,8},{1,17},{9,25},{17,1},{25,9},{2,18},{10... | collective-permute-start | bytes 3145736 | tf_op jit(solution)/shard_map/ppermute | solution.py:219
  417.7 25.5 %collective-permute-start.54 = (bf16[256,2048]{1,0:T(8,128)(2,1)}, bf16[256,2048]{1,0:T(8,128)(2,1)S(1)}, u32[]{:S(2)}, u32[]{:S(2)}) collective-permute-start(bf16[256,2048]{1,0:T(8,128)(2,1)} %get-tuple-element.403), channel_id=1, source_target_pairs={{0,4},{4,0},{1,5},{5,1},{2,6},{6,2},{3,7},{7,3},{8,12},{12,8},{9,1... | collective-permute-start | bytes 3145736 | tf_op jit(solution)/shard_map/ppermute | solution.py:219
  418.1 26.1 %collective-permute-start.51 = (bf16[256,2048]{1,0:T(8,128)(2,1)}, bf16[256,2048]{1,0:T(8,128)(2,1)}, u32[]{:S(2)}, u32[]{:S(2)}) collective-permute-start(bf16[256,2048]{1,0:T(8,128)(2,1)} %get-tuple-element.400.refs_1_), channel_id=1, source_target_pairs={{0,1},{3,2},{4,5},{7,6},{8,9},{11,10},{12,13},{15,14},{16,17},{19,... | collective-permute-start | bytes 3145736 | tf_op jit(solution)/shard_map/ppermute | solution.py:589
  422.7 26.9 %collective-permute-start.53 = (bf16[256,2048]{1,0:T(8,128)(2,1)}, bf16[256,2048]{1,0:T(8,128)(2,1)}, u32[]{:S(2)}, u32[]{:S(2)}) collective-permute-start(bf16[256,2048]{1,0:T(8,128)(2,1)} %get-tuple-element.401.refs_5_), channel_id=1, source_target_pairs={{1,0},{2,3},{5,4},{6,7},{9,8},{10,11},{13,12},{14,15},{17,16},{18,... | collective-permute-start | bytes 3145736 | tf_op jit(solution)/shard_map/ppermute | solution.py:627
  454.4 28.1 %collective-permute-start.58 = (bf16[256,2048]{1,0:T(8,128)(2,1)}, bf16[256,2048]{1,0:T(8,128)(2,1)S(1)}, u32[]{:S(2)}, u32[]{:S(2)}) collective-permute-start(bf16[256,2048]{1,0:T(8,128)(2,1)} %get-tuple-element.416.refs_3_), channel_id=1, source_target_pairs={{1,2},{2,1},{5,6},{6,5},{9,10},{10,9},{13,14},{14,13},{17,18},{18,... | collective-permute-start | bytes 3145736 | tf_op jit(solution)/shard_map/ppermute | solution.py:624
  461.2 25.4 %collective-permute-start.59 = (bf16[256,2048]{1,0:T(8,128)(2,1)}, bf16[256,2048]{1,0:T(8,128)(2,1)S(1)}, u32[]{:S(2)}, u32[]{:S(2)}) collective-permute-start(bf16[256,2048]{1,0:T(8,128)(2,1)} %get-tuple-element.418.refs_5_), channel_id=1, source_target_pairs={{1,0},{2,3},{5,4},{6,7},{9,8},{10,11},{13,12},{14,15},{17,16},{18,... | collective-permute-start | bytes 3145736 | tf_op jit(solution)/shard_map/ppermute | solution.py:627
  524.3 31.8 %collective-permute-start.71 = (bf16[256,2048]{1,0:T(8,128)(2,1)}, bf16[256,2048]{1,0:T(8,128)(2,1)}, u32[]{:S(2)}, u32[]{:S(2)}) collective-permute-start(bf16[256,2048]{1,0:T(8,128)(2,1)} %add_convert_fusion.1), channel_id=1, source_target_pairs={{0,4},{4,0},{1,5},{5,1},{2,6},{6,2},{3,7},{7,3},{8,12},{12,8},{9,1... | collective-permute-start | bytes 3145736 | tf_op jit(solution)/shard_map/ppermute | solution.py:219
  526.6 29.6 %collective-permute-start.68 = (bf16[256,2048]{1,0:T(8,128)(2,1)}, bf16[256,2048]{1,0:T(8,128)(2,1)}, u32[]{:S(2)}, u32[]{:S(2)}) collective-permute-start(bf16[256,2048]{1,0:T(8,128)(2,1)} %add_convert_fusion), channel_id=1, source_target_pairs={{0,16},{8,24},{16,0},{24,8},{1,17},{9,25},{17,1},{25,9},{2,18},{10... | collective-permute-start | bytes 3145736 | tf_op jit(solution)/shard_map/ppermute | solution.py:219
  527.5 28.7 %collective-permute-start.67 = (bf16[256,2048]{1,0:T(8,128)(2,1)}, bf16[256,2048]{1,0:T(8,128)(2,1)}, u32[]{:S(2)}, u32[]{:S(2)}) collective-permute-start(bf16[256,2048]{1,0:T(8,128)(2,1)} %get-tuple-element.444.refs_1_), channel_id=1, source_target_pairs={{1,0},{2,3},{5,4},{6,7},{9,8},{10,11},{13,12},{14,15},{17,16},{18,... | collective-permute-start | bytes 3145736 | tf_op jit(solution)/shard_map/ppermute | solution.py:627
  (102 other events, 1291.1 us)
